TPU v7x, 32 devices: a whole 2x2x4 slice. The times are simulated.
32 devices in a mesh: sec: 2 (over y), dev: 16 (over z, x, core).
Axes of the slice: x: 2, y: 2, z: 4, core: 2. Of those that a mesh axis runs over, the one named last changes fastest.
Arguments:
- hidden_in: bfloat16 [1024, 4096], P(('sec', 'dev')), may hold values from -6 to 6
- routes: int32 [1024, 8], P(('sec', 'dev')), may hold values from 0 to 15, all different within a row; in each aligned block of 32 rows (0 to 31, 32 to 63, ...) at most 32 rows name the same one
- scores: float32 [1024, 8], P(('sec', 'dev')), may hold values from 0.05 to 1
- w_gate: bfloat16 [16, 4096, 1536], P('dev', None, 'sec'), may hold values from -0.09375 to 0.09375
- w_up: bfloat16 [16, 4096, 1536], P('dev', None, 'sec'), may hold values from -0.09375 to 0.09375
- w_down: bfloat16 [16, 1536, 4096], P('dev', 'sec'), may hold values from -0.15625 to 0.15625
Outputs:
- mixed: bfloat16 [1024, 4096], P(('sec', 'dev'))
Inputs may be any that keep to these rules, and one draw needn't show every extreme that they name: `routes`: each row names 8 different experts; among the rows of one device no expert is named by more than 32 rows, and in every draw some expert is named by exactly 32 rows of some device.
All inputs are finite; a program needn't handle non-finite values.
Results may differ from a plain program's by a relative error of at most 0.017.
Values may be sent and summed in bfloat16 or wider, within the bound.
No kernel may reach another device: no remote copies, remote signals or barrier semaphores. Data moves between devices by JAX's collectives and lax.ppermute only.
A program may use at most 128 MiB of HBM per device.

v0:
```python
import jax
import jax.numpy as jnp
from jax import lax
from jax.sharding import PartitionSpec as P


def on_device(hidden_in, routes, scores, w_gate, w_up, w_down):
    rows_dev, model_width = hidden_in.shape
    top_k = routes.shape[1]
    experts = lax.axis_size("dev")
    slots_dev = 2 * rows_dev * top_k // experts
    slot_rows = experts * slots_dev
    values = hidden_in.astype(jnp.float32)
    normed = (values * lax.rsqrt(jnp.mean(values * values, -1, keepdims=True) + 1e-06)).astype(
        jnp.bfloat16
    )
    shares = scores / jnp.sum(scores, -1, keepdims=True)
    chosen = routes.reshape(-1)
    onehot = (chosen[:, None] == jnp.arange(experts, dtype=jnp.int32)[None, :]).astype(jnp.int32)
    before = jnp.cumsum(onehot, 0) - onehot
    position = jnp.sum(before * onehot, 1)
    target = (chosen * slots_dev + position).reshape(rows_dev, top_k)
    places = jnp.arange(slot_rows, dtype=jnp.int32)
    picker = jnp.any(target[None, :, :] == places[:, None, None], -1).astype(jnp.bfloat16)
    outgoing = jnp.dot(picker, normed, preferred_element_type=jnp.float32).astype(jnp.bfloat16)
    outgoing = outgoing.reshape(experts, slots_dev, model_width)
    arrived = lax.all_to_all(outgoing, "dev", split_axis=0, concat_axis=0, tiled=True).reshape(
        slot_rows, model_width
    )
    paired = lax.all_gather(arrived, "sec", axis=0, tiled=True)
    gate_part = jnp.dot(paired, w_gate[0], preferred_element_type=jnp.float32)
    up_part = jnp.dot(paired, w_up[0], preferred_element_type=jnp.float32)
    hidden_part = (jax.nn.silu(gate_part) * up_part).astype(jnp.bfloat16)
    result = lax.psum_scatter(
        jnp.dot(hidden_part, w_down[0], preferred_element_type=jnp.float32).astype(jnp.bfloat16),
        "sec",
        scatter_dimension=0,
        tiled=True,
    )
    expert_out = result.reshape(experts, slots_dev, model_width)
    returned = lax.all_to_all(expert_out, "dev", split_axis=0, concat_axis=0, tiled=True).reshape(
        slot_rows, model_width
    )
    picked = jnp.take(returned, target.reshape(-1), axis=0).reshape(rows_dev, top_k, model_width)
    combined = jnp.einsum("rk,rkd->rd", shares, picked.astype(jnp.float32))
    return combined.astype(jnp.bfloat16)


def solution(mesh):
    placed = (
        P(("sec", "dev"), None),
        P(("sec", "dev"), None),
        P(("sec", "dev"), None),
        P("dev", None, "sec"),
        P("dev", None, "sec"),
        P("dev", "sec", None),
    )
    return jax.shard_map(
        on_device, mesh=mesh, in_specs=placed, out_specs=P(("sec", "dev"), None), check_vma=False
    )
```

profile of v0, /device:TPU:11, one launch (start us, length us, event | category | flops | bytes accessed | tf_op | source)
XLA Modules:
  0.0 458.4 jit_solution(12845307896784713352)
XLA Ops:
  6.5 0.8 copy.13
  7.3 0.1 eq.39
  7.4 0.1 reshape.89
  7.5 0.6 reduce-window.6
  8.1 0.2 slice_reduce_fusion
  8.3 0.1 fusion.17
  8.4 0.1 reduce_sum.33
  8.5 0.2 fusion.12
  8.8 1.1 fusion.10
  9.9 2.3 convolution_convert_fusion.1
  12.1 98.7 %all_to_all.10 = bf16[16,32,4096]{2,1,0:T(8,128)(2,1)} all-to-all(bf16[16,32,4096]{2,1,0:T(8,128)(2,1)S(1)} %bitcast.50), channel_id=1, replica_groups=mesh['sec'=2,'dev'=16] {'dev'}, dimensions={0} | all-to-all | bytes 8388608 | tf_op jit(solution)/shard_map/all_to_all | solution.py:27
  110.9 0.0 reduce-scatter.2.cloned.1.call-start
  110.9 104.0 %all-gather.2.cloned.1.call-done = bf16[1024,4096]{1,0:T(8,128)(2,1)} async-done(((bf16[512,4096]{1,0:T(8,128)(2,1)}), bf16[1024,4096]{1,0:T(8,128)(2,1)}) %all-gather.2.cloned.1.call-update) | async-done | bytes 8388624 | tf_op jit(solution)/shard_map/all_gather | solution.py:30
  214.9 11.0 %fusion.1 = f32[1024,768]{1,0:T(8,128)S(1)} fusion(bf16[1024,4096]{1,0:T(8,128)(2,1)} %all-gather.2.cloned.1.call-done, bf16[1,4096,768]{2,1,0:T(8,128)(2,1)} %param.10), kind=kOutput, calls=%fused_computation.3 | convolution fusion | flops 6442450944 | bytes 17825792 | tf_op jit(solution)/shard_map/dot_general | solution.py:32
  226.0 9.9 %multiply_convert_fusion = bf16[1024,768]{1,0:T(8,128)(2,1)S(1)} fusion(f32[1024,768]{1,0:T(8,128)S(1)} %fusion.1, bf16[1024,4096]{1,0:T(8,128)(2,1)S(1)} %copy-done.1, bf16[1,4096,768]{2,1,0:T(8,128)(2,1)} %param.9), kind=kOutput, calls=%fused_computation.8 | convolution fusion | flops 6447169536 | bytes 19398656 | tf_op jit(solution)/shard_map/dot_general | solution.py:31
  235.9 8.8 %convolution_convert_fusion = bf16[1024,4096]{1,0:T(8,128)(2,1)} fusion(bf16[1024,768]{1,0:T(8,128)(2,1)S(1)} %multiply_convert_fusion, bf16[1,768,4096]{2,1,0:T(8,128)(2,1)S(1)} %bitcast.55), kind=kOutput, calls=%fused_computation.1 | convolution fusion | flops 6446645248 | bytes 16252928 | tf_op jit(solution)/shard_map/dot_general | solution.py:35
  244.8 99.4 %reduce-scatter.2.cloned.1.call-done = bf16[512,4096]{1,0:T(8,128)(2,1)} async-done(((bf16[1024,4096]{1,0:T(8,128)(2,1)}), bf16[512,4096]{1,0:T(8,128)(2,1)}) %reduce-scatter.2.cloned.1.call-update) | async-done | bytes 4194320 | tf_op jit(solution)/shard_map/reduce_scatter | solution.py:34
  344.2 6.5 %all-to-all-start.1 = ((bf16[16,32,4096]{2,1,0:T(8,128)(2,1)}), bf16[16,32,4096]{2,1,0:T(8,128)(2,1)}, u32[]{:S(2)}, u32[]{:S(2)}) async-start(bf16[16,32,4096]{2,1,0:T(8,128)(2,1)} %bitcast.51), calls=%async_computation.2 | async-start | bytes 8388608 | tf_op jit(solution)/shard_map/all_to_all | solution.py:41
  350.7 0.1 mul.50
  350.8 0.1 copy.17
  351.0 92.2 %all-to-all-done.1 = bf16[16,32,4096]{2,1,0:T(8,128)(2,1)} async-done(((bf16[16,32,4096]{2,1,0:T(8,128)(2,1)}), bf16[16,32,4096]{2,1,0:T(8,128)(2,1)}, u32[]{:S(2)}, u32[]{:S(2)}) %all-to-all-start.1) | async-done | bytes 4194336 | tf_op jit(solution)/shard_map/all_to_all | solution.py:41
  443.2 6.6 %gather_fusion = bf16[256,4096]{1,0:T(8,128)(2,1)S(1)} fusion(bf16[512,4096]{1,0:T(8,128)(2,1)} %bitcast.8, s32[1024]{0:T(1024)S(1)} %pad_clamp_fusion), kind=kCustom, calls=%fused_computation | custom fusion | bytes 4195328 | tf_op jit(solution)/shard_map/jit(_take)/gather | solution.py:44
  449.8 0.8 fusion.7
  450.6 1.0 copy.22
  (22 shorter events, 0.2 us)
Async XLA Ops:
  6.5 208.4 %all-gather.2.cloned.1.call-start = ((), (), s32[]{:S(2)}) async-start(), calls=%async_computation.3 | async-start | bytes 12582912 | tf_op jit(solution)/shard_map/all_gather | solution.py:30
  110.9 233.3 %reduce-scatter.2.cloned.1.call-start = ((), (), s32[]{:S(2)}) async-start(), calls=%async_computation.4 | async-start | bytes 12582912 | tf_op jit(solution)/shard_map/reduce_scatter | solution.py:34
  214.9 11.0 %copy-start.1 = (bf16[1024,4096]{1,0:T(8,128)(2,1)S(1)}, bf16[1024,4096]{1,0:T(8,128)(2,1)}, u32[]{:S(2)}) copy-start(bf16[1024,4096]{1,0:T(8,128)(2,1)} %all-gather.2.cloned.1.call-done) | copy-start | bytes 25165828
  214.9 21.0 %slice-start = ((s8[6291456]{0:T(1024)(128)(4,1)}), s8[4194304]{0:T(1024)(128)(4,1)S(1)}, s32[]{:S(2)}) async-start(s8[6291456]{0:T(1024)(128)(4,1)} %bitcast.54), calls=%async_computation.5 | async-start | bytes 8388608
  226.0 9.9 %slice-start.1 = ((s8[6291456]{0:T(1024)(128)(4,1)}), s8[2097152]{0:T(1024)(128)(4,1)S(1)}, s32[]{:S(2)}) async-start(s8[6291456]{0:T(1024)(128)(4,1)} %bitcast.54), calls=%async_computation.6 | async-start | bytes 4194304
  344.2 6.6 %copy-start = (f32[32,8]{0,1:T(8,128)S(1)}, f32[32,8]{0,1:T(8,128)}, u32[]{:S(2)}) copy-start(f32[32,8]{0,1:T(8,128)} %param.8) | copy-start | bytes 3076
  344.2 99.0 %all-to-all-start.1 = ((bf16[16,32,4096]{2,1,0:T(8,128)(2,1)}), bf16[16,32,4096]{2,1,0:T(8,128)(2,1)}, u32[]{:S(2)}, u32[]{:S(2)}) async-start(bf16[16,32,4096]{2,1,0:T(8,128)(2,1)} %bitcast.51), calls=%async_computation.2 | async-start | bytes 8388608 | tf_op jit(solution)/shard_map/all_to_all | solution.py:41
Sparse Core Ops, SparseCore 0:
  111.0 103.8 all-gather.1
  244.9 99.2 reduce-scatter.1
where the time goes:
time: 459 us; the launch traced here: 458 us
  waiting for transfers between devices  296 us (64%)
  blocking collectives  98.7 us (22%)
  matrix products  32.8 us (7%)
  between operations  13.5 us (3%)
  local copies, waits for them, and re-layouts  9.01 us (2%)
  starting transfers between devices  6.56 us (1%)
    all_gather x1, waiting for transfers between devices, on_device(): paired = lax.all_gather(arrived, 'sec', axis=0, tiled=True)  104 us
    reduce_scatter x1, waiting for transfers between devices, on_device(): lax.psum_scatter(jnp.dot(hidden_part, w_down[0], preferred_element_type=j...  99.4 us
    all_to_all x1, blocking collectives, on_device(): lax.all_to_all(outgoing, 'dev', split_axis=0, concat_axis=0, tiled=True)  98.7 us
    all_to_all x1, waiting for transfers between devices, on_device(): lax.all_to_all(expert_out, 'dev', split_axis=0, concat_axis=0, tiled=True)  92.2 us
    dot_general x1, matrix products, on_device(): up_part = jnp.dot(paired, w_up[0], preferred_element_type=jnp.float32)  11 us
    dot_general x1, matrix products, on_device(): gate_part = jnp.dot(paired, w_gate[0], preferred_element_type=jnp.float32)  9.88 us
  transfers between devices with their start and end apart: 3, of which 3 were waited for; matrix products, arithmetic and copies ran while one was open for 0% of the time, Pallas kernels for 0%

commit v1 on v0

--- a/solution.py
+++ b/solution.py
@@ -3,17 +3,101 @@
 from jax import lax
 from jax.sharding import PartitionSpec as P
 
+BOTH = ("sec", "dev")
+CORE, X, ZA, ZB, Y = 1, 2, 4, 8, 16
+GATHER = (
+    (ZB, 0),
+    (X, 0),
+    (Y, 0),
+    (ZA, 0),
+    (X, Y),
+    (Y, ZA),
+    (ZA, X),
+    (X, ZB),
+    (Y, ZB),
+    (ZA, ZB),
+    (X, Y | ZA),
+    (X, Y | ZB),
+    (Y, ZA | ZB),
+    (ZA, X | ZB),
+    (Y, X | ZA | ZB),
+)
 
-def on_device(hidden_in, routes, scores, w_gate, w_up, w_down):
+
+def normalise(hidden_in):
+    values = hidden_in.astype(jnp.float32)
+    return (values * lax.rsqrt(jnp.mean(values * values, -1, keepdims=True) + 1e-06)).astype(
+        jnp.bfloat16
+    )
+
+
+def swap(block, mask, devices):
+    return lax.ppermute(block, BOTH, [(i, i ^ mask) for i in range(devices)])
+
+
+def expert(rows, w_gate, w_up, w_down):
+    gate_part = jnp.dot(rows, w_gate, preferred_element_type=jnp.float32)
+    up_part = jnp.dot(rows, w_up, preferred_element_type=jnp.float32)
+    hidden_part = (jax.nn.silu(gate_part) * up_part).astype(jnp.bfloat16)
+    return jnp.dot(hidden_part, w_down, preferred_element_type=jnp.float32)
+
+
+def spread(hidden_in, routes, scores, w_gate, w_up, w_down):
+    rows_dev, model_width = hidden_in.shape
+    experts = lax.axis_size("dev")
+    devices = experts * lax.axis_size("sec")
+    shares = scores / jnp.sum(scores, -1, keepdims=True)
+    table = jnp.sum(
+        jnp.where(
+            routes[:, :, None] == jnp.arange(experts, dtype=jnp.int32), shares[:, :, None], 0.0
+        ),
+        1,
+    )
+    terms = []
+    for _ in range(3):
+        term = table.astype(jnp.bfloat16)
+        terms.append(term)
+        table = table - term.astype(jnp.float32)
+    blank = jnp.zeros((rows_dev, -3 * experts % 128), jnp.bfloat16)
+    held = {0: jnp.concatenate([normalise(hidden_in), *terms, blank], 1)}
+    mine = (jnp.arange(experts) == lax.axis_index("dev")).astype(jnp.float32)
+
+    for link, block in GATHER:
+        held[block ^ link] = swap(held[block], link, devices)
+    for block in [m for m in held]:
+        held[block ^ CORE] = swap(held[block], CORE, devices)
+
+    sums = {}
+    for high in (0, ZB):
+        group = [m for m in range(devices) if m & ZB == high]
+        rows = jnp.concatenate([held[m] for m in group], 0)
+        table = rows[:, model_width : model_width + 3 * experts].astype(jnp.float32)
+        weight = jnp.sum(table.reshape(-1, 3, experts) * mine, (1, 2))
+        out = expert(rows[:, :model_width], w_gate[0], w_up[0], w_down[0]) * weight[:, None]
+        out = out.astype(jnp.bfloat16).reshape(len(group), rows_dev, model_width)
+        for at, m in enumerate(group):
+            sums[m] = out[at]
+
+    pending = {}
+    for m in range(devices):
+        if not m & CORE:
+            pending[m] = [sums[m], swap(sums[m ^ CORE], CORE, devices)]
+
+    def total(m):
+        return sum(part.astype(jnp.float32) for part in pending[m]).astype(jnp.bfloat16)
+
+    for link, block in reversed(GATHER):
+        pending[block].append(swap(total(block ^ link), link, devices))
+    return total(0)
+
+
+def dispatch(hidden_in, routes, scores, w_gate, w_up, w_down):
     rows_dev, model_width = hidden_in.shape
     top_k = routes.shape[1]
     experts = lax.axis_size("dev")
     slots_dev = 2 * rows_dev * top_k // experts
     slot_rows = experts * slots_dev
-    values = hidden_in.astype(jnp.float32)
-    normed = (values * lax.rsqrt(jnp.mean(values * values, -1, keepdims=True) + 1e-06)).astype(
-        jnp.bfloat16
-    )
+    normed = normalise(hidden_in)
     shares = scores / jnp.sum(scores, -1, keepdims=True)
     chosen = routes.reshape(-1)
     onehot = (chosen[:, None] == jnp.arange(experts, dtype=jnp.int32)[None, :]).astype(jnp.int32)
@@ -28,11 +112,8 @@
         slot_rows, model_width
     )
     paired = lax.all_gather(arrived, "sec", axis=0, tiled=True)
-    gate_part = jnp.dot(paired, w_gate[0], preferred_element_type=jnp.float32)
-    up_part = jnp.dot(paired, w_up[0], preferred_element_type=jnp.float32)
-    hidden_part = (jax.nn.silu(gate_part) * up_part).astype(jnp.bfloat16)
     result = lax.psum_scatter(
-        jnp.dot(hidden_part, w_down[0], preferred_element_type=jnp.float32).astype(jnp.bfloat16),
+        expert(paired, w_gate[0], w_up[0], w_down[0]).astype(jnp.bfloat16),
         "sec",
         scatter_dimension=0,
         tiled=True,
@@ -44,6 +125,13 @@
     picked = jnp.take(returned, target.reshape(-1), axis=0).reshape(rows_dev, top_k, model_width)
     combined = jnp.einsum("rk,rkd->rd", shares, picked.astype(jnp.float32))
     return combined.astype(jnp.bfloat16)
+
+
+def on_device(hidden_in, routes, scores, *weights):
+    experts, halves = lax.axis_size("dev"), lax.axis_size("sec")
+    roomy = 2 * routes.shape[1] >= experts
+    plan = spread if roomy and (halves, experts) == (2, 16) else dispatch
+    return plan(hidden_in, routes, scores, *weights)
 
 
 def solution(mesh):

time: 459 us -> 194 us (0.42)
  the two profiles are of different devices: /device:TPU:11 before, /device:TPU:0 now
where the time goes in v1:
time: 194 us; the launch traced here: 193 us
  waiting for transfers between devices  74.9 us (39%)
  matrix products  45.7 us (24%)
  starting transfers between devices  43.5 us (22%)
  local copies, waits for them, and re-layouts  16 us (8%)
  other arithmetic  12.6 us (6%)
    ppermute x62, waiting for transfers between devices, swap(): return lax.ppermute(block, BOTH, [(i, i ^ mask) for i in range(devices)])  74.9 us
    ppermute x62, starting transfers between devices, swap(): return lax.ppermute(block, BOTH, [(i, i ^ mask) for i in range(devices)])  43.5 us
    dot_general x2, matrix products, expert(): return jnp.dot(hidden_part, w_down, preferred_element_type=jnp.float32)  34.1 us
    dot_general x2, matrix products, expert(): up_part = jnp.dot(rows, w_up, preferred_element_type=jnp.float32)  11.7 us
    unnamed x38, local copies, waits for them, and re-layouts  11.3 us
    convert_element_type x10, other arithmetic, total(): sum((part.astype(jnp.float32) for part in pending[m])).astype(jnp.bfloat16)  7.21 us
  transfers between devices with their start and end apart: 62, of which 20 were waited for; matrix products, arithmetic and copies ran while one was open for 19% of the time, Pallas kernels for 0%

profile of v1, /device:TPU:0, one launch (start us, length us, event | category | flops | bytes accessed | tf_op | source)
XLA Modules:
  0.0 193.1 jit_solution(17426347407408768446)
XLA Ops:
  4.7 4.1 %collective-permute-start.30 = (bf16[32,4224]{1,0:T(8,128)(2,1)S(1)}, bf16[32,4224]{1,0:T(8,128)(2,1)S(1)}, u32[]{:S(2)}, u32[]{:S(2)}) collective-permute-start(bf16[32,4224]{1,0:T(8,128)(2,1)S(1)} %concatenate.9), channel_id=1, source_target_pairs={{0,8},{1,9},{2,10},{3,11},{4,12},{5,13},{6,14},{7,15},{8,0},{9,1},... | collective-permute-start | bytes 811016 | tf_op jit(solution)/shard_map/ppermute | solution.py:35
  14.2 7.0 %collective-permute-done.30 = bf16[32,4224]{1,0:T(8,128)(2,1)S(1)} collective-permute-done((bf16[32,4224]{1,0:T(8,128)(2,1)S(1)}, bf16[32,4224]{1,0:T(8,128)(2,1)S(1)}, u32[]{:S(2)}, u32[]{:S(2)}) %collective-permute-start.30) | collective-permute-done | bytes 270368 | tf_op jit(solution)/shard_map/ppermute | solution.py:35
  32.6 6.5 %collective-permute-done.5 = bf16[32,4224]{1,0:T(8,128)(2,1)S(1)} collective-permute-done((bf16[32,4224]{1,0:T(8,128)(2,1)S(1)}, bf16[32,4224]{1,0:T(8,128)(2,1)S(1)}, u32[]{:S(2)}, u32[]{:S(2)}) %collective-permute-start.5) | collective-permute-done | bytes 270368 | tf_op jit(solution)/shard_map/ppermute | solution.py:35
  51.4 2.7 %collective-permute-done.36 = bf16[32,4224]{1,0:T(8,128)(2,1)S(1)} collective-permute-done((bf16[32,4224]{1,0:T(8,128)(2,1)S(1)}, bf16[32,4224]{1,0:T(8,128)(2,1)S(1)}, u32[]{:S(2)}, u32[]{:S(2)}) %collective-permute-start.36) | collective-permute-done | bytes 270368 | tf_op jit(solution)/shard_map/ppermute | solution.py:35
  55.5 6.7 %collective-permute-done.13 = bf16[32,4224]{1,0:T(8,128)(2,1)S(1)} collective-permute-done((bf16[32,4224]{1,0:T(8,128)(2,1)S(1)}, bf16[32,4224]{1,0:T(8,128)(2,1)S(1)}, u32[]{:S(2)}, u32[]{:S(2)}) %collective-permute-start.13) | collective-permute-done | bytes 270368 | tf_op jit(solution)/shard_map/ppermute | solution.py:35
  65.4 4.0 %collective-permute-done.44 = bf16[32,4224]{1,0:T(8,128)(2,1)S(1)} collective-permute-done((bf16[32,4224]{1,0:T(8,128)(2,1)S(1)}, bf16[32,4224]{1,0:T(8,128)(2,1)S(1)}, u32[]{:S(2)}, u32[]{:S(2)}) %collective-permute-start.44) | collective-permute-done | bytes 270368 | tf_op jit(solution)/shard_map/ppermute | solution.py:35
  71.7 8.3 %fusion.4 = f32[512,768]{1,0:T(8,128)} fusion(bf16[1,4096,768]{2,1,0:T(8,128)(2,1)S(1)} %bitcast.24, bf16[512,4224]{1,0:T(8,128)(2,1)} %get-tuple-element.36), kind=kOutput, calls=%fused_computation.6 | convolution fusion | flops 3221225472 | bytes 12058624 | tf_op jit(solution)/shard_map/dot_general | solution.py:40
  80.0 3.4 %fusion.2 = f32[512,768]{1,0:T(8,128)S(1)} fusion(bf16[1,4096,768]{2,1,0:T(8,128)(2,1)S(1)} %bitcast.24, bf16[512,4224]{1,0:T(8,128)(2,1)S(1)} %get-tuple-element.37), kind=kOutput, calls=%fused_computation.4 | convolution fusion | flops 3221225472 | bytes 12058624 | tf_op jit(solution)/shard_map/dot_general | solution.py:40
  84.6 17.0 %multiply_convert_fusion = bf16[512,4096]{1,0:T(8,128)(2,1)} fusion(bf16[1,768,4096]{2,1,0:T(8,128)(2,1)} %param.11, f32[512]{0:T(512)S(1)} %get-tuple-element.6, f32[512,768]{1,0:T(8,128)S(1)} %fusion.2, bf16[1,4096,768]{2,1,0:T(8,128)(2,1)} %param.9, bf16[512,4224]{1,0:T(8,128)(2,1)} %copy-done.1), kind=kOutput, calls=%fused_computation | convolution fusion | flops 6449004544 | bytes 22546432 | tf_op jit(solution)/shard_map/dot_general | solution.py:42
  103.4 17.1 %multiply_convert_fusion.1 = bf16[512,4096]{1,0:T(8,128)(2,1)} fusion(bf16[1,768,4096]{2,1,0:T(8,128)(2,1)} %param.11, f32[512]{0:T(512)S(1)} %get-tuple-element.5, f32[512,768]{1,0:T(8,128)} %fusion.4, bf16[1,4096,768]{2,1,0:T(8,128)(2,1)} %param.9, bf16[512,4224]{1,0:T(8,128)(2,1)} %get-tuple-element.36), kind=kOutput, calls=%fused_computation.1 | convolution fusion | flops 6449004544 | bytes 22546432 | tf_op jit(solution)/shard_map/dot_general | solution.py:42
  120.5 1.8 fusion.37
  126.1 7.1 %collective-permute-done.49 = bf16[32,4096]{1,0:T(8,128)(2,1)S(1)} collective-permute-done((bf16[32,4096]{1,0:T(8,128)(2,1)S(1)}, bf16[32,4096]{1,0:T(8,128)(2,1)S(1)}, u32[]{:S(2)}, u32[]{:S(2)}) %collective-permute-start.49) | collective-permute-done | bytes 262176 | tf_op jit(solution)/shard_map/ppermute | solution.py:35
  136.6 5.8 %collective-permute-done.19 = bf16[32,4096]{1,0:T(8,128)(2,1)S(1)} collective-permute-done((bf16[32,4096]{1,0:T(8,128)(2,1)S(1)}, bf16[32,4096]{1,0:T(8,128)(2,1)S(1)}, u32[]{:S(2)}, u32[]{:S(2)}) %collective-permute-start.19) | collective-permute-done | bytes 262176 | tf_op jit(solution)/shard_map/ppermute | solution.py:35
  143.6 2.7 %collective-permute-done.53 = bf16[32,4096]{1,0:T(8,128)(2,1)S(1)} collective-permute-done((bf16[32,4096]{1,0:T(8,128)(2,1)S(1)}, bf16[32,4096]{1,0:T(8,128)(2,1)S(1)}, u32[]{:S(2)}, u32[]{:S(2)}) %collective-permute-start.53) | collective-permute-done | bytes 262176 | tf_op jit(solution)/shard_map/ppermute | solution.py:35
  146.3 2.5 %collective-permute-done.58 = bf16[32,4096]{1,0:T(8,128)(2,1)S(1)} collective-permute-done((bf16[32,4096]{1,0:T(8,128)(2,1)S(1)}, bf16[32,4096]{1,0:T(8,128)(2,1)S(1)}, u32[]{:S(2)}, u32[]{:S(2)}) %collective-permute-start.58) | collective-permute-done | bytes 262176 | tf_op jit(solution)/shard_map/ppermute | solution.py:35
  151.2 4.0 %collective-permute-done.20 = bf16[32,4096]{1,0:T(8,128)(2,1)S(1)} collective-permute-done((bf16[32,4096]{1,0:T(8,128)(2,1)S(1)}, bf16[32,4096]{1,0:T(8,128)(2,1)S(1)}, u32[]{:S(2)}, u32[]{:S(2)}) %collective-permute-start.20) | collective-permute-done | bytes 262176 | tf_op jit(solution)/shard_map/ppermute | solution.py:35
  155.1 1.9 collective-permute-start.59
  157.8 5.2 %collective-permute-done.59 = bf16[32,4096]{1,0:T(8,128)(2,1)S(1)} collective-permute-done((bf16[32,4096]{1,0:T(8,128)(2,1)S(1)}, bf16[32,4096]{1,0:T(8,128)(2,1)S(1)}, u32[]{:S(2)}, u32[]{:S(2)}) %collective-permute-start.59) | collective-permute-done | bytes 262176 | tf_op jit(solution)/shard_map/ppermute | solution.py:35
  163.0 2.0 %collective-permute-start.28 = (bf16[32,4096]{1,0:T(8,128)(2,1)S(1)}, bf16[32,4096]{1,0:T(8,128)(2,1)S(1)}, u32[]{:S(2)}, u32[]{:S(2)}) collective-permute-start(bf16[32,4096]{1,0:T(8,128)(2,1)S(1)} %get-tuple-element.16), channel_id=1, source_target_pairs={{0,4},{1,5},{2,6},{3,7},{4,0},{5,1},{6,2},{7,3},{8,12},{9,13},{10,... | collective-permute-start | bytes 786440 | tf_op jit(solution)/shard_map/ppermute | solution.py:35
  166.3 4.4 %collective-permute-done.28 = bf16[32,4096]{1,0:T(8,128)(2,1)S(1)} collective-permute-done((bf16[32,4096]{1,0:T(8,128)(2,1)S(1)}, bf16[32,4096]{1,0:T(8,128)(2,1)S(1)}, u32[]{:S(2)}, u32[]{:S(2)}) %collective-permute-start.28) | collective-permute-done | bytes 262176 | tf_op jit(solution)/shard_map/ppermute | solution.py:35
  171.5 2.5 %collective-permute-start.21 = (bf16[32,4096]{1,0:T(8,128)(2,1)S(1)}, bf16[32,4096]{1,0:T(8,128)(2,1)S(1)}, u32[]{:S(2)}, u32[]{:S(2)}) collective-permute-start(bf16[32,4096]{1,0:T(8,128)(2,1)S(1)} %get-tuple-element.15), channel_id=1, source_target_pairs={{0,4},{1,5},{2,6},{3,7},{4,0},{5,1},{6,2},{7,3},{8,12},{9,13},{10,... | collective-permute-start | bytes 786440 | tf_op jit(solution)/shard_map/ppermute | solution.py:35
  174.1 2.3 %collective-permute-done.50 = bf16[32,4096]{1,0:T(8,128)(2,1)S(1)} collective-permute-done((bf16[32,4096]{1,0:T(8,128)(2,1)S(1)}, bf16[32,4096]{1,0:T(8,128)(2,1)S(1)}, u32[]{:S(2)}, u32[]{:S(2)}) %collective-permute-start.50) | collective-permute-done | bytes 262176 | tf_op jit(solution)/shard_map/ppermute | solution.py:35
  178.3 5.6 %collective-permute-start.61 = (bf16[32,4096]{1,0:T(8,128)(2,1)S(1)}, bf16[32,4096]{1,0:T(8,128)(2,1)S(1)}, u32[]{:S(2)}, u32[]{:S(2)}) collective-permute-start(bf16[32,4096]{1,0:T(8,128)(2,1)S(1)} %add_convert_fusion.1), channel_id=1, source_target_pairs={{0,8},{1,9},{2,10},{3,11},{4,12},{5,13},{6,14},{7,15},{8,0},{9,1},... | collective-permute-start | bytes 786440 | tf_op jit(solution)/shard_map/ppermute | solution.py:35
  183.9 8.4 %collective-permute-done.61 = bf16[32,4096]{1,0:T(8,128)(2,1)S(1)} collective-permute-done((bf16[32,4096]{1,0:T(8,128)(2,1)S(1)}, bf16[32,4096]{1,0:T(8,128)(2,1)S(1)}, u32[]{:S(2)}, u32[]{:S(2)}) %collective-permute-start.61) | collective-permute-done | bytes 262176 | tf_op jit(solution)/shard_map/ppermute | solution.py:35
  (172 shorter events, 60.0 us)
Async XLA Ops:
  4.7 16.5 %collective-permute-start.30 = (bf16[32,4224]{1,0:T(8,128)(2,1)S(1)}, bf16[32,4224]{1,0:T(8,128)(2,1)S(1)}, u32[]{:S(2)}, u32[]{:S(2)}) collective-permute-start(bf16[32,4224]{1,0:T(8,128)(2,1)S(1)} %concatenate.9), channel_id=1, source_target_pairs={{0,8},{1,9},{2,10},{3,11},{4,12},{5,13},{6,14},{7,15},{8,0},{9,1},... | collective-permute-start | bytes 811016 | tf_op jit(solution)/shard_map/ppermute | solution.py:35
  8.8 12.5 %collective-permute-start = (bf16[32,4224]{1,0:T(8,128)(2,1)S(1)}, bf16[32,4224]{1,0:T(8,128)(2,1)S(1)}, u32[]{:S(2)}, u32[]{:S(2)}) collective-permute-start(bf16[32,4224]{1,0:T(8,128)(2,1)S(1)} %concatenate.9), channel_id=1, source_target_pairs={{0,1},{1,0},{2,3},{3,2},{4,5},{5,4},{6,7},{7,6},{8,9},{9,8},{10,11... | collective-permute-start | bytes 811016 | tf_op jit(solution)/shard_map/ppermute | solution.py:35
  8.8 14.1 %collective-permute-start.1 = (bf16[32,4224]{1,0:T(8,128)(2,1)S(1)}, bf16[32,4224]{1,0:T(8,128)(2,1)S(1)}, u32[]{:S(2)}, u32[]{:S(2)}) collective-permute-start(bf16[32,4224]{1,0:T(8,128)(2,1)S(1)} %concatenate.9), channel_id=1, source_target_pairs={{0,2},{1,3},{2,0},{3,1},{4,6},{5,7},{6,4},{7,5},{8,10},{9,11},{10,... | collective-permute-start | bytes 811016 | tf_op jit(solution)/shard_map/ppermute | solution.py:35
  10.3 15.5 %collective-permute-start.3 = (bf16[32,4224]{1,0:T(8,128)(2,1)S(1)}, bf16[32,4224]{1,0:T(8,128)(2,1)S(1)}, u32[]{:S(2)}, u32[]{:S(2)}) collective-permute-start(bf16[32,4224]{1,0:T(8,128)(2,1)S(1)} %concatenate.9), channel_id=1, source_target_pairs={{0,4},{1,5},{2,6},{3,7},{4,0},{5,1},{6,2},{7,3},{8,12},{9,13},{10,... | collective-permute-start | bytes 811016 | tf_op jit(solution)/shard_map/ppermute | solution.py:35
  11.9 16.2 %collective-permute-start.7 = (bf16[32,4224]{1,0:T(8,128)(2,1)S(1)}, bf16[32,4224]{1,0:T(8,128)(2,1)S(1)}, u32[]{:S(2)}, u32[]{:S(2)}) collective-permute-start(bf16[32,4224]{1,0:T(8,128)(2,1)S(1)} %concatenate.9), channel_id=1, source_target_pairs={{0,16},{1,17},{2,18},{3,19},{4,20},{5,21},{6,22},{7,23},{8,24},{9,... | collective-permute-start | bytes 811016 | tf_op jit(solution)/shard_map/ppermute | solution.py:35
  24.5 17.6 %collective-permute-start.34 = (bf16[32,4224]{1,0:T(8,128)(2,1)S(1)}, bf16[32,4224]{1,0:T(8,128)(2,1)S(1)}, u32[]{:S(2)}, u32[]{:S(2)}) collective-permute-start(bf16[32,4224]{1,0:T(8,128)(2,1)S(1)} %collective-permute-done.30), channel_id=1, source_target_pairs={{0,4},{1,5},{2,6},{3,7},{4,0},{5,1},{6,2},{7,3},{8,12},{9,13},{10,... | collective-permute-start | bytes 811016 | tf_op jit(solution)/shard_map/ppermute | solution.py:35
  25.8 19.5 %collective-permute-start.38 = (bf16[32,4224]{1,0:T(8,128)(2,1)S(1)}, bf16[32,4224]{1,0:T(8,128)(2,1)S(1)}, u32[]{:S(2)}, u32[]{:S(2)}) collective-permute-start(bf16[32,4224]{1,0:T(8,128)(2,1)S(1)} %collective-permute-done.30), channel_id=1, source_target_pairs={{0,16},{1,17},{2,18},{3,19},{4,20},{5,21},{6,22},{7,23},{8,24},{9,... | collective-permute-start | bytes 811016 | tf_op jit(solution)/shard_map/ppermute | solution.py:35
  28.1 10.9 %collective-permute-start.5 = (bf16[32,4224]{1,0:T(8,128)(2,1)S(1)}, bf16[32,4224]{1,0:T(8,128)(2,1)S(1)}, u32[]{:S(2)}, u32[]{:S(2)}) collective-permute-start(bf16[32,4224]{1,0:T(8,128)(2,1)S(1)} %collective-permute-done.1), channel_id=1, source_target_pairs={{0,4},{1,5},{2,6},{3,7},{4,0},{5,1},{6,2},{7,3},{8,12},{9,13},{10,... | collective-permute-start | bytes 811016 | tf_op jit(solution)/shard_map/ppermute | solution.py:35
  30.2 15.8 %collective-permute-start.8 = (bf16[32,4224]{1,0:T(8,128)(2,1)S(1)}, bf16[32,4224]{1,0:T(8,128)(2,1)S(1)}, u32[]{:S(2)}, u32[]{:S(2)}) collective-permute-start(bf16[32,4224]{1,0:T(8,128)(2,1)S(1)} %collective-permute-done.7), channel_id=1, source_target_pairs={{0,1},{1,0},{2,3},{3,2},{4,5},{5,4},{6,7},{7,6},{8,9},{9,8},{10,11... | collective-permute-start | bytes 811016 | tf_op jit(solution)/shard_map/ppermute | solution.py:35
  30.2 15.8 %collective-permute-start.9 = (bf16[32,4224]{1,0:T(8,128)(2,1)S(1)}, bf16[32,4224]{1,0:T(8,128)(2,1)S(1)}, u32[]{:S(2)}, u32[]{:S(2)}) collective-permute-start(bf16[32,4224]{1,0:T(8,128)(2,1)S(1)} %collective-permute-done.7), channel_id=1, source_target_pairs={{0,2},{1,3},{2,0},{3,1},{4,6},{5,7},{6,4},{7,5},{8,10},{9,11},{10,... | collective-permute-start | bytes 811016 | tf_op jit(solution)/shard_map/ppermute | solution.py:35
  45.9 18.1 %collective-permute-start.39 = (bf16[32,4224]{1,0:T(8,128)(2,1)S(1)}, bf16[32,4224]{1,0:T(8,128)(2,1)S(1)}, u32[]{:S(2)}, u32[]{:S(2)}) collective-permute-start(bf16[32,4224]{1,0:T(8,128)(2,1)S(1)} %collective-permute-done.38), channel_id=1, source_target_pairs={{0,1},{1,0},{2,3},{3,2},{4,5},{5,4},{6,7},{7,6},{8,9},{9,8},{10,11... | collective-permute-start | bytes 811016 | tf_op jit(solution)/shard_map/ppermute | solution.py:35
  47.9 15.5 %collective-permute-start.40 = (bf16[32,4224]{1,0:T(8,128)(2,1)S(1)}, bf16[32,4224]{1,0:T(8,128)(2,1)S(1)}, u32[]{:S(2)}, u32[]{:S(2)}) collective-permute-start(bf16[32,4224]{1,0:T(8,128)(2,1)S(1)} %collective-permute-done.38), channel_id=1, source_target_pairs={{0,2},{1,3},{2,0},{3,1},{4,6},{5,7},{6,4},{7,5},{8,10},{9,11},{10,... | collective-permute-start | bytes 811016 | tf_op jit(solution)/shard_map/ppermute | solution.py:35
  49.2 14.3 %collective-permute-start.42 = (bf16[32,4224]{1,0:T(8,128)(2,1)S(1)}, bf16[32,4224]{1,0:T(8,128)(2,1)S(1)}, u32[]{:S(2)}, u32[]{:S(2)}) collective-permute-start(bf16[32,4224]{1,0:T(8,128)(2,1)S(1)} %collective-permute-done.34), channel_id=1, source_target_pairs={{0,16},{1,17},{2,18},{3,19},{4,20},{5,21},{6,22},{7,23},{8,24},{9,... | collective-permute-start | bytes 811016 | tf_op jit(solution)/shard_map/ppermute | solution.py:35
  103.2 20.2 %collective-permute-start.48 = (bf16[32,4096]{1,0:T(8,128)(2,1)S(1)}, bf16[32,4096]{1,0:T(8,128)(2,1)S(1)}, u32[]{:S(2)}, u32[]{:S(2)}) collective-permute-start(bf16[32,4096]{1,0:T(8,128)(2,1)S(1)} %get-tuple-element.26), channel_id=1, source_target_pairs={{0,1},{1,0},{2,3},{3,2},{4,5},{5,4},{6,7},{7,6},{8,9},{9,8},{10,11... | collective-permute-start | bytes 786440 | tf_op jit(solution)/shard_map/ppermute | solution.py:35
  122.7 12.3 %collective-permute-start.17 = (bf16[32,4096]{1,0:T(8,128)(2,1)S(1)}, bf16[32,4096]{1,0:T(8,128)(2,1)S(1)}, u32[]{:S(2)}, u32[]{:S(2)}) collective-permute-start(bf16[32,4096]{1,0:T(8,128)(2,1)S(1)} %get-tuple-element.13), channel_id=1, source_target_pairs={{0,1},{1,0},{2,3},{3,2},{4,5},{5,4},{6,7},{7,6},{8,9},{9,8},{10,11... | collective-permute-start | bytes 786440 | tf_op jit(solution)/shard_map/ppermute | solution.py:35
  125.4 25.1 %collective-permute-start.16 = (bf16[32,4096]{1,0:T(8,128)(2,1)S(1)}, bf16[32,4096]{1,0:T(8,128)(2,1)S(1)}, u32[]{:S(2)}, u32[]{:S(2)}) collective-permute-start(bf16[32,4096]{1,0:T(8,128)(2,1)S(1)} %get-tuple-element.14), channel_id=1, source_target_pairs={{0,1},{1,0},{2,3},{3,2},{4,5},{5,4},{6,7},{7,6},{8,9},{9,8},{10,11... | collective-permute-start | bytes 786440 | tf_op jit(solution)/shard_map/ppermute | solution.py:35
  125.5 17.5 %collective-permute-start.51 = (bf16[32,4096]{1,0:T(8,128)(2,1)S(1)}, bf16[32,4096]{1,0:T(8,128)(2,1)S(1)}, u32[]{:S(2)}, u32[]{:S(2)}) collective-permute-start(bf16[32,4096]{1,0:T(8,128)(2,1)S(1)} %get-tuple-element.25), channel_id=1, source_target_pairs={{0,1},{1,0},{2,3},{3,2},{4,5},{5,4},{6,7},{7,6},{8,9},{9,8},{10,11... | collective-permute-start | bytes 786440 | tf_op jit(solution)/shard_map/ppermute | solution.py:35
  126.0 17.1 %collective-permute-start.56 = (bf16[32,4096]{1,0:T(8,128)(2,1)S(1)}, bf16[32,4096]{1,0:T(8,128)(2,1)S(1)}, u32[]{:S(2)}, u32[]{:S(2)}) collective-permute-start(bf16[32,4096]{1,0:T(8,128)(2,1)S(1)} %get-tuple-element.22), channel_id=1, source_target_pairs={{0,1},{1,0},{2,3},{3,2},{4,5},{5,4},{6,7},{7,6},{8,9},{9,8},{10,11... | collective-permute-start | bytes 786440 | tf_op jit(solution)/shard_map/ppermute | solution.py:35
  135.0 11.3 %collective-permute-start.53 = (bf16[32,4096]{1,0:T(8,128)(2,1)S(1)}, bf16[32,4096]{1,0:T(8,128)(2,1)S(1)}, u32[]{:S(2)}, u32[]{:S(2)}) collective-permute-start(bf16[32,4096]{1,0:T(8,128)(2,1)S(1)} %get-tuple-element.30), channel_id=1, source_target_pairs={{0,2},{1,3},{2,0},{3,1},{4,6},{5,7},{6,4},{7,5},{8,10},{9,11},{10,... | collective-permute-start | bytes 786440 | tf_op jit(solution)/shard_map/ppermute | solution.py:35
  146.3 19.8 %collective-permute-start.22 = (bf16[32,4096]{1,0:T(8,128)(2,1)S(1)}, bf16[32,4096]{1,0:T(8,128)(2,1)S(1)}, u32[]{:S(2)}, u32[]{:S(2)}) collective-permute-start(bf16[32,4096]{1,0:T(8,128)(2,1)S(1)} %get-tuple-element.11), channel_id=1, source_target_pairs={{0,1},{1,0},{2,3},{3,2},{4,5},{5,4},{6,7},{7,6},{8,9},{9,8},{10,11... | collective-permute-start | bytes 786440 | tf_op jit(solution)/shard_map/ppermute | solution.py:35
  150.5 15.7 %collective-permute-start.26 = (bf16[32,4096]{1,0:T(8,128)(2,1)S(1)}, bf16[32,4096]{1,0:T(8,128)(2,1)S(1)}, u32[]{:S(2)}, u32[]{:S(2)}) collective-permute-start(bf16[32,4096]{1,0:T(8,128)(2,1)S(1)} %get-tuple-element.9), channel_id=1, source_target_pairs={{0,1},{1,0},{2,3},{3,2},{4,5},{5,4},{6,7},{7,6},{8,9},{9,8},{10,11... | collective-permute-start | bytes 786440 | tf_op jit(solution)/shard_map/ppermute | solution.py:35
  150.6 33.3 %collective-permute-start.15 = (bf16[32,4096]{1,0:T(8,128)(2,1)S(1)}, bf16[32,4096]{1,0:T(8,128)(2,1)S(1)}, u32[]{:S(2)}, u32[]{:S(2)}) collective-permute-start(bf16[32,4096]{1,0:T(8,128)(2,1)S(1)} %get-tuple-element.7), channel_id=1, source_target_pairs={{0,1},{1,0},{2,3},{3,2},{4,5},{5,4},{6,7},{7,6},{8,9},{9,8},{10,11... | collective-permute-start | bytes 786440 | tf_op jit(solution)/shard_map/ppermute | solution.py:35
  171.5 12.3 %collective-permute-start.21 = (bf16[32,4096]{1,0:T(8,128)(2,1)S(1)}, bf16[32,4096]{1,0:T(8,128)(2,1)S(1)}, u32[]{:S(2)}, u32[]{:S(2)}) collective-permute-start(bf16[32,4096]{1,0:T(8,128)(2,1)S(1)} %get-tuple-element.15), channel_id=1, source_target_pairs={{0,4},{1,5},{2,6},{3,7},{4,0},{5,1},{6,2},{7,3},{8,12},{9,13},{10,... | collective-permute-start | bytes 786440 | tf_op jit(solution)/shard_map/ppermute | solution.py:35
  178.3 14.0 %collective-permute-start.61 = (bf16[32,4096]{1,0:T(8,128)(2,1)S(1)}, bf16[32,4096]{1,0:T(8,128)(2,1)S(1)}, u32[]{:S(2)}, u32[]{:S(2)}) collective-permute-start(bf16[32,4096]{1,0:T(8,128)(2,1)S(1)} %add_convert_fusion.1), channel_id=1, source_target_pairs={{0,8},{1,9},{2,10},{3,11},{4,12},{5,13},{6,14},{7,15},{8,0},{9,1},... | collective-permute-start | bytes 786440 | tf_op jit(solution)/shard_map/ppermute | solution.py:35
  (42 other events, 307.5 us)

commit v2 on v0

--- a/solution.py
+++ b/solution.py
@@ -1,19 +1,184 @@
+import functools
+
 import jax
 import jax.numpy as jnp
 from jax import lax
+from jax.experimental import pallas as pl
+from jax.experimental.pallas import tpu as pltpu
 from jax.sharding import PartitionSpec as P
 
-
-def on_device(hidden_in, routes, scores, w_gate, w_up, w_down):
+BOTH = ("sec", "dev")
+CORE, X, ZA, ZB, Y = 1, 2, 4, 8, 16
+NEAR = (0, ZA, X, Y)
+FAR = (X | Y, X | ZA, Y | ZA, X | Y | ZA)
+TERMS = 3
+VMEM = pl.BlockSpec(memory_space=pltpu.VMEM)
+
+
+def normalise(hidden_in):
+    values = hidden_in.astype(jnp.float32)
+    return (values * lax.rsqrt(jnp.mean(values * values, -1, keepdims=True) + 1e-06)).astype(
+        jnp.bfloat16
+    )
+
+
+def swap(block, mask, devices):
+    return lax.ppermute(block, BOTH, [(i, i ^ mask) for i in range(devices)])
+
+
+def expert(rows, w_gate, w_up, w_down):
+    gate_part = jnp.dot(rows, w_gate, preferred_element_type=jnp.float32)
+    up_part = jnp.dot(rows, w_up, preferred_element_type=jnp.float32)
+    hidden_part = (jax.nn.silu(gate_part) * up_part).astype(jnp.bfloat16)
+    return jnp.dot(hidden_part, w_down, preferred_element_type=jnp.float32)
+
+
+def local(body, outs, operands, scratch=(), limit=8, **cost):
+    return pl.pallas_call(
+        body,
+        out_shape=[jax.ShapeDtypeStruct(shape, jnp.bfloat16) for shape in outs],
+        in_specs=[VMEM] * len(operands),
+        out_specs=[VMEM] * len(outs),
+        scratch_shapes=list(scratch),
+        compiler_params=pltpu.CompilerParams(vmem_limit_bytes=limit * 2**20),
+        cost_estimate=pl.CostEstimate(**{"flops": 0, "transcendentals": 0, "bytes_accessed": 0, **cost}),
+    )(*operands)
+
+
+def prepare_body(experts, hidden_ref, routes_ref, scores_ref, out_ref):
+    width = hidden_ref.shape[1]
+    out_ref[:, :width] = normalise(hidden_ref[...])
+    scores = scores_ref[...]
+    shares = scores / jnp.sum(scores, -1, keepdims=True)
+    lanes = lax.broadcasted_iota(jnp.int32, (hidden_ref.shape[0], 128), 1)
+    table = jnp.zeros(lanes.shape, jnp.float32)
+    for k in range(routes_ref.shape[1]):
+        named = routes_ref[:, k : k + 1] == lanes % experts
+        table = table + jnp.where(named, shares[:, k : k + 1], 0.0)
+    packed = jnp.zeros(lanes.shape, jnp.float32)
+    for at in range(TERMS):
+        term = table.astype(jnp.bfloat16).astype(jnp.float32)
+        packed = jnp.where(lanes // experts == at, term, packed)
+        table = table - term
+    out_ref[:, width:] = packed.astype(jnp.bfloat16)
+
+
+def prepare(hidden_in, routes, scores, experts):
+    rows, width = hidden_in.shape
+    return local(
+        functools.partial(prepare_body, experts), [(rows, width + 128)], (hidden_in, routes, scores)
+    )[0]
+
+
+def expert_body(count, mine_ref, *refs):
+    blocks, (gate_ref, up_ref, down_ref), outs = refs[:count], refs[count : count + 3], refs[count + 3 : count + 5]
+    rows_ref, hidden_ref = refs[count + 5 :]
+    rows, width = blocks[0].shape[0], down_ref.shape[1]
+    shares = []
+    for at, block in enumerate(blocks):
+        rows_ref[at * rows : (at + 1) * rows, :] = block[:, :width]
+        shares.append(jnp.sum(block[:, width:].astype(jnp.float32) * mine_ref[...], -1, keepdims=True))
+    weight = jnp.concatenate(shares, 0)
+    for at in range(0, gate_ref.shape[1], 256):
+        cols = slice(at, at + 256)
+        gate_part = jnp.dot(rows_ref[...], gate_ref[:, cols], preferred_element_type=jnp.float32)
+        up_part = jnp.dot(rows_ref[...], up_ref[:, cols], preferred_element_type=jnp.float32)
+        hidden_ref[:, cols] = (gate_part / (1.0 + jnp.exp(-gate_part)) * up_part).astype(jnp.bfloat16)
+    half = count // 2 * rows
+
+    @pl.loop(0, width // 1024)
+    def _(at):
+        cols = pl.ds(pl.multiple_of(at * 1024, 1024), 1024)
+        out = jnp.dot(hidden_ref[...], down_ref[:, cols], preferred_element_type=jnp.float32) * weight
+        outs[0][:, cols] = out[:half].astype(jnp.bfloat16)
+        outs[1][:, cols] = out[half:].astype(jnp.bfloat16)
+
+
+def expert_rows(blocks, mine, w_gate, w_up, w_down):
+    count, rows = len(blocks), blocks[0].shape[0]
+    width, units = w_down.shape[1], w_gate.shape[1]
+    return local(
+        functools.partial(expert_body, count),
+        [(count // 2 * rows, width)] * 2,
+        (mine, *blocks, w_gate, w_up, w_down),
+        [pltpu.VMEM((count * rows, width), jnp.bfloat16), pltpu.VMEM((count * rows, units), jnp.bfloat16)],
+        flops=6 * count * rows * width * units,
+        bytes_accessed=2 * count * rows * width,
+    )
+
+
+def add_body(plan, count, *refs):
+    for out, parts in zip(refs[count:], plan):
+        rows = out.shape[0]
+        total = 0.0
+        for ref, at in parts:
+            total = total + refs[ref][at * rows : (at + 1) * rows, :].astype(jnp.float32)
+        out[...] = total.astype(jnp.bfloat16)
+
+
+def add_up(plan, arrays, rows):
+    shapes = [(rows, arrays[0].shape[1])] * len(plan)
+    return local(functools.partial(add_body, plan, len(arrays)), shapes, arrays, limit=4)
+
+
+def spread(hidden_in, routes, scores, w_gate, w_up, w_down):
+    rows = hidden_in.shape[0]
+    experts = lax.axis_size("dev")
+    devices = experts * lax.axis_size("sec")
+    lanes = jnp.arange(128)
+    mine = (lanes % experts == lax.axis_index("dev")) & (lanes < TERMS * experts)
+    mine = mine.astype(jnp.float32)[None, :]
+    weights = (mine, w_gate[0], w_up[0], w_down[0])
+    held = {0: prepare(hidden_in, routes, scores, experts)}
+
+    def send(link, block):
+        held[block ^ link] = swap(held[block], link, devices)
+
+    send(ZB, 0)
+    for top in (0, ZB):
+        for link in (ZA, X, Y, X | Y):
+            send(link, top)
+        send(X, top | ZA)
+        send(Y, top | ZA)
+        send(ZA, top | X | Y)
+    for m in list(held):
+        send(CORE, m)
+
+    outs = {}
+    for top in (0, ZB):
+        for at, group in enumerate((NEAR, FAR)):
+            group = [top | m for m in group]
+            own, other = expert_rows([held[m] for m in group] + [held[m ^ CORE] for m in group], *weights)
+            outs[top, at] = own, swap(other, CORE, devices)
+
+    ends = []
+    for top in (0, ZB):
+        far, near = outs[top, 1], outs[top, 0]
+        xa, ya, xya = add_up([[(0, at), (1, at)] for at in (1, 2, 3)], far, rows)
+        xa, ya, xya = swap(xa, X, devices), swap(ya, Y, devices), swap(xya, ZA, devices)
+        a, x, y, xy = add_up(
+            [
+                [(0, 1), (1, 1), (4, 0), (5, 0)],
+                [(0, 2), (1, 2)],
+                [(0, 3), (1, 3)],
+                [(2, 0), (3, 0), (6, 0)],
+            ],
+            (*near, *far, xa, ya, xya),
+            rows,
+        )
+        ends.append((*near, swap(a, ZA, devices), swap(x, X, devices), swap(y, Y, devices), swap(xy, X | Y, devices)))
+    whole = [(at, 0) for at in range(6)]
+    top = add_up([whole], ends[1], rows)[0]
+    return add_up([[*whole, (6, 0)]], (*ends[0], swap(top, ZB, devices)), rows)[0]
+
+
+def dispatch(hidden_in, routes, scores, w_gate, w_up, w_down):
     rows_dev, model_width = hidden_in.shape
     top_k = routes.shape[1]
     experts = lax.axis_size("dev")
     slots_dev = 2 * rows_dev * top_k // experts
     slot_rows = experts * slots_dev
-    values = hidden_in.astype(jnp.float32)
-    normed = (values * lax.rsqrt(jnp.mean(values * values, -1, keepdims=True) + 1e-06)).astype(
-        jnp.bfloat16
-    )
+    normed = normalise(hidden_in)
     shares = scores / jnp.sum(scores, -1, keepdims=True)
     chosen = routes.reshape(-1)
     onehot = (chosen[:, None] == jnp.arange(experts, dtype=jnp.int32)[None, :]).astype(jnp.int32)
@@ -28,11 +193,8 @@
         slot_rows, model_width
     )
     paired = lax.all_gather(arrived, "sec", axis=0, tiled=True)
-    gate_part = jnp.dot(paired, w_gate[0], preferred_element_type=jnp.float32)
-    up_part = jnp.dot(paired, w_up[0], preferred_element_type=jnp.float32)
-    hidden_part = (jax.nn.silu(gate_part) * up_part).astype(jnp.bfloat16)
     result = lax.psum_scatter(
-        jnp.dot(hidden_part, w_down[0], preferred_element_type=jnp.float32).astype(jnp.bfloat16),
+        expert(paired, w_gate[0], w_up[0], w_down[0]).astype(jnp.bfloat16),
         "sec",
         scatter_dimension=0,
         tiled=True,
@@ -44,6 +206,13 @@
     picked = jnp.take(returned, target.reshape(-1), axis=0).reshape(rows_dev, top_k, model_width)
     combined = jnp.einsum("rk,rkd->rd", shares, picked.astype(jnp.float32))
     return combined.astype(jnp.bfloat16)
+
+
+def on_device(hidden_in, routes, scores, *weights):
+    experts, halves = lax.axis_size("dev"), lax.axis_size("sec")
+    roomy = 2 * routes.shape[1] >= experts
+    plan = spread if roomy and (halves, experts) == (2, 16) else dispatch
+    return plan(hidden_in, routes, scores, *weights)
 
 
 def solution(mesh):

time: 459 us -> 131 us (0.29)
  the two profiles are of different devices: /device:TPU:11 before, /device:TPU:0 now
where the time goes in v2:
time: 131 us
  waiting for transfers between devices  46.8 us (36%)
  starting transfers between devices  43.9 us (34%)
  Pallas kernels  27.2 us (21%)
  local copies, waits for them, and re-layouts  12.5 us (10%)
    ppermute x50, waiting for transfers between devices, swap(): return lax.ppermute(block, BOTH, [(i, i ^ mask) for i in range(devices)])  46.8 us
    ppermute x50, starting transfers between devices, swap(): return lax.ppermute(block, BOTH, [(i, i ^ mask) for i in range(devices)])  43.9 us
    pallas_call x11, Pallas kernels, local(): pl.pallas_call(body, out_shape=[jax.ShapeDtypeStruct(shape, jnp.bfloat16)...  27.2 us
    unnamed x18, local copies, waits for them, and re-layouts  12.5 us
  transfers between devices with their start and end apart: 50, of which 16 were waited for; matrix products, arithmetic and copies ran while one was open for 0% of the time, Pallas kernels for 20%

profile of v2, /device:TPU:0, one launch (start us, length us, event | category | flops | bytes accessed | tf_op | source)
XLA Modules:
  0.0 130.6 jit_solution(13867363852561926175)
XLA Ops:
  2.7 4.1 %collective-permute-start.24 = (bf16[32,4224]{1,0:T(8,128)(2,1)S(1)}, bf16[32,4224]{1,0:T(8,128)(2,1)S(1)}, u32[]{:S(2)}, u32[]{:S(2)}) collective-permute-start(bf16[32,4224]{1,0:T(8,128)(2,1)S(1)} %shard_map.64.refs_0_), channel_id=1, source_target_pairs={{0,8},{1,9},{2,10},{3,11},{4,12},{5,13},{6,14},{7,15},{8,0},{9,1},... | collective-permute-start | bytes 811016 | tf_op jit(solution)/shard_map/ppermute | solution.py:26
  8.4 2.4 %collective-permute-start.8 = (bf16[32,4224]{1,0:T(8,128)(2,1)S(1)}, bf16[32,4224]{1,0:T(8,128)(2,1)S(1)}, u32[]{:S(2)}, u32[]{:S(2)}) collective-permute-start(bf16[32,4224]{1,0:T(8,128)(2,1)S(1)} %shard_map.64.refs_0_), channel_id=1, source_target_pairs={{0,18},{1,19},{2,16},{3,17},{4,22},{5,23},{6,20},{7,21},{8,26},{9,... | collective-permute-start | bytes 811016 | tf_op jit(solution)/shard_map/ppermute | solution.py:26
  11.4 7.8 %collective-permute-done.24.refs_0_ = bf16[32,4224]{1,0:T(8,128)(2,1)S(1)} collective-permute-done((bf16[32,4224]{1,0:T(8,128)(2,1)S(1)}, bf16[32,4224]{1,0:T(8,128)(2,1)S(1)}, u32[]{:S(2)}, u32[]{:S(2)}) %collective-permute-start.24) | collective-permute-done | bytes 270368 | tf_op jit(solution)/shard_map/ppermute | solution.py:26
  19.8 2.4 %collective-permute-start.33 = (bf16[32,4224]{1,0:T(8,128)(2,1)S(1)}, bf16[32,4224]{1,0:T(8,128)(2,1)S(1)}, u32[]{:S(2)}, u32[]{:S(2)}) collective-permute-start(bf16[32,4224]{1,0:T(8,128)(2,1)S(1)} %collective-permute-done.24.refs_0_), channel_id=1, source_target_pairs={{0,18},{1,19},{2,16},{3,17},{4,22},{5,23},{6,20},{7,21},{8,26},{9,... | collective-permute-start | bytes 811016 | tf_op jit(solution)/shard_map/ppermute | solution.py:26
  23.3 3.5 %collective-permute-done.25.refs_1_ = bf16[32,4224]{1,0:T(8,128)(2,1)S(1)} collective-permute-done((bf16[32,4224]{1,0:T(8,128)(2,1)S(1)}, bf16[32,4224]{1,0:T(8,128)(2,1)S(1)}, u32[]{:S(2)}, u32[]{:S(2)}) %collective-permute-start.25) | collective-permute-done | bytes 270368 | tf_op jit(solution)/shard_map/ppermute | solution.py:26
  28.0 2.1 %collective-permute-done.33.refs_0_ = bf16[32,4224]{1,0:T(8,128)(2,1)S(1)} collective-permute-done((bf16[32,4224]{1,0:T(8,128)(2,1)S(1)}, bf16[32,4224]{1,0:T(8,128)(2,1)S(1)}, u32[]{:S(2)}, u32[]{:S(2)}) %collective-permute-start.33) | collective-permute-done | bytes 270368 | tf_op jit(solution)/shard_map/ppermute | solution.py:26
  31.7 4.3 %collective-permute-done.26.refs_2_ = bf16[32,4224]{1,0:T(8,128)(2,1)S(1)} collective-permute-done((bf16[32,4224]{1,0:T(8,128)(2,1)S(1)}, bf16[32,4224]{1,0:T(8,128)(2,1)S(1)}, u32[]{:S(2)}, u32[]{:S(2)}) %collective-permute-start.26) | collective-permute-done | bytes 270368 | tf_op jit(solution)/shard_map/ppermute | solution.py:26
  42.3 4.0 %collective-permute-done.34.refs_1_ = bf16[32,4224]{1,0:T(8,128)(2,1)S(1)} collective-permute-done((bf16[32,4224]{1,0:T(8,128)(2,1)S(1)}, bf16[32,4224]{1,0:T(8,128)(2,1)S(1)}, u32[]{:S(2)}, u32[]{:S(2)}) %collective-permute-start.34) | collective-permute-done | bytes 270368 | tf_op jit(solution)/shard_map/ppermute | solution.py:26
  48.3 2.8 %copy-done = bf16[1,4096,768]{2,1,0:T(8,128)(2,1)S(1)} copy-done((bf16[1,4096,768]{2,1,0:T(8,128)(2,1)S(1)}, bf16[1,4096,768]{2,1,0:T(8,128)(2,1)}, u32[]{:S(2)}) %copy-start) | copy-done | bytes 6291480
  51.1 2.8 %copy-done.1 = bf16[1,4096,768]{2,1,0:T(8,128)(2,1)S(1)} copy-done((bf16[1,4096,768]{2,1,0:T(8,128)(2,1)S(1)}, bf16[1,4096,768]{2,1,0:T(8,128)(2,1)}, u32[]{:S(2)}) %copy-start.1) | copy-done | bytes 6291480
  53.9 2.8 %copy-done.2 = bf16[1,768,4096]{2,1,0:T(8,128)(2,1)S(1)} copy-done((bf16[1,768,4096]{2,1,0:T(8,128)(2,1)S(1)}, bf16[1,768,4096]{2,1,0:T(8,128)(2,1)}, u32[]{:S(2)}) %copy-start.2) | copy-done | bytes 6291480
  57.6 7.2 %shard_map.69 = (bf16[128,4096]{1,0:T(8,128)(2,1)S(1)}, bf16[128,4096]{1,0:T(8,128)(2,1)S(1)}) custom-call(f32[1,128]{1,0:T(1,128)S(1)} %and_convert_fusion.mine_ref, bf16[32,4224]{1,0:T(8,128)(2,1)S(1)} %collective-permute-done.24.refs_0_, bf16[32,4224]{1,0:T(8,128)(2,1)S(1)} %collective-permute-done.25.refs_1_, ...), custom_call_target="tpu_custom_call" | custom-call | flops 4831838208 | bytes 2097152 | tf_op jit(solution)/shard_map/pallas_call | solution.py:37
  66.7 5.8 %shard_map.70 = (bf16[128,4096]{1,0:T(8,128)(2,1)S(1)}, bf16[128,4096]{1,0:T(8,128)(2,1)S(1)}) custom-call(f32[1,128]{1,0:T(1,128)S(1)} %and_convert_fusion.mine_ref, bf16[32,4224]{1,0:T(8,128)(2,1)S(1)} %collective-permute-done.33.refs_0_, bf16[32,4224]{1,0:T(8,128)(2,1)S(1)} %collective-permute-done.34.refs_1_, ...), custom_call_target="tpu_custom_call" | custom-call | flops 4831838208 | bytes 2097152 | tf_op jit(solution)/shard_map/pallas_call | solution.py:37
  74.8 5.8 %shard_map.66 = (bf16[128,4096]{1,0:T(8,128)(2,1)S(1)}, bf16[128,4096]{1,0:T(8,128)(2,1)S(1)}) custom-call(f32[1,128]{1,0:T(1,128)S(1)} %and_convert_fusion.mine_ref, bf16[32,4224]{1,0:T(8,128)(2,1)S(1)} %collective-permute-done.8.refs_0_, bf16[32,4224]{1,0:T(8,128)(2,1)S(1)} %collective-permute-done.9.refs_1_, ...), custom_call_target="tpu_custom_call" | custom-call | flops 4831838208 | bytes 2097152 | tf_op jit(solution)/shard_map/pallas_call | solution.py:37
  81.3 6.0 %shard_map.65 = (bf16[128,4096]{1,0:T(8,128)(2,1)S(1)}, bf16[128,4096]{1,0:T(8,128)(2,1)S(1)}) custom-call(f32[1,128]{1,0:T(1,128)S(1)} %and_convert_fusion.mine_ref, bf16[32,4224]{1,0:T(8,128)(2,1)S(1)} %shard_map.64.refs_0_, bf16[32,4224]{1,0:T(8,128)(2,1)S(1)} %collective-permute-done.refs_1_, bf16[32,4224]{1,0:T(8,128)(2,1)S(1)} %collective-permute-done.1.refs_2_, ...), custom_call_target="tpu_custom_call" | custom-call | flops 4831838208 | bytes 2097152 | tf_op jit(solution)/shard_map/pallas_call | solution.py:37
  90.0 1.6 %collective-permute-start.44 = (bf16[32,4096]{1,0:T(8,128)(2,1)S(1)}, bf16[32,4096]{1,0:T(8,128)(2,1)S(1)}, u32[]{:S(2)}, u32[]{:S(2)}) collective-permute-start(bf16[32,4096]{1,0:T(8,128)(2,1)S(1)} %get-tuple-element.44), channel_id=1, source_target_pairs={{0,4},{1,5},{2,6},{3,7},{4,0},{5,1},{6,2},{7,3},{8,12},{9,13},{10,... | collective-permute-start | bytes 786440 | tf_op jit(solution)/shard_map/ppermute | solution.py:26
  92.5 4.7 %collective-permute-done.42.refs_4_ = bf16[32,4096]{1,0:T(8,128)(2,1)S(1)} collective-permute-done((bf16[32,4096]{1,0:T(8,128)(2,1)S(1)}, bf16[32,4096]{1,0:T(8,128)(2,1)S(1)}, u32[]{:S(2)}, u32[]{:S(2)}) %collective-permute-start.42) | collective-permute-done | bytes 262176 | tf_op jit(solution)/shard_map/ppermute | solution.py:26
  103.8 1.9 %collective-permute-start.48 = (bf16[32,4096]{1,0:T(8,128)(2,1)S(1)}, bf16[32,4096]{1,0:T(8,128)(2,1)S(1)}, u32[]{:S(2)}, u32[]{:S(2)}) collective-permute-start(bf16[32,4096]{1,0:T(8,128)(2,1)S(1)} %get-tuple-element.48), channel_id=1, source_target_pairs={{0,18},{1,19},{2,16},{3,17},{4,22},{5,23},{6,20},{7,21},{8,26},{9,... | collective-permute-start | bytes 786440 | tf_op jit(solution)/shard_map/ppermute | solution.py:26
  107.3 1.7 %collective-permute-start.20 = (bf16[32,4096]{1,0:T(8,128)(2,1)S(1)}, bf16[32,4096]{1,0:T(8,128)(2,1)S(1)}, u32[]{:S(2)}, u32[]{:S(2)}) collective-permute-start(bf16[32,4096]{1,0:T(8,128)(2,1)S(1)} %get-tuple-element.34), channel_id=1, source_target_pairs={{0,4},{1,5},{2,6},{3,7},{4,0},{5,1},{6,2},{7,3},{8,12},{9,13},{10,... | collective-permute-start | bytes 786440 | tf_op jit(solution)/shard_map/ppermute | solution.py:26
  109.0 3.6 %collective-permute-done.45.refs_2_ = bf16[32,4096]{1,0:T(8,128)(2,1)S(1)} collective-permute-done((bf16[32,4096]{1,0:T(8,128)(2,1)S(1)}, bf16[32,4096]{1,0:T(8,128)(2,1)S(1)}, u32[]{:S(2)}, u32[]{:S(2)}) %collective-permute-start.45) | collective-permute-done | bytes 262176 | tf_op jit(solution)/shard_map/ppermute | solution.py:26
  115.5 3.1 %collective-permute-done.47.refs_4_ = bf16[32,4096]{1,0:T(8,128)(2,1)S(1)} collective-permute-done((bf16[32,4096]{1,0:T(8,128)(2,1)S(1)}, bf16[32,4096]{1,0:T(8,128)(2,1)S(1)}, u32[]{:S(2)}, u32[]{:S(2)}) %collective-permute-start.47) | collective-permute-done | bytes 262176 | tf_op jit(solution)/shard_map/ppermute | solution.py:26
  118.8 3.7 %collective-permute-start.49 = (bf16[32,4096]{1,0:T(8,128)(2,1)S(1)}, bf16[32,4096]{1,0:T(8,128)(2,1)S(1)}, u32[]{:S(2)}, u32[]{:S(2)}) collective-permute-start(bf16[32,4096]{1,0:T(8,128)(2,1)S(1)} %shard_map.73), channel_id=1, source_target_pairs={{0,8},{1,9},{2,10},{3,11},{4,12},{5,13},{6,14},{7,15},{8,0},{9,1},... | collective-permute-start | bytes 786440 | tf_op jit(solution)/shard_map/ppermute | solution.py:26
  122.5 3.8 %collective-permute-done.22.refs_4_ = bf16[32,4096]{1,0:T(8,128)(2,1)S(1)} collective-permute-done((bf16[32,4096]{1,0:T(8,128)(2,1)S(1)}, bf16[32,4096]{1,0:T(8,128)(2,1)S(1)}, u32[]{:S(2)}, u32[]{:S(2)}) %collective-permute-start.22) | collective-permute-done | bytes 262176 | tf_op jit(solution)/shard_map/ppermute | solution.py:26
  126.3 3.4 %collective-permute-done.49.refs_6_ = bf16[32,4096]{1,0:T(8,128)(2,1)S(1)} collective-permute-done((bf16[32,4096]{1,0:T(8,128)(2,1)S(1)}, bf16[32,4096]{1,0:T(8,128)(2,1)S(1)}, u32[]{:S(2)}, u32[]{:S(2)}) %collective-permute-start.49) | collective-permute-done | bytes 262176 | tf_op jit(solution)/shard_map/ppermute | solution.py:26
  (107 shorter events, 39.0 us)
Async XLA Ops:
  2.7 16.5 %collective-permute-start.24 = (bf16[32,4224]{1,0:T(8,128)(2,1)S(1)}, bf16[32,4224]{1,0:T(8,128)(2,1)S(1)}, u32[]{:S(2)}, u32[]{:S(2)}) collective-permute-start(bf16[32,4224]{1,0:T(8,128)(2,1)S(1)} %shard_map.64.refs_0_), channel_id=1, source_target_pairs={{0,8},{1,9},{2,10},{3,11},{4,12},{5,13},{6,14},{7,15},{8,0},{9,1},... | collective-permute-start | bytes 811016 | tf_op jit(solution)/shard_map/ppermute | solution.py:26
  6.8 15.4 %collective-permute-start = (bf16[32,4224]{1,0:T(8,128)(2,1)S(1)}, bf16[32,4224]{1,0:T(8,128)(2,1)S(1)}, u32[]{:S(2)}, u32[]{:S(2)}) collective-permute-start(bf16[32,4224]{1,0:T(8,128)(2,1)S(1)} %shard_map.64.refs_0_), channel_id=1, source_target_pairs={{0,4},{1,5},{2,6},{3,7},{4,0},{5,1},{6,2},{7,3},{8,12},{9,13},{10,... | collective-permute-start | bytes 811016 | tf_op jit(solution)/shard_map/ppermute | solution.py:26
  8.4 14.4 %collective-permute-start.8 = (bf16[32,4224]{1,0:T(8,128)(2,1)S(1)}, bf16[32,4224]{1,0:T(8,128)(2,1)S(1)}, u32[]{:S(2)}, u32[]{:S(2)}) collective-permute-start(bf16[32,4224]{1,0:T(8,128)(2,1)S(1)} %shard_map.64.refs_0_), channel_id=1, source_target_pairs={{0,18},{1,19},{2,16},{3,17},{4,22},{5,23},{6,20},{7,21},{8,26},{9,... | collective-permute-start | bytes 811016 | tf_op jit(solution)/shard_map/ppermute | solution.py:26
  10.8 12.5 %collective-permute-start.1 = (bf16[32,4224]{1,0:T(8,128)(2,1)S(1)}, bf16[32,4224]{1,0:T(8,128)(2,1)S(1)}, u32[]{:S(2)}, u32[]{:S(2)}) collective-permute-start(bf16[32,4224]{1,0:T(8,128)(2,1)S(1)} %shard_map.64.refs_0_), channel_id=1, source_target_pairs={{0,2},{1,3},{2,0},{3,1},{4,6},{5,7},{6,4},{7,5},{8,10},{9,11},{10,... | collective-permute-start | bytes 811016 | tf_op jit(solution)/shard_map/ppermute | solution.py:26
  22.3 13.7 %collective-permute-start.26 = (bf16[32,4224]{1,0:T(8,128)(2,1)S(1)}, bf16[32,4224]{1,0:T(8,128)(2,1)S(1)}, u32[]{:S(2)}, u32[]{:S(2)}) collective-permute-start(bf16[32,4224]{1,0:T(8,128)(2,1)S(1)} %collective-permute-done.24.refs_0_), channel_id=1, source_target_pairs={{0,2},{1,3},{2,0},{3,1},{4,6},{5,7},{6,4},{7,5},{8,10},{9,11},{10,... | collective-permute-start | bytes 811016 | tf_op jit(solution)/shard_map/ppermute | solution.py:26
  22.8 14.7 %collective-permute-start.27 = (bf16[32,4224]{1,0:T(8,128)(2,1)S(1)}, bf16[32,4224]{1,0:T(8,128)(2,1)}, u32[]{:S(2)}, u32[]{:S(2)}) collective-permute-start(bf16[32,4224]{1,0:T(8,128)(2,1)S(1)} %collective-permute-done.24.refs_0_), channel_id=1, source_target_pairs={{0,16},{1,17},{2,18},{3,19},{4,20},{5,21},{6,22},{7,23},{8,24},{9,... | collective-permute-start | bytes 811016 | tf_op jit(solution)/shard_map/ppermute | solution.py:26
  23.3 14.7 %collective-permute-start.28 = (bf16[32,4224]{1,0:T(8,128)(2,1)S(1)}, bf16[32,4224]{1,0:T(8,128)(2,1)S(1)}, u32[]{:S(2)}, u32[]{:S(2)}) collective-permute-start(bf16[32,4224]{1,0:T(8,128)(2,1)S(1)} %collective-permute-done.24.refs_0_), channel_id=1, source_target_pairs={{0,1},{1,0},{2,3},{3,2},{4,5},{5,4},{6,7},{7,6},{8,9},{9,8},{10,11... | collective-permute-start | bytes 811016 | tf_op jit(solution)/shard_map/ppermute | solution.py:26
  26.8 15.0 %collective-permute-start.9 = (bf16[32,4224]{1,0:T(8,128)(2,1)S(1)}, bf16[32,4224]{1,0:T(8,128)(2,1)S(1)}, u32[]{:S(2)}, u32[]{:S(2)}) collective-permute-start(bf16[32,4224]{1,0:T(8,128)(2,1)S(1)} %collective-permute-done.refs_1_), channel_id=1, source_target_pairs={{0,2},{1,3},{2,0},{3,1},{4,6},{5,7},{6,4},{7,5},{8,10},{9,11},{10,... | collective-permute-start | bytes 811016 | tf_op jit(solution)/shard_map/ppermute | solution.py:26
  30.1 11.6 %collective-permute-start.10 = (bf16[32,4224]{1,0:T(8,128)(2,1)S(1)}, bf16[32,4224]{1,0:T(8,128)(2,1)S(1)}, u32[]{:S(2)}, u32[]{:S(2)}) collective-permute-start(bf16[32,4224]{1,0:T(8,128)(2,1)S(1)} %collective-permute-done.refs_1_), channel_id=1, source_target_pairs={{0,16},{1,17},{2,18},{3,19},{4,20},{5,21},{6,22},{7,23},{8,24},{9,... | collective-permute-start | bytes 811016 | tf_op jit(solution)/shard_map/ppermute | solution.py:26
  46.3 18.5 %collective-permute-start.11 = (bf16[32,4224]{1,0:T(8,128)(2,1)S(1)}, bf16[32,4224]{1,0:T(8,128)(2,1)S(1)}, u32[]{:S(2)}, u32[]{:S(2)}) collective-permute-start(bf16[32,4224]{1,0:T(8,128)(2,1)S(1)} %collective-permute-done.8.refs_0_), channel_id=1, source_target_pairs={{0,4},{1,5},{2,6},{3,7},{4,0},{5,1},{6,2},{7,3},{8,12},{9,13},{10,... | collective-permute-start | bytes 811016 | tf_op jit(solution)/shard_map/ppermute | solution.py:26
  46.8 18.9 %collective-permute-start.37 = (bf16[32,4224]{1,0:T(8,128)(2,1)S(1)}, bf16[32,4224]{1,0:T(8,128)(2,1)S(1)}, u32[]{:S(2)}, u32[]{:S(2)}) collective-permute-start(bf16[32,4224]{1,0:T(8,128)(2,1)S(1)} %collective-permute-done.33.refs_0_), channel_id=1, source_target_pairs={{0,1},{1,0},{2,3},{3,2},{4,5},{5,4},{6,7},{7,6},{8,9},{9,8},{10,11... | collective-permute-start | bytes 811016 | tf_op jit(solution)/shard_map/ppermute | solution.py:26
  47.0 18.7 %collective-permute-start.38 = (bf16[32,4224]{1,0:T(8,128)(2,1)S(1)}, bf16[32,4224]{1,0:T(8,128)(2,1)S(1)}, u32[]{:S(2)}, u32[]{:S(2)}) collective-permute-start(bf16[32,4224]{1,0:T(8,128)(2,1)S(1)} %collective-permute-done.34.refs_1_), channel_id=1, source_target_pairs={{0,1},{1,0},{2,3},{3,2},{4,5},{5,4},{6,7},{7,6},{8,9},{9,8},{10,11... | collective-permute-start | bytes 811016 | tf_op jit(solution)/shard_map/ppermute | solution.py:26
  47.3 18.9 %collective-permute-start.39 = (bf16[32,4224]{1,0:T(8,128)(2,1)S(1)}, bf16[32,4224]{1,0:T(8,128)(2,1)S(1)}, u32[]{:S(2)}, u32[]{:S(2)}) collective-permute-start(bf16[32,4224]{1,0:T(8,128)(2,1)S(1)} %collective-permute-done.35.refs_2_), channel_id=1, source_target_pairs={{0,1},{1,0},{2,3},{3,2},{4,5},{5,4},{6,7},{7,6},{8,9},{9,8},{10,11... | collective-permute-start | bytes 811016 | tf_op jit(solution)/shard_map/ppermute | solution.py:26
  48.2 18.1 %collective-permute-start.40 = (bf16[32,4224]{1,0:T(8,128)(2,1)S(1)}, bf16[32,4224]{1,0:T(8,128)(2,1)S(1)}, u32[]{:S(2)}, u32[]{:S(2)}) collective-permute-start(bf16[32,4224]{1,0:T(8,128)(2,1)S(1)} %collective-permute-done.36.refs_3_), channel_id=1, source_target_pairs={{0,1},{1,0},{2,3},{3,2},{4,5},{5,4},{6,7},{7,6},{8,9},{9,8},{10,11... | collective-permute-start | bytes 811016 | tf_op jit(solution)/shard_map/ppermute | solution.py:26
  74.7 13.1 %collective-permute-start.41 = (bf16[128,4096]{1,0:T(8,128)(2,1)S(1)}, bf16[128,4096]{1,0:T(8,128)(2,1)S(1)}, u32[]{:S(2)}, u32[]{:S(2)}) collective-permute-start(bf16[128,4096]{1,0:T(8,128)(2,1)S(1)} %get-tuple-element.41), channel_id=1, source_target_pairs={{0,1},{1,0},{2,3},{3,2},{4,5},{5,4},{6,7},{7,6},{8,9},{9,8},{10,11... | collective-permute-start | bytes 3145736 | tf_op jit(solution)/shard_map/ppermute | solution.py:26
  80.7 11.2 %collective-permute-start.32 = (bf16[128,4096]{1,0:T(8,128)(2,1)S(1)}, bf16[128,4096]{1,0:T(8,128)(2,1)S(1)}, u32[]{:S(2)}, u32[]{:S(2)}) collective-permute-start(bf16[128,4096]{1,0:T(8,128)(2,1)S(1)} %get-tuple-element.39), channel_id=1, source_target_pairs={{0,1},{1,0},{2,3},{3,2},{4,5},{5,4},{6,7},{7,6},{8,9},{9,8},{10,11... | collective-permute-start | bytes 3145736 | tf_op jit(solution)/shard_map/ppermute | solution.py:26
  87.3 12.8 %collective-permute-start.7 = (bf16[128,4096]{1,0:T(8,128)(2,1)S(1)}, bf16[128,4096]{1,0:T(8,128)(2,1)S(1)}, u32[]{:S(2)}, u32[]{:S(2)}) collective-permute-start(bf16[128,4096]{1,0:T(8,128)(2,1)S(1)} %get-tuple-element.28), channel_id=1, source_target_pairs={{0,1},{1,0},{2,3},{3,2},{4,5},{5,4},{6,7},{7,6},{8,9},{9,8},{10,11... | collective-permute-start | bytes 3145736 | tf_op jit(solution)/shard_map/ppermute | solution.py:26
  91.9 10.9 %collective-permute-start.17 = (bf16[32,4096]{1,0:T(8,128)(2,1)S(1)}, bf16[32,4096]{1,0:T(8,128)(2,1)S(1)}, u32[]{:S(2)}, u32[]{:S(2)}) collective-permute-start(bf16[32,4096]{1,0:T(8,128)(2,1)S(1)} %get-tuple-element.31), channel_id=1, source_target_pairs={{0,2},{1,3},{2,0},{3,1},{4,6},{5,7},{6,4},{7,5},{8,10},{9,11},{10,... | collective-permute-start | bytes 786440 | tf_op jit(solution)/shard_map/ppermute | solution.py:26
  99.7 12.9 %collective-permute-start.45 = (bf16[32,4096]{1,0:T(8,128)(2,1)S(1)}, bf16[32,4096]{1,0:T(8,128)(2,1)S(1)}, u32[]{:S(2)}, u32[]{:S(2)}) collective-permute-start(bf16[32,4096]{1,0:T(8,128)(2,1)S(1)} %get-tuple-element.45), channel_id=1, source_target_pairs={{0,4},{1,5},{2,6},{3,7},{4,0},{5,1},{6,2},{7,3},{8,12},{9,13},{10,... | collective-permute-start | bytes 786440 | tf_op jit(solution)/shard_map/ppermute | solution.py:26
  100.1 13.8 %collective-permute-start.46 = (bf16[32,4096]{1,0:T(8,128)(2,1)S(1)}, bf16[32,4096]{1,0:T(8,128)(2,1)S(1)}, u32[]{:S(2)}, u32[]{:S(2)}) collective-permute-start(bf16[32,4096]{1,0:T(8,128)(2,1)S(1)} %get-tuple-element.46), channel_id=1, source_target_pairs={{0,2},{1,3},{2,0},{3,1},{4,6},{5,7},{6,4},{7,5},{8,10},{9,11},{10,... | collective-permute-start | bytes 786440 | tf_op jit(solution)/shard_map/ppermute | solution.py:26
  102.8 15.8 %collective-permute-start.47 = (bf16[32,4096]{1,0:T(8,128)(2,1)S(1)}, bf16[32,4096]{1,0:T(8,128)(2,1)S(1)}, u32[]{:S(2)}, u32[]{:S(2)}) collective-permute-start(bf16[32,4096]{1,0:T(8,128)(2,1)S(1)} %get-tuple-element.47), channel_id=1, source_target_pairs={{0,16},{1,17},{2,18},{3,19},{4,20},{5,21},{6,22},{7,23},{8,24},{9,... | collective-permute-start | bytes 786440 | tf_op jit(solution)/shard_map/ppermute | solution.py:26
  103.8 14.8 %collective-permute-start.48 = (bf16[32,4096]{1,0:T(8,128)(2,1)S(1)}, bf16[32,4096]{1,0:T(8,128)(2,1)S(1)}, u32[]{:S(2)}, u32[]{:S(2)}) collective-permute-start(bf16[32,4096]{1,0:T(8,128)(2,1)S(1)} %get-tuple-element.48), channel_id=1, source_target_pairs={{0,18},{1,19},{2,16},{3,17},{4,22},{5,23},{6,20},{7,21},{8,26},{9,... | collective-permute-start | bytes 786440 | tf_op jit(solution)/shard_map/ppermute | solution.py:26
  107.3 15.2 %collective-permute-start.20 = (bf16[32,4096]{1,0:T(8,128)(2,1)S(1)}, bf16[32,4096]{1,0:T(8,128)(2,1)S(1)}, u32[]{:S(2)}, u32[]{:S(2)}) collective-permute-start(bf16[32,4096]{1,0:T(8,128)(2,1)S(1)} %get-tuple-element.34), channel_id=1, source_target_pairs={{0,4},{1,5},{2,6},{3,7},{4,0},{5,1},{6,2},{7,3},{8,12},{9,13},{10,... | collective-permute-start | bytes 786440 | tf_op jit(solution)/shard_map/ppermute | solution.py:26
  114.0 12.3 %collective-permute-start.22 = (bf16[32,4096]{1,0:T(8,128)(2,1)S(1)}, bf16[32,4096]{1,0:T(8,128)(2,1)S(1)}, u32[]{:S(2)}, u32[]{:S(2)}) collective-permute-start(bf16[32,4096]{1,0:T(8,128)(2,1)S(1)} %get-tuple-element.36), channel_id=1, source_target_pairs={{0,16},{1,17},{2,18},{3,19},{4,20},{5,21},{6,22},{7,23},{8,24},{9,... | collective-permute-start | bytes 786440 | tf_op jit(solution)/shard_map/ppermute | solution.py:26
  (34 other events, 232.0 us)

commit v3 on v2

--- a/solution.py
+++ b/solution.py
@@ -9,8 +9,6 @@
 
 BOTH = ("sec", "dev")
 CORE, X, ZA, ZB, Y = 1, 2, 4, 8, 16
-NEAR = (0, ZA, X, Y)
-FAR = (X | Y, X | ZA, Y | ZA, X | Y | ZA)
 TERMS = 3
 VMEM = pl.BlockSpec(memory_space=pltpu.VMEM)
 
@@ -107,18 +105,32 @@
     )
 
 
-def add_body(plan, count, *refs):
-    for out, parts in zip(refs[count:], plan):
-        rows = out.shape[0]
-        total = 0.0
-        for ref, at in parts:
-            total = total + refs[ref][at * rows : (at + 1) * rows, :].astype(jnp.float32)
-        out[...] = total.astype(jnp.bfloat16)
-
-
-def add_up(plan, arrays, rows):
-    shapes = [(rows, arrays[0].shape[1])] * len(plan)
-    return local(functools.partial(add_body, plan, len(arrays)), shapes, arrays, limit=4)
+def add_body(plan, count, rows, *refs):
+    for out, blocks in zip(refs[count:], plan):
+        for at, parts in enumerate(blocks):
+            cut = [refs[ref][place * rows : (place + 1) * rows, :] for ref, place in parts]
+            if len(cut) > 1:
+                cut = [sum(part.astype(jnp.float32) for part in cut).astype(jnp.bfloat16)]
+            out[at * rows : (at + 1) * rows, :] = cut[0]
+
+
+def combine(wanted, pieces, rows):
+    plan = [
+        [
+            [(ref, names.index(m)) for ref, (names, _) in enumerate(pieces) if m in names]
+            for m in blocks
+        ]
+        for blocks in wanted
+    ]
+    arrays = [array for _, array in pieces]
+    width = arrays[0].shape[1]
+    outs = local(
+        functools.partial(add_body, plan, len(arrays), rows),
+        [(len(blocks) * rows, width) for blocks in wanted],
+        arrays,
+        limit=4,
+    )
+    return list(zip(wanted, outs))
 
 
 def spread(hidden_in, routes, scores, w_gate, w_up, w_down):
@@ -128,48 +140,59 @@
     lanes = jnp.arange(128)
     mine = (lanes % experts == lax.axis_index("dev")) & (lanes < TERMS * experts)
     mine = mine.astype(jnp.float32)[None, :]
-    weights = (mine, w_gate[0], w_up[0], w_down[0])
-    held = {0: prepare(hidden_in, routes, scores, experts)}
-
-    def send(link, block):
-        held[block ^ link] = swap(held[block], link, devices)
-
-    send(ZB, 0)
-    for top in (0, ZB):
-        for link in (ZA, X, Y, X | Y):
-            send(link, top)
-        send(X, top | ZA)
-        send(Y, top | ZA)
-        send(ZA, top | X | Y)
-    for m in list(held):
-        send(CORE, m)
-
-    outs = {}
-    for top in (0, ZB):
-        for at, group in enumerate((NEAR, FAR)):
-            group = [top | m for m in group]
-            own, other = expert_rows([held[m] for m in group] + [held[m ^ CORE] for m in group], *weights)
-            outs[top, at] = own, swap(other, CORE, devices)
-
-    ends = []
-    for top in (0, ZB):
-        far, near = outs[top, 1], outs[top, 0]
-        xa, ya, xya = add_up([[(0, at), (1, at)] for at in (1, 2, 3)], far, rows)
-        xa, ya, xya = swap(xa, X, devices), swap(ya, Y, devices), swap(xya, ZA, devices)
-        a, x, y, xy = add_up(
-            [
-                [(0, 1), (1, 1), (4, 0), (5, 0)],
-                [(0, 2), (1, 2)],
-                [(0, 3), (1, 3)],
-                [(2, 0), (3, 0), (6, 0)],
-            ],
-            (*near, *far, xa, ya, xya),
-            rows,
-        )
-        ends.append((*near, swap(a, ZA, devices), swap(x, X, devices), swap(y, Y, devices), swap(xy, X | Y, devices)))
-    whole = [(at, 0) for at in range(6)]
-    top = add_up([whole], ends[1], rows)[0]
-    return add_up([[*whole, (6, 0)]], (*ends[0], swap(top, ZB, devices)), rows)[0]
+    weights = w_gate[0], w_up[0], w_down[0]
+
+    def send(link, piece):
+        names, array = piece
+        return tuple(m ^ link for m in names), swap(array, link, devices)
+
+    def sums(group):
+        there = swap(group[1], CORE, devices)
+        own, other = expert_rows([group[1], there], mine, *weights)
+        return [(group[0], own), (group[0], swap(other, CORE, devices))]
+
+    def tie(*pieces):
+        arrays = lax.optimization_barrier(tuple(array for _, array in pieces))
+        return [(names, array) for (names, _), array in zip(pieces, arrays)]
+
+    start = [0], prepare(hidden_in, routes, scores, experts)
+    za, x, y, zb, xy = [send(link, start) for link in (ZA, X, Y, ZB, X | Y)]
+    near0, zs, ps = combine(
+        [[0, ZA, X, Y], [ZA, ZB], [X | Y, ZB]], [start, za, x, y, zb, xy], rows
+    )
+    got = [send(X, zs), send(Y, zs), send(ZA, ps), send(X | Y, zb)]
+    near0 = sums(near0)
+    near0[0], *got = tie(near0[0], xy, zb, *got)
+    far0, near1, zab, xyb = combine(
+        [
+            [X | Y, X | ZA, Y | ZA, X | Y | ZA],
+            [ZB, ZA | ZB, X | ZB, Y | ZB],
+            [ZA | ZB],
+            [X | Y | ZB],
+        ],
+        got,
+        rows,
+    )
+    got = [send(X, zab), send(Y, zab), send(ZA, xyb)]
+    far0 = sums(far0)
+    near1 = sums(near1)
+    far0[0], near1[0], *got = tie(far0[0], near1[0], xyb, *got)
+    (far1,) = combine([[X | Y | ZB, X | ZA | ZB, Y | ZA | ZB, X | Y | ZA | ZB]], got, rows)
+    far1 = sums(far1)
+
+    x, y = combine([[X], [Y]], near0, rows)
+    end = [*near0, send(X, x), send(Y, y)]
+    x, y, xya = combine(
+        [[X | ZA, X | ZB], [Y | ZA, Y | ZB], [X | Y | ZA]], [*far0, *near1], rows
+    )
+    x, y, xya = send(X, x), send(Y, y), send(ZA, xya)
+    xa, ya, xyab = combine([[X | ZA | ZB], [Y | ZA | ZB], [X | Y | ZA | ZB]], far1, rows)
+    xa, ya, xyab = send(X, xa), send(Y, ya), send(ZA, xyab)
+    za, xy = combine([[ZA], [X | Y]], [*near0, *far0, x, y, xya], rows)
+    end += [send(ZA, za), send(X | Y, xy)]
+    zab, xyb = combine([[ZA | ZB], [X | Y | ZB]], [*near1, *far1, xa, ya, xyab], rows)
+    (zb,) = combine([[ZB]], [*near1, x, y, send(ZA, zab), send(X | Y, xyb)], rows)
+    return combine([[0]], [*end, send(ZB, zb)], rows)[0][1]
 
 
 def dispatch(hidden_in, routes, scores, w_gate, w_up, w_down):

time: 131 us -> 115 us (0.88)
  starting transfers between devices: 43.9 us -> 35.6 us
  waiting for transfers between devices: 46.8 us -> 40.9 us
    ppermute x50 -> x33, starting transfers between devices: 43.9 us -> 35.6 us  [swap(): return lax.ppermute(block, BOTH, [(i, i ^ mask) for i in range(devices)])]
    ppermute x50 -> x33, waiting for transfers between devices: 46.8 us -> 40.9 us  [swap(): return lax.ppermute(block, BOTH, [(i, i ^ mask) for i in range(devices)])]
    pallas_call x11 -> x15, Pallas kernels: 27.2 us -> 26.4 us  [local(): pl.pallas_call(body, out_shape=[jax.ShapeDtypeStruct(shape, jnp.bfloat16)...]
  transfers between devices with their start and end apart: 50 -> 33, of which waited for: 16 -> 15; matrix products, arithmetic and copies ran while one was open for 0% -> 0% of each run, Pallas kernels for 20% -> 16%
where the time goes in v3:
time: 115 us
  waiting for transfers between devices  40.9 us (36%)
  starting transfers between devices  35.6 us (31%)
  Pallas kernels  26.4 us (23%)
  local copies, waits for them, and re-layouts  11.6 us (10%)
    ppermute x33, waiting for transfers between devices, swap(): return lax.ppermute(block, BOTH, [(i, i ^ mask) for i in range(devices)])  40.9 us
    ppermute x33, starting transfers between devices, swap(): return lax.ppermute(block, BOTH, [(i, i ^ mask) for i in range(devices)])  35.6 us
    pallas_call x15, Pallas kernels, local(): pl.pallas_call(body, out_shape=[jax.ShapeDtypeStruct(shape, jnp.bfloat16)...  26.4 us
    unnamed x18, local copies, waits for them, and re-layouts  11.6 us
  transfers between devices with their start and end apart: 33, of which 15 were waited for; matrix products, arithmetic and copies ran while one was open for 0% of the time, Pallas kernels for 16%

profile of v3, /device:TPU:0, one launch (start us, length us, event | category | flops | bytes accessed | tf_op | source)
XLA Modules:
  0.0 114.6 jit_solution(6897713820050276391)
XLA Ops:
  2.7 3.1 %collective-permute-start = (bf16[32,4224]{1,0:T(8,128)(2,1)S(1)}, bf16[32,4224]{1,0:T(8,128)(2,1)S(1)}, u32[]{:S(2)}, u32[]{:S(2)}) collective-permute-start(bf16[32,4224]{1,0:T(8,128)(2,1)S(1)} %shard_map.64.refs_0_), channel_id=1, source_target_pairs={{0,4},{1,5},{2,6},{3,7},{4,0},{5,1},{6,2},{7,3},{8,12},{9,13},{10,... | collective-permute-start | bytes 811016 | tf_op jit(solution)/shard_map/ppermute | solution.py:24
  8.8 2.6 %collective-permute-start.3 = (bf16[32,4224]{1,0:T(8,128)(2,1)S(1)}, bf16[32,4224]{1,0:T(8,128)(2,1)S(1)}, u32[]{:S(2)}, u32[]{:S(2)}) collective-permute-start(bf16[32,4224]{1,0:T(8,128)(2,1)S(1)} %shard_map.64.refs_0_), channel_id=1, source_target_pairs={{0,8},{1,9},{2,10},{3,11},{4,12},{5,13},{6,14},{7,15},{8,0},{9,1},... | collective-permute-start | bytes 811016 | tf_op jit(solution)/shard_map/ppermute | solution.py:24
  11.9 3.3 %collective-permute-done.refs_1_ = bf16[32,4224]{1,0:T(8,128)(2,1)S(1)} collective-permute-done((bf16[32,4224]{1,0:T(8,128)(2,1)S(1)}, bf16[32,4224]{1,0:T(8,128)(2,1)S(1)}, u32[]{:S(2)}, u32[]{:S(2)}) %collective-permute-start) | collective-permute-done | bytes 270368 | tf_op jit(solution)/shard_map/ppermute | solution.py:24
  15.2 5.5 %collective-permute-done.2.refs_3_ = bf16[32,4224]{1,0:T(8,128)(2,1)S(1)} collective-permute-done((bf16[32,4224]{1,0:T(8,128)(2,1)S(1)}, bf16[32,4224]{1,0:T(8,128)(2,1)S(1)}, u32[]{:S(2)}, u32[]{:S(2)}) %collective-permute-start.2) | collective-permute-done | bytes 270368 | tf_op jit(solution)/shard_map/ppermute | solution.py:24
  20.7 2.2 %collective-permute-done.3.refs_4_.refs_1_ = bf16[32,4224]{1,0:T(8,128)(2,1)S(1)} collective-permute-done((bf16[32,4224]{1,0:T(8,128)(2,1)S(1)}, bf16[32,4224]{1,0:T(8,128)(2,1)S(1)}, u32[]{:S(2)}, u32[]{:S(2)}) %collective-permute-start.3) | collective-permute-done | bytes 270368 | tf_op jit(solution)/shard_map/ppermute | solution.py:24
  24.9 2.5 %collective-permute-start.9 = (bf16[32,4224]{1,0:T(8,128)(2,1)S(1)}, bf16[32,4224]{1,0:T(8,128)(2,1)S(1)}, u32[]{:S(2)}, u32[]{:S(2)}) collective-permute-start(bf16[32,4224]{1,0:T(8,128)(2,1)S(1)} %collective-permute-done.3.refs_4_.refs_1_), channel_id=1, source_target_pairs={{0,18},{1,19},{2,16},{3,17},{4,22},{5,23},{6,20},{7,21},{8,26},{9,... | collective-permute-start | bytes 811016 | tf_op jit(solution)/shard_map/ppermute | solution.py:24
  27.5 2.8 %copy-done = bf16[1,4096,768]{2,1,0:T(8,128)(2,1)S(1)} copy-done((bf16[1,4096,768]{2,1,0:T(8,128)(2,1)S(1)}, bf16[1,4096,768]{2,1,0:T(8,128)(2,1)}, u32[]{:S(2)}) %copy-start) | copy-done | bytes 6291480
  30.2 2.8 %copy-done.2 = bf16[1,4096,768]{2,1,0:T(8,128)(2,1)S(1)} copy-done((bf16[1,4096,768]{2,1,0:T(8,128)(2,1)S(1)}, bf16[1,4096,768]{2,1,0:T(8,128)(2,1)}, u32[]{:S(2)}) %copy-start.2) | copy-done | bytes 6291480
  33.0 2.8 %copy-done.4 = bf16[1,768,4096]{2,1,0:T(8,128)(2,1)S(1)} copy-done((bf16[1,768,4096]{2,1,0:T(8,128)(2,1)S(1)}, bf16[1,768,4096]{2,1,0:T(8,128)(2,1)}, u32[]{:S(2)}) %copy-start.4) | copy-done | bytes 6291480
  35.8 6.0 %shard_map.66 = (bf16[128,4096]{1,0:T(8,128)(2,1)S(1)}, bf16[128,4096]{1,0:T(8,128)(2,1)S(1)}) custom-call(f32[1,128]{1,0:T(1,128)S(1)} %and_convert_fusion.mine_ref, bf16[128,4224]{1,0:T(8,128)(2,1)S(1)} %get-tuple-element.45.refs_0_, bf16[128,4224]{1,0:T(8,128)(2,1)S(1)} %collective-permute-done.5.refs_1_, bf16[4096,768]{1,0:T(8,128)(2,1)S(1)} %bitcast.3, ...), custom_call_target="tpu_custom_call" | custom-call | flops 4831838208 | bytes 2097152 | tf_op jit(solution)/shard_map/pallas_call | solution.py:35
  41.8 2.8 %collective-permute-done.9.refs_5_ = bf16[32,4224]{1,0:T(8,128)(2,1)S(1)} collective-permute-done((bf16[32,4224]{1,0:T(8,128)(2,1)S(1)}, bf16[32,4224]{1,0:T(8,128)(2,1)S(1)}, u32[]{:S(2)}, u32[]{:S(2)}) %collective-permute-start.9) | collective-permute-done | bytes 270368 | tf_op jit(solution)/shard_map/ppermute | solution.py:24
  47.8 5.8 %shard_map.69 = (bf16[128,4096]{1,0:T(8,128)(2,1)S(1)}, bf16[128,4096]{1,0:T(8,128)(2,1)S(1)}) custom-call(f32[1,128]{1,0:T(1,128)S(1)} %and_convert_fusion.mine_ref, bf16[128,4224]{1,0:T(8,128)(2,1)S(1)} %get-tuple-element.59.refs_0_, bf16[128,4224]{1,0:T(8,128)(2,1)S(1)} %collective-permute-done.13.refs_1_, bf16[4096,768]{1,0:T(8,128)(2,1)S(1)} %bitcast.4, ...), custom_call_target="tpu_custom_call" | custom-call | flops 4831838208 | bytes 2097152 | tf_op jit(solution)/shard_map/pallas_call | solution.py:35
  53.6 5.8 %shard_map.70 = (bf16[128,4096]{1,0:T(8,128)(2,1)S(1)}, bf16[128,4096]{1,0:T(8,128)(2,1)S(1)}) custom-call(f32[1,128]{1,0:T(1,128)S(1)} %and_convert_fusion.mine_ref, bf16[128,4224]{1,0:T(8,128)(2,1)S(1)} %get-tuple-element.61.refs_0_, bf16[128,4224]{1,0:T(8,128)(2,1)S(1)} %collective-permute-done.14.refs_1_, bf16[4096,768]{1,0:T(8,128)(2,1)S(1)} %bitcast.5, ...), custom_call_target="tpu_custom_call" | custom-call | flops 4831838208 | bytes 2097152 | tf_op jit(solution)/shard_map/pallas_call | solution.py:35
  59.8 2.6 %collective-permute-done.25.refs_1_ = bf16[128,4224]{1,0:T(8,128)(2,1)S(1)} collective-permute-done((bf16[128,4224]{1,0:T(8,128)(2,1)S(1)}, bf16[128,4224]{1,0:T(8,128)(2,1)S(1)}, u32[]{:S(2)}, u32[]{:S(2)}) %collective-permute-start.25) | collective-permute-done | bytes 1081376 | tf_op jit(solution)/shard_map/ppermute | solution.py:24
  62.4 6.0 %shard_map.74 = (bf16[128,4096]{1,0:T(8,128)(2,1)S(1)}, bf16[128,4096]{1,0:T(8,128)(2,1)S(1)}) custom-call(f32[1,128]{1,0:T(1,128)S(1)} %and_convert_fusion.mine_ref, bf16[128,4224]{1,0:T(8,128)(2,1)S(1)} %shard_map.73.refs_0_, bf16[128,4224]{1,0:T(8,128)(2,1)S(1)} %collective-permute-done.25.refs_1_, bf16[4096,768]{1,0:T(8,128)(2,1)S(1)} %bitcast.6, ...), custom_call_target="tpu_custom_call" | custom-call | flops 4831838208 | bytes 2097152 | tf_op jit(solution)/shard_map/pallas_call | solution.py:35
  76.4 4.0 %collective-permute-done.27.refs_4_ = bf16[32,4096]{1,0:T(8,128)(2,1)S(1)} collective-permute-done((bf16[32,4096]{1,0:T(8,128)(2,1)S(1)}, bf16[32,4096]{1,0:T(8,128)(2,1)S(1)}, u32[]{:S(2)}, u32[]{:S(2)}) %collective-permute-start.27) | collective-permute-done | bytes 262176 | tf_op jit(solution)/shard_map/ppermute | solution.py:24
  80.5 1.8 %collective-permute-start.29 = (bf16[32,4096]{1,0:T(8,128)(2,1)S(1)}, bf16[32,4096]{1,0:T(8,128)(2,1)S(1)}, u32[]{:S(2)}, u32[]{:S(2)}) collective-permute-start(bf16[32,4096]{1,0:T(8,128)(2,1)S(1)} %get-tuple-element.82), channel_id=1, source_target_pairs={{0,4},{1,5},{2,6},{3,7},{4,0},{5,1},{6,2},{7,3},{8,12},{9,13},{10,... | collective-permute-start | bytes 786440 | tf_op jit(solution)/shard_map/ppermute | solution.py:24
  83.6 6.1 %collective-permute-done.29.refs_6_ = bf16[32,4096]{1,0:T(8,128)(2,1)S(1)} collective-permute-done((bf16[32,4096]{1,0:T(8,128)(2,1)S(1)}, bf16[32,4096]{1,0:T(8,128)(2,1)S(1)}, u32[]{:S(2)}, u32[]{:S(2)}) %collective-permute-start.29) | collective-permute-done | bytes 262176 | tf_op jit(solution)/shard_map/ppermute | solution.py:24
  89.9 1.9 %collective-permute-start.30 = (bf16[32,4096]{1,0:T(8,128)(2,1)S(1)}, bf16[32,4096]{1,0:T(8,128)(2,1)S(1)}, u32[]{:S(2)}, u32[]{:S(2)}) collective-permute-start(bf16[32,4096]{1,0:T(8,128)(2,1)S(1)} %get-tuple-element.83), channel_id=1, source_target_pairs={{0,4},{1,5},{2,6},{3,7},{4,0},{5,1},{6,2},{7,3},{8,12},{9,13},{10,... | collective-permute-start | bytes 786440 | tf_op jit(solution)/shard_map/ppermute | solution.py:24
  93.5 1.9 %collective-permute-done.22.refs_6_ = bf16[32,4096]{1,0:T(8,128)(2,1)S(1)} collective-permute-done((bf16[32,4096]{1,0:T(8,128)(2,1)S(1)}, bf16[32,4096]{1,0:T(8,128)(2,1)S(1)}, u32[]{:S(2)}, u32[]{:S(2)}) %collective-permute-start.22) | collective-permute-done | bytes 262176 | tf_op jit(solution)/shard_map/ppermute | solution.py:24
  97.6 2.0 %collective-permute-start.23 = (bf16[32,4096]{1,0:T(8,128)(2,1)S(1)}, bf16[32,4096]{1,0:T(8,128)(2,1)S(1)}, u32[]{:S(2)}, u32[]{:S(2)}) collective-permute-start(bf16[32,4096]{1,0:T(8,128)(2,1)S(1)} %get-tuple-element.72), channel_id=1, source_target_pairs={{0,4},{1,5},{2,6},{3,7},{4,0},{5,1},{6,2},{7,3},{8,12},{9,13},{10,... | collective-permute-start | bytes 786440 | tf_op jit(solution)/shard_map/ppermute | solution.py:24
  102.6 3.0 %collective-permute-start.32 = (bf16[32,4096]{1,0:T(8,128)(2,1)S(1)}, bf16[32,4096]{1,0:T(8,128)(2,1)S(1)}, u32[]{:S(2)}, u32[]{:S(2)}) collective-permute-start(bf16[32,4096]{1,0:T(8,128)(2,1)S(1)} %shard_map.77), channel_id=1, source_target_pairs={{0,8},{1,9},{2,10},{3,11},{4,12},{5,13},{6,14},{7,15},{8,0},{9,1},... | collective-permute-start | bytes 786440 | tf_op jit(solution)/shard_map/ppermute | solution.py:24
  105.6 3.4 %collective-permute-done.12.refs_3_ = bf16[32,4096]{1,0:T(8,128)(2,1)S(1)} collective-permute-done((bf16[32,4096]{1,0:T(8,128)(2,1)S(1)}, bf16[32,4096]{1,0:T(8,128)(2,1)S(1)}, u32[]{:S(2)}, u32[]{:S(2)}) %collective-permute-start.12) | collective-permute-done | bytes 262176 | tf_op jit(solution)/shard_map/ppermute | solution.py:24
  109.0 4.7 %collective-permute-done.32.refs_6_ = bf16[32,4096]{1,0:T(8,128)(2,1)S(1)} collective-permute-done((bf16[32,4096]{1,0:T(8,128)(2,1)S(1)}, bf16[32,4096]{1,0:T(8,128)(2,1)S(1)}, u32[]{:S(2)}, u32[]{:S(2)}) %collective-permute-start.32) | collective-permute-done | bytes 262176 | tf_op jit(solution)/shard_map/ppermute | solution.py:24
  (76 shorter events, 29.1 us)
Async XLA Ops:
  2.7 12.5 %collective-permute-start = (bf16[32,4224]{1,0:T(8,128)(2,1)S(1)}, bf16[32,4224]{1,0:T(8,128)(2,1)S(1)}, u32[]{:S(2)}, u32[]{:S(2)}) collective-permute-start(bf16[32,4224]{1,0:T(8,128)(2,1)S(1)} %shard_map.64.refs_0_), channel_id=1, source_target_pairs={{0,4},{1,5},{2,6},{3,7},{4,0},{5,1},{6,2},{7,3},{8,12},{9,13},{10,... | collective-permute-start | bytes 811016 | tf_op jit(solution)/shard_map/ppermute | solution.py:24
  5.8 9.4 %collective-permute-start.1 = (bf16[32,4224]{1,0:T(8,128)(2,1)S(1)}, bf16[32,4224]{1,0:T(8,128)(2,1)S(1)}, u32[]{:S(2)}, u32[]{:S(2)}) collective-permute-start(bf16[32,4224]{1,0:T(8,128)(2,1)S(1)} %shard_map.64.refs_0_), channel_id=1, source_target_pairs={{0,2},{1,3},{2,0},{3,1},{4,6},{5,7},{6,4},{7,5},{8,10},{9,11},{10,... | collective-permute-start | bytes 811016 | tf_op jit(solution)/shard_map/ppermute | solution.py:24
  7.3 13.5 %collective-permute-start.2 = (bf16[32,4224]{1,0:T(8,128)(2,1)S(1)}, bf16[32,4224]{1,0:T(8,128)(2,1)S(1)}, u32[]{:S(2)}, u32[]{:S(2)}) collective-permute-start(bf16[32,4224]{1,0:T(8,128)(2,1)S(1)} %shard_map.64.refs_0_), channel_id=1, source_target_pairs={{0,16},{1,17},{2,18},{3,19},{4,20},{5,21},{6,22},{7,23},{8,24},{9,... | collective-permute-start | bytes 811016 | tf_op jit(solution)/shard_map/ppermute | solution.py:24
  8.8 14.1 %collective-permute-start.3 = (bf16[32,4224]{1,0:T(8,128)(2,1)S(1)}, bf16[32,4224]{1,0:T(8,128)(2,1)S(1)}, u32[]{:S(2)}, u32[]{:S(2)}) collective-permute-start(bf16[32,4224]{1,0:T(8,128)(2,1)S(1)} %shard_map.64.refs_0_), channel_id=1, source_target_pairs={{0,8},{1,9},{2,10},{3,11},{4,12},{5,13},{6,14},{7,15},{8,0},{9,1},... | collective-permute-start | bytes 811016 | tf_op jit(solution)/shard_map/ppermute | solution.py:24
  11.4 11.5 %collective-permute-start.4 = (bf16[32,4224]{1,0:T(8,128)(2,1)S(1)}, bf16[32,4224]{1,0:T(8,128)(2,1)S(1)}, u32[]{:S(2)}, u32[]{:S(2)}) collective-permute-start(bf16[32,4224]{1,0:T(8,128)(2,1)S(1)} %shard_map.64.refs_0_), channel_id=1, source_target_pairs={{0,18},{1,19},{2,16},{3,17},{4,22},{5,23},{6,20},{7,21},{8,26},{9,... | collective-permute-start | bytes 811016 | tf_op jit(solution)/shard_map/ppermute | solution.py:24
  23.9 20.7 %collective-permute-start.6 = (bf16[64,4224]{1,0:T(8,128)(2,1)}, bf16[64,4224]{1,0:T(8,128)(2,1)S(1)}, u32[]{:S(2)}, u32[]{:S(2)}) collective-permute-start(bf16[64,4224]{1,0:T(8,128)(2,1)} %copy-done.7), channel_id=1, source_target_pairs={{0,2},{1,3},{2,0},{3,1},{4,6},{5,7},{6,4},{7,5},{8,10},{9,11},{10,... | collective-permute-start | bytes 1622024 | tf_op jit(solution)/shard_map/ppermute | solution.py:24
  24.4 20.4 %collective-permute-start.7 = (bf16[64,4224]{1,0:T(8,128)(2,1)}, bf16[64,4224]{1,0:T(8,128)(2,1)S(1)}, u32[]{:S(2)}, u32[]{:S(2)}) collective-permute-start(bf16[64,4224]{1,0:T(8,128)(2,1)} %copy-done.7), channel_id=1, source_target_pairs={{0,16},{1,17},{2,18},{3,19},{4,20},{5,21},{6,22},{7,23},{8,24},{9,... | collective-permute-start | bytes 1622024 | tf_op jit(solution)/shard_map/ppermute | solution.py:24
  24.9 19.9 %collective-permute-start.8 = (bf16[64,4224]{1,0:T(8,128)(2,1)S(1)}, bf16[64,4224]{1,0:T(8,128)(2,1)S(1)}, u32[]{:S(2)}, u32[]{:S(2)}) collective-permute-start(bf16[64,4224]{1,0:T(8,128)(2,1)S(1)} %get-tuple-element.48), channel_id=1, source_target_pairs={{0,4},{1,5},{2,6},{3,7},{4,0},{5,1},{6,2},{7,3},{8,12},{9,13},{10,... | collective-permute-start | bytes 1622024 | tf_op jit(solution)/shard_map/ppermute | solution.py:24
  24.9 19.7 %collective-permute-start.9 = (bf16[32,4224]{1,0:T(8,128)(2,1)S(1)}, bf16[32,4224]{1,0:T(8,128)(2,1)S(1)}, u32[]{:S(2)}, u32[]{:S(2)}) collective-permute-start(bf16[32,4224]{1,0:T(8,128)(2,1)S(1)} %collective-permute-done.3.refs_4_.refs_1_), channel_id=1, source_target_pairs={{0,18},{1,19},{2,16},{3,17},{4,22},{5,23},{6,20},{7,21},{8,26},{9,... | collective-permute-start | bytes 811016 | tf_op jit(solution)/shard_map/ppermute | solution.py:24
  45.6 13.9 %collective-permute-start.15 = (bf16[32,4224]{1,0:T(8,128)(2,1)S(1)}, bf16[32,4224]{1,0:T(8,128)(2,1)S(1)}, u32[]{:S(2)}, u32[]{:S(2)}) collective-permute-start(bf16[32,4224]{1,0:T(8,128)(2,1)S(1)} %get-tuple-element.64), channel_id=1, source_target_pairs={{0,2},{1,3},{2,0},{3,1},{4,6},{5,7},{6,4},{7,5},{8,10},{9,11},{10,... | collective-permute-start | bytes 811016 | tf_op jit(solution)/shard_map/ppermute | solution.py:24
  47.1 12.4 %collective-permute-start.16 = (bf16[32,4224]{1,0:T(8,128)(2,1)S(1)}, bf16[32,4224]{1,0:T(8,128)(2,1)S(1)}, u32[]{:S(2)}, u32[]{:S(2)}) collective-permute-start(bf16[32,4224]{1,0:T(8,128)(2,1)S(1)} %get-tuple-element.64), channel_id=1, source_target_pairs={{0,16},{1,17},{2,18},{3,19},{4,20},{5,21},{6,22},{7,23},{8,24},{9,... | collective-permute-start | bytes 811016 | tf_op jit(solution)/shard_map/ppermute | solution.py:24
  47.6 11.9 %collective-permute-start.17 = (bf16[32,4224]{1,0:T(8,128)(2,1)S(1)}, bf16[32,4224]{1,0:T(8,128)(2,1)S(1)}, u32[]{:S(2)}, u32[]{:S(2)}) collective-permute-start(bf16[32,4224]{1,0:T(8,128)(2,1)S(1)} %get-tuple-element.74.refs_0_), channel_id=1, source_target_pairs={{0,4},{1,5},{2,6},{3,7},{4,0},{5,1},{6,2},{7,3},{8,12},{9,13},{10,... | collective-permute-start | bytes 811016 | tf_op jit(solution)/shard_map/ppermute | solution.py:24
  69.1 22.8 %collective-permute-start.10 = (bf16[128,4096]{1,0:T(8,128)(2,1)S(1)}, bf16[128,4096]{1,0:T(8,128)(2,1)S(1)}, u32[]{:S(2)}, u32[]{:S(2)}) collective-permute-start(bf16[128,4096]{1,0:T(8,128)(2,1)S(1)} %get-tuple-element.50), channel_id=1, source_target_pairs={{0,1},{1,0},{2,3},{3,2},{4,5},{5,4},{6,7},{7,6},{8,9},{9,8},{10,11... | collective-permute-start | bytes 3145736 | tf_op jit(solution)/shard_map/ppermute | solution.py:24
  72.8 9.5 %collective-permute-start.28 = (bf16[32,4096]{1,0:T(8,128)(2,1)S(1)}, bf16[32,4096]{1,0:T(8,128)(2,1)S(1)}, u32[]{:S(2)}, u32[]{:S(2)}) collective-permute-start(bf16[32,4096]{1,0:T(8,128)(2,1)S(1)} %get-tuple-element.81), channel_id=1, source_target_pairs={{0,16},{1,17},{2,18},{3,19},{4,20},{5,21},{6,22},{7,23},{8,24},{9,... | collective-permute-start | bytes 786440 | tf_op jit(solution)/shard_map/ppermute | solution.py:24
  74.4 22.4 %collective-permute-start.20 = (bf16[64,4096]{1,0:T(8,128)(2,1)S(1)}, bf16[64,4096]{1,0:T(8,128)(2,1)S(1)}, u32[]{:S(2)}, u32[]{:S(2)}) collective-permute-start(bf16[64,4096]{1,0:T(8,128)(2,1)S(1)} %get-tuple-element.69), channel_id=1, source_target_pairs={{0,2},{1,3},{2,0},{3,1},{4,6},{5,7},{6,4},{7,5},{8,10},{9,11},{10,... | collective-permute-start | bytes 1572872 | tf_op jit(solution)/shard_map/ppermute | solution.py:24
  75.9 21.4 %collective-permute-start.21 = (bf16[64,4096]{1,0:T(8,128)(2,1)S(1)}, bf16[64,4096]{1,0:T(8,128)(2,1)S(1)}, u32[]{:S(2)}, u32[]{:S(2)}) collective-permute-start(bf16[64,4096]{1,0:T(8,128)(2,1)S(1)} %get-tuple-element.70), channel_id=1, source_target_pairs={{0,16},{1,17},{2,18},{3,19},{4,20},{5,21},{6,22},{7,23},{8,24},{9,... | collective-permute-start | bytes 1572872 | tf_op jit(solution)/shard_map/ppermute | solution.py:24
  80.5 9.2 %collective-permute-start.29 = (bf16[32,4096]{1,0:T(8,128)(2,1)S(1)}, bf16[32,4096]{1,0:T(8,128)(2,1)S(1)}, u32[]{:S(2)}, u32[]{:S(2)}) collective-permute-start(bf16[32,4096]{1,0:T(8,128)(2,1)S(1)} %get-tuple-element.82), channel_id=1, source_target_pairs={{0,4},{1,5},{2,6},{3,7},{4,0},{5,1},{6,2},{7,3},{8,12},{9,13},{10,... | collective-permute-start | bytes 786440 | tf_op jit(solution)/shard_map/ppermute | solution.py:24
  82.3 13.0 %collective-permute-start.22 = (bf16[32,4096]{1,0:T(8,128)(2,1)S(1)}, bf16[32,4096]{1,0:T(8,128)(2,1)S(1)}, u32[]{:S(2)}, u32[]{:S(2)}) collective-permute-start(bf16[32,4096]{1,0:T(8,128)(2,1)S(1)} %get-tuple-element.71), channel_id=1, source_target_pairs={{0,4},{1,5},{2,6},{3,7},{4,0},{5,1},{6,2},{7,3},{8,12},{9,13},{10,... | collective-permute-start | bytes 786440 | tf_op jit(solution)/shard_map/ppermute | solution.py:24
  89.9 11.0 %collective-permute-start.30 = (bf16[32,4096]{1,0:T(8,128)(2,1)S(1)}, bf16[32,4096]{1,0:T(8,128)(2,1)S(1)}, u32[]{:S(2)}, u32[]{:S(2)}) collective-permute-start(bf16[32,4096]{1,0:T(8,128)(2,1)S(1)} %get-tuple-element.83), channel_id=1, source_target_pairs={{0,4},{1,5},{2,6},{3,7},{4,0},{5,1},{6,2},{7,3},{8,12},{9,13},{10,... | collective-permute-start | bytes 786440 | tf_op jit(solution)/shard_map/ppermute | solution.py:24
  91.8 10.6 %collective-permute-start.31 = (bf16[32,4096]{1,0:T(8,128)(2,1)S(1)}, bf16[32,4096]{1,0:T(8,128)(2,1)S(1)}, u32[]{:S(2)}, u32[]{:S(2)}) collective-permute-start(bf16[32,4096]{1,0:T(8,128)(2,1)S(1)} %get-tuple-element.84), channel_id=1, source_target_pairs={{0,18},{1,19},{2,16},{3,17},{4,22},{5,23},{6,20},{7,21},{8,26},{9,... | collective-permute-start | bytes 786440 | tf_op jit(solution)/shard_map/ppermute | solution.py:24
  95.3 10.2 %collective-permute-start.11 = (bf16[32,4096]{1,0:T(8,128)(2,1)S(1)}, bf16[32,4096]{1,0:T(8,128)(2,1)S(1)}, u32[]{:S(2)}, u32[]{:S(2)}) collective-permute-start(bf16[32,4096]{1,0:T(8,128)(2,1)S(1)} %get-tuple-element.51), channel_id=1, source_target_pairs={{0,2},{1,3},{2,0},{3,1},{4,6},{5,7},{6,4},{7,5},{8,10},{9,11},{10,... | collective-permute-start | bytes 786440 | tf_op jit(solution)/shard_map/ppermute | solution.py:24
  96.8 12.1 %collective-permute-start.12 = (bf16[32,4096]{1,0:T(8,128)(2,1)S(1)}, bf16[32,4096]{1,0:T(8,128)(2,1)S(1)}, u32[]{:S(2)}, u32[]{:S(2)}) collective-permute-start(bf16[32,4096]{1,0:T(8,128)(2,1)S(1)} %get-tuple-element.52), channel_id=1, source_target_pairs={{0,16},{1,17},{2,18},{3,19},{4,20},{5,21},{6,22},{7,23},{8,24},{9,... | collective-permute-start | bytes 786440 | tf_op jit(solution)/shard_map/ppermute | solution.py:24
  97.6 11.4 %collective-permute-start.23 = (bf16[32,4096]{1,0:T(8,128)(2,1)S(1)}, bf16[32,4096]{1,0:T(8,128)(2,1)S(1)}, u32[]{:S(2)}, u32[]{:S(2)}) collective-permute-start(bf16[32,4096]{1,0:T(8,128)(2,1)S(1)} %get-tuple-element.72), channel_id=1, source_target_pairs={{0,4},{1,5},{2,6},{3,7},{4,0},{5,1},{6,2},{7,3},{8,12},{9,13},{10,... | collective-permute-start | bytes 786440 | tf_op jit(solution)/shard_map/ppermute | solution.py:24
  102.6 11.1 %collective-permute-start.32 = (bf16[32,4096]{1,0:T(8,128)(2,1)S(1)}, bf16[32,4096]{1,0:T(8,128)(2,1)S(1)}, u32[]{:S(2)}, u32[]{:S(2)}) collective-permute-start(bf16[32,4096]{1,0:T(8,128)(2,1)S(1)} %shard_map.77), channel_id=1, source_target_pairs={{0,8},{1,9},{2,10},{3,11},{4,12},{5,13},{6,14},{7,15},{8,0},{9,1},... | collective-permute-start | bytes 786440 | tf_op jit(solution)/shard_map/ppermute | solution.py:24
  (17 other events, 93.6 us)

commit v4 on v3

--- a/solution.py
+++ b/solution.py
@@ -31,19 +31,19 @@
     return jnp.dot(hidden_part, w_down, preferred_element_type=jnp.float32)
 
 
-def local(body, outs, operands, scratch=(), limit=8, **cost):
+def local(body, outs, operands, scratch=(), limit=12, after=(), **cost):
     return pl.pallas_call(
         body,
         out_shape=[jax.ShapeDtypeStruct(shape, jnp.bfloat16) for shape in outs],
-        in_specs=[VMEM] * len(operands),
+        in_specs=[VMEM] * len(operands) + [pl.BlockSpec(memory_space=pl.ANY)] * len(after),
         out_specs=[VMEM] * len(outs),
         scratch_shapes=list(scratch),
         compiler_params=pltpu.CompilerParams(vmem_limit_bytes=limit * 2**20),
         cost_estimate=pl.CostEstimate(**{"flops": 0, "transcendentals": 0, "bytes_accessed": 0, **cost}),
-    )(*operands)
-
-
-def prepare_body(experts, hidden_ref, routes_ref, scores_ref, out_ref):
+    )(*operands, *after)
+
+
+def prepare_body(experts, hidden_ref, routes_ref, scores_ref, _, out_ref):
     width = hidden_ref.shape[1]
     out_ref[:, :width] = normalise(hidden_ref[...])
     scores = scores_ref[...]
@@ -61,20 +61,49 @@
     out_ref[:, width:] = packed.astype(jnp.bfloat16)
 
 
-def prepare(hidden_in, routes, scores, experts):
+def prepare(hidden_in, routes, scores, experts, after):
     rows, width = hidden_in.shape
     return local(
-        functools.partial(prepare_body, experts), [(rows, width + 128)], (hidden_in, routes, scores)
+        functools.partial(prepare_body, experts),
+        [(rows, width + 128)],
+        (hidden_in, routes, scores),
+        after=after,
     )[0]
 
 
+def fetch_body(count, after_ref, *refs):
+    sources, outs, (token_ref, sems) = refs[:count], refs[count : 2 * count], refs[2 * count :]
+    token_ref[...] = jnp.zeros(token_ref.shape, token_ref.dtype)
+    copies = [pltpu.make_async_copy(sources[at], outs[at], sems.at[at]) for at in range(count)]
+    for copy in copies:
+        copy.start()
+    for copy in copies:
+        copy.wait()
+
+
+def fetch(arrays, after):
+    sources = [pltpu.with_memory_space_constraint(a, pltpu.HBM) for a in arrays]
+    anywhere = pl.BlockSpec(memory_space=pl.ANY)
+    *outs, token = pl.pallas_call(
+        functools.partial(fetch_body, len(arrays)),
+        out_shape=[pltpu.VMEM(a.shape, a.dtype) for a in arrays]
+        + [jax.ShapeDtypeStruct((16, 128), jnp.bfloat16)],
+        in_specs=[anywhere] * (1 + len(arrays)),
+        out_specs=[VMEM] * (len(arrays) + 1),
+        scratch_shapes=[pltpu.SemaphoreType.DMA((len(arrays),))],
+        compiler_params=pltpu.CompilerParams(vmem_limit_bytes=4 * 2**20),
+    )(after, *sources)
+    return [pltpu.with_memory_space_constraint(a, pltpu.VMEM) for a in outs], token
+
+
 def expert_body(count, mine_ref, *refs):
-    blocks, (gate_ref, up_ref, down_ref), outs = refs[:count], refs[count : count + 3], refs[count + 3 : count + 5]
-    rows_ref, hidden_ref = refs[count + 5 :]
-    rows, width = blocks[0].shape[0], down_ref.shape[1]
+    blocks, (gate_ref, up_ref, down_ref) = refs[:count], refs[count : count + 3]
+    *outs, rows_ref, hidden_ref = refs[count + 3 :]
+    width, first = down_ref.shape[1], 0
     shares = []
-    for at, block in enumerate(blocks):
-        rows_ref[at * rows : (at + 1) * rows, :] = block[:, :width]
+    for block in blocks:
+        rows_ref[first : first + block.shape[0], :] = block[:, :width]
+        first += block.shape[0]
         shares.append(jnp.sum(block[:, width:].astype(jnp.float32) * mine_ref[...], -1, keepdims=True))
     weight = jnp.concatenate(shares, 0)
     for at in range(0, gate_ref.shape[1], 256):
@@ -82,7 +111,7 @@
         gate_part = jnp.dot(rows_ref[...], gate_ref[:, cols], preferred_element_type=jnp.float32)
         up_part = jnp.dot(rows_ref[...], up_ref[:, cols], preferred_element_type=jnp.float32)
         hidden_ref[:, cols] = (gate_part / (1.0 + jnp.exp(-gate_part)) * up_part).astype(jnp.bfloat16)
-    half = count // 2 * rows
+    half = first // 2
 
     @pl.loop(0, width // 1024)
     def _(at):
@@ -93,15 +122,15 @@
 
 
 def expert_rows(blocks, mine, w_gate, w_up, w_down):
-    count, rows = len(blocks), blocks[0].shape[0]
+    rows = sum(block.shape[0] for block in blocks)
     width, units = w_down.shape[1], w_gate.shape[1]
     return local(
-        functools.partial(expert_body, count),
-        [(count // 2 * rows, width)] * 2,
+        functools.partial(expert_body, len(blocks)),
+        [(rows // 2, width)] * 2,
         (mine, *blocks, w_gate, w_up, w_down),
-        [pltpu.VMEM((count * rows, width), jnp.bfloat16), pltpu.VMEM((count * rows, units), jnp.bfloat16)],
-        flops=6 * count * rows * width * units,
-        bytes_accessed=2 * count * rows * width,
+        [pltpu.VMEM((rows, width), jnp.bfloat16), pltpu.VMEM((rows, units), jnp.bfloat16)],
+        flops=6 * rows * width * units,
+        bytes_accessed=2 * rows * width,
     )
 
 
@@ -114,7 +143,7 @@
             out[at * rows : (at + 1) * rows, :] = cut[0]
 
 
-def combine(wanted, pieces, rows):
+def combine(wanted, pieces, rows, after=()):
     plan = [
         [
             [(ref, names.index(m)) for ref, (names, _) in enumerate(pieces) if m in names]
@@ -125,10 +154,11 @@
     arrays = [array for _, array in pieces]
     width = arrays[0].shape[1]
     outs = local(
-        functools.partial(add_body, plan, len(arrays), rows),
+        functools.partial(add_body, plan, len(arrays) + len(after), rows),
         [(len(blocks) * rows, width) for blocks in wanted],
         arrays,
         limit=4,
+        after=after,
     )
     return list(zip(wanted, outs))
 
@@ -140,59 +170,48 @@
     lanes = jnp.arange(128)
     mine = (lanes % experts == lax.axis_index("dev")) & (lanes < TERMS * experts)
     mine = mine.astype(jnp.float32)[None, :]
-    weights = w_gate[0], w_up[0], w_down[0]
 
     def send(link, piece):
         names, array = piece
         return tuple(m ^ link for m in names), swap(array, link, devices)
 
-    def sums(group):
-        there = swap(group[1], CORE, devices)
-        own, other = expert_rows([group[1], there], mine, *weights)
-        return [(group[0], own), (group[0], swap(other, CORE, devices))]
-
-    def tie(*pieces):
-        arrays = lax.optimization_barrier(tuple(array for _, array in pieces))
-        return [(names, array) for (names, _), array in zip(pieces, arrays)]
-
-    start = [0], prepare(hidden_in, routes, scores, experts)
-    za, x, y, zb, xy = [send(link, start) for link in (ZA, X, Y, ZB, X | Y)]
-    near0, zs, ps = combine(
-        [[0, ZA, X, Y], [ZA, ZB], [X | Y, ZB]], [start, za, x, y, zb, xy], rows
-    )
-    got = [send(X, zs), send(Y, zs), send(ZA, ps), send(X | Y, zb)]
-    near0 = sums(near0)
-    near0[0], *got = tie(near0[0], xy, zb, *got)
-    far0, near1, zab, xyb = combine(
-        [
-            [X | Y, X | ZA, Y | ZA, X | Y | ZA],
-            [ZB, ZA | ZB, X | ZB, Y | ZB],
-            [ZA | ZB],
-            [X | Y | ZB],
-        ],
-        got,
+    def sums(pieces, *beside):
+        names = sum((tuple(names) for names, _ in pieces), ())
+        here = [array for _, array in pieces]
+        there = [swap(array, CORE, devices) for array in here]
+        own, other = expert_rows(here + there, mine, *weights)
+        own, other, *arrays = lax.optimization_barrier(
+            (own, other, *(array for _, array in beside))
+        )
+        arrived = [(names, array) for (names, _), array in zip(beside, arrays)]
+        return [(names, own), (names, swap(other, CORE, devices))], *arrived
+
+    start = [0], prepare(hidden_in, routes, scores, experts, [mine])
+    zb, za, x, y, xy = [send(link, start) for link in (ZB, ZA, X, Y, X | Y)]
+    weights, token = fetch((w_gate[0], w_up[0], w_down[0]), start[1])
+    near, zs, ps = combine(
+        [[0, ZA, X, Y, ZB, X | Y], [ZA, ZB], [X | Y, ZB]], [start, za, x, y, zb, xy], rows, [token]
+    )
+
+    near, xs, ys, pz, xyb = sums(
+        [near], send(X, zs), send(Y, zs), send(ZA, ps), send(X | Y, zb)
+    )
+    side, rest, zab = combine(
+        [[X | ZA, X | ZB, Y | ZA, Y | ZB, X | Y | ZA], [ZA | ZB, X | Y | ZB], [ZA | ZB]],
+        [xs, ys, pz, xyb],
         rows,
     )
-    got = [send(X, zab), send(Y, zab), send(ZA, xyb)]
-    far0 = sums(far0)
-    near1 = sums(near1)
-    far0[0], near1[0], *got = tie(far0[0], near1[0], xyb, *got)
-    (far1,) = combine([[X | Y | ZB, X | ZA | ZB, Y | ZA | ZB, X | Y | ZA | ZB]], got, rows)
-    far1 = sums(far1)
-
-    x, y = combine([[X], [Y]], near0, rows)
-    end = [*near0, send(X, x), send(Y, y)]
-    x, y, xya = combine(
-        [[X | ZA, X | ZB], [Y | ZA, Y | ZB], [X | Y | ZA]], [*far0, *near1], rows
-    )
-    x, y, xya = send(X, x), send(Y, y), send(ZA, xya)
-    xa, ya, xyab = combine([[X | ZA | ZB], [Y | ZA | ZB], [X | Y | ZA | ZB]], far1, rows)
-    xa, ya, xyab = send(X, xa), send(Y, ya), send(ZA, xyab)
-    za, xy = combine([[ZA], [X | Y]], [*near0, *far0, x, y, xya], rows)
-    end += [send(ZA, za), send(X | Y, xy)]
-    zab, xyb = combine([[ZA | ZB], [X | Y | ZB]], [*near1, *far1, xa, ya, xyab], rows)
-    (zb,) = combine([[ZB]], [*near1, x, y, send(ZA, zab), send(X | Y, xyb)], rows)
-    return combine([[0]], [*end, send(ZB, zb)], rows)[0][1]
+    side, *got = sums([side], send(X, zab), send(Y, zab), send(ZA, xyb))
+    (far,) = combine([[X | ZA | ZB, Y | ZA | ZB, X | Y | ZA | ZB]], got, rows)
+    x, y, xya = combine([[X | ZA, X | ZB], [Y | ZA, Y | ZB], [X | Y | ZA]], side, rows)
+    far, x, y, xya = sums([rest, far], send(X, x), send(Y, y), send(ZA, xya))
+
+    xa, ya, xyab = combine([[X | ZA | ZB], [Y | ZA | ZB], [X | Y | ZA | ZB]], far, rows)
+    got = send(X, xa), send(Y, ya), send(ZA, xyab)
+    zab, xyb = combine([[ZA | ZB], [X | Y | ZB]], [*far, *got], rows)
+    got = x, y, xya, send(ZA, zab), send(X | Y, xyb)
+    ends = combine([[ZB], [X], [Y], [ZA], [X | Y]], [*near, *got], rows)
+    return combine([[0]], [*near, *(send(piece[0][0], piece) for piece in ends)], rows)[0][1]
 
 
 def dispatch(hidden_in, routes, scores, w_gate, w_up, w_down):

time: 115 us -> 110 us (0.957)
  local copies, waits for them, and re-layouts: 11.6 us -> 2.47 us
  Pallas kernels: 26.4 us -> 31.6 us
  starting transfers between devices: 35.6 us -> 30.4 us
  waiting for transfers between devices: 40.9 us -> 44.6 us
    unnamed x18 -> x4, local copies, waits for them, and re-layouts: 11.6 us -> 2.47 us
    pallas_call x0 -> x1, Pallas kernels: none -> 6.42 us  [fetch(): pl.pallas_call(functools.partial(fetch_body, len(arrays)), out_shape=[plt...]
    ppermute x33 -> x32, starting transfers between devices: 35.6 us -> 30.4 us  [swap(): return lax.ppermute(block, BOTH, [(i, i ^ mask) for i in range(devices)])]
    ppermute x33 -> x32, waiting for transfers between devices: 40.9 us -> 44.6 us  [swap(): return lax.ppermute(block, BOTH, [(i, i ^ mask) for i in range(devices)])]
    pallas_call x15 -> x12, Pallas kernels: 26.4 us -> 25.2 us  [local(): pl.pallas_call(body, out_shape=[jax.ShapeDtypeStruct(shape, jnp.bfloat16)...]
  transfers between devices with their start and end apart: 33 -> 32, of which waited for: 15 -> 17; matrix products, arithmetic and copies ran while one was open for 0% -> 0% of each run, Pallas kernels for 16% -> 27%
where the time goes in v4:
time: 110 us; the launch traced here: 109 us
  waiting for transfers between devices  44.6 us (41%)
  Pallas kernels  31.6 us (29%)
  starting transfers between devices  30.4 us (28%)
  local copies, waits for them, and re-layouts  2.47 us (2%)
    ppermute x32, waiting for transfers between devices, swap(): return lax.ppermute(block, BOTH, [(i, i ^ mask) for i in range(devices)])  44.6 us
    ppermute x32, starting transfers between devices, swap(): return lax.ppermute(block, BOTH, [(i, i ^ mask) for i in range(devices)])  30.4 us
    pallas_call x12, Pallas kernels, local(): pl.pallas_call(body, out_shape=[jax.ShapeDtypeStruct(shape, jnp.bfloat16)...  25.2 us
    pallas_call x1, Pallas kernels, fetch(): pl.pallas_call(functools.partial(fetch_body, len(arrays)), out_shape=[plt...  6.42 us
    unnamed x4, local copies, waits for them, and re-layouts  2.47 us
  transfers between devices with their start and end apart: 32, of which 17 were waited for; matrix products, arithmetic and copies ran while one was open for 0% of the time, Pallas kernels for 27%

profile of v4, /device:TPU:0, one launch (start us, length us, event | category | flops | bytes accessed | tf_op | source)
XLA Modules:
  0.0 109.3 jit_solution(6401763158005921137)
XLA Ops:
  2.7 4.1 %collective-permute-start.3 = (bf16[32,4224]{1,0:T(8,128)(2,1)S(1)}, bf16[32,4224]{1,0:T(8,128)(2,1)S(1)}, u32[]{:S(2)}, u32[]{:S(2)}) collective-permute-start(bf16[32,4224]{1,0:T(8,128)(2,1)S(1)} %shard_map.64.after_ref.refs_0_), channel_id=1, source_target_pairs={{0,8},{1,9},{2,10},{3,11},{4,12},{5,13},{6,14},{7,15},{8,0},{9,1},... | collective-permute-start | bytes 811016 | tf_op jit(solution)/shard_map/ppermute | solution.py:24
  6.8 1.6 %collective-permute-start = (bf16[32,4224]{1,0:T(8,128)(2,1)S(1)}, bf16[32,4224]{1,0:T(8,128)(2,1)S(1)}, u32[]{:S(2)}, u32[]{:S(2)}) collective-permute-start(bf16[32,4224]{1,0:T(8,128)(2,1)S(1)} %shard_map.64.after_ref.refs_0_), channel_id=1, source_target_pairs={{0,4},{1,5},{2,6},{3,7},{4,0},{5,1},{6,2},{7,3},{8,12},{9,13},{10,... | collective-permute-start | bytes 811016 | tf_op jit(solution)/shard_map/ppermute | solution.py:24
  8.4 1.5 %collective-permute-start.1 = (bf16[32,4224]{1,0:T(8,128)(2,1)S(1)}, bf16[32,4224]{1,0:T(8,128)(2,1)S(1)}, u32[]{:S(2)}, u32[]{:S(2)}) collective-permute-start(bf16[32,4224]{1,0:T(8,128)(2,1)S(1)} %shard_map.64.after_ref.refs_0_), channel_id=1, source_target_pairs={{0,2},{1,3},{2,0},{3,1},{4,6},{5,7},{6,4},{7,5},{8,10},{9,11},{10,... | collective-permute-start | bytes 811016 | tf_op jit(solution)/shard_map/ppermute | solution.py:24
  9.9 1.5 %collective-permute-start.2 = (bf16[32,4224]{1,0:T(8,128)(2,1)S(1)}, bf16[32,4224]{1,0:T(8,128)(2,1)S(1)}, u32[]{:S(2)}, u32[]{:S(2)}) collective-permute-start(bf16[32,4224]{1,0:T(8,128)(2,1)S(1)} %shard_map.64.after_ref.refs_0_), channel_id=1, source_target_pairs={{0,16},{1,17},{2,18},{3,19},{4,20},{5,21},{6,22},{7,23},{8,24},{9,... | collective-permute-start | bytes 811016 | tf_op jit(solution)/shard_map/ppermute | solution.py:24
  11.9 6.4 %shard_map.65 = (bf16[4096,768]{1,0:T(8,128)(2,1)S(1)}, bf16[4096,768]{1,0:T(8,128)(2,1)S(1)}, bf16[768,4096]{1,0:T(8,128)(2,1)S(1)}, bf16[16,128]{1,0:T(8,128)(2,1)S(1)}) custom-call(bf16[32,4224]{1,0:T(8,128)(2,1)S(1)} %shard_map.64.after_ref.refs_0_, bf16[4096,768]{1,0:T(8,128)(2,1)} %bitcast.3, bf16[4096,768]{1,0:T(8,128)(2,1)} %bitcast.4, ...), custom_call_target="tpu_custom_call" | custom-call | tf_op jit(solution)/shard_map/pallas_call | solution.py:87
  19.4 3.7 %collective-permute-done.2.refs_3_ = bf16[32,4224]{1,0:T(8,128)(2,1)S(1)} collective-permute-done((bf16[32,4224]{1,0:T(8,128)(2,1)S(1)}, bf16[32,4224]{1,0:T(8,128)(2,1)S(1)}, u32[]{:S(2)}, u32[]{:S(2)}) %collective-permute-start.2) | collective-permute-done | bytes 270368 | tf_op jit(solution)/shard_map/ppermute | solution.py:24
  23.3 1.3 %collective-permute-start.6 = (bf16[64,4224]{1,0:T(8,128)(2,1)S(1)}, bf16[64,4224]{1,0:T(8,128)(2,1)S(1)}, u32[]{:S(2)}, u32[]{:S(2)}) collective-permute-start(bf16[64,4224]{1,0:T(8,128)(2,1)S(1)} %get-tuple-element.57), channel_id=1, source_target_pairs={{0,2},{1,3},{2,0},{3,1},{4,6},{5,7},{6,4},{7,5},{8,10},{9,11},{10,... | collective-permute-start | bytes 1622024 | tf_op jit(solution)/shard_map/ppermute | solution.py:24
  25.9 1.4 %collective-permute-start.9 = (bf16[32,4224]{1,0:T(8,128)(2,1)S(1)}, bf16[32,4224]{1,0:T(8,128)(2,1)S(1)}, u32[]{:S(2)}, u32[]{:S(2)}) collective-permute-start(bf16[32,4224]{1,0:T(8,128)(2,1)S(1)} %collective-permute-done.3.refs_4_), channel_id=1, source_target_pairs={{0,18},{1,19},{2,16},{3,17},{4,22},{5,23},{6,20},{7,21},{8,26},{9,... | collective-permute-start | bytes 811016 | tf_op jit(solution)/shard_map/ppermute | solution.py:24
  27.3 8.4 %shard_map.67 = (bf16[192,4096]{1,0:T(8,128)(2,1)S(1)}, bf16[192,4096]{1,0:T(8,128)(2,1)S(1)}) custom-call(f32[1,128]{1,0:T(1,128)S(1)} %and_convert_fusion._.mine_ref, bf16[192,4224]{1,0:T(8,128)(2,1)S(1)} %get-tuple-element.51.refs_0_, bf16[192,4224]{1,0:T(8,128)(2,1)S(1)} %collective-permute-done.5.refs_1_, ...), custom_call_target="tpu_custom_call" | custom-call | flops 7247757312 | bytes 3145728 | tf_op jit(solution)/shard_map/pallas_call | solution.py:35
  35.7 9.0 %collective-permute-done.9.refs_3_ = bf16[32,4224]{1,0:T(8,128)(2,1)S(1)} collective-permute-done((bf16[32,4224]{1,0:T(8,128)(2,1)S(1)}, bf16[32,4224]{1,0:T(8,128)(2,1)S(1)}, u32[]{:S(2)}, u32[]{:S(2)}) %collective-permute-start.9) | collective-permute-done | bytes 270368 | tf_op jit(solution)/shard_map/ppermute | solution.py:24
  45.9 1.5 %collective-permute-start.13 = (bf16[32,4224]{1,0:T(8,128)(2,1)S(1)}, bf16[32,4224]{1,0:T(8,128)(2,1)S(1)}, u32[]{:S(2)}, u32[]{:S(2)}) collective-permute-start(bf16[32,4224]{1,0:T(8,128)(2,1)S(1)} %get-tuple-element.69), channel_id=1, source_target_pairs={{0,16},{1,17},{2,18},{3,19},{4,20},{5,21},{6,22},{7,23},{8,24},{9,... | collective-permute-start | bytes 811016 | tf_op jit(solution)/shard_map/ppermute | solution.py:24
  48.1 7.0 %shard_map.69 = (bf16[160,4096]{1,0:T(8,128)(2,1)S(1)}, bf16[160,4096]{1,0:T(8,128)(2,1)S(1)}) custom-call(f32[1,128]{1,0:T(1,128)S(1)} %and_convert_fusion._.mine_ref, bf16[160,4224]{1,0:T(8,128)(2,1)S(1)} %get-tuple-element.66.refs_0_, bf16[160,4224]{1,0:T(8,128)(2,1)S(1)} %collective-permute-done.11.refs_1_, ...), custom_call_target="tpu_custom_call" | custom-call | flops 6039797760 | bytes 2621440 | tf_op jit(solution)/shard_map/pallas_call | solution.py:35
  56.4 2.3 %collective-permute-done.17.refs_1_ = bf16[160,4096]{1,0:T(8,128)(2,1)S(1)} collective-permute-done((bf16[160,4096]{1,0:T(8,128)(2,1)S(1)}, bf16[160,4096]{1,0:T(8,128)(2,1)S(1)}, u32[]{:S(2)}, u32[]{:S(2)}) %collective-permute-start.17) | collective-permute-done | bytes 1310752 | tf_op jit(solution)/shard_map/ppermute | solution.py:24
  59.6 1.3 %collective-permute-start.19 = (bf16[64,4096]{1,0:T(8,128)(2,1)S(1)}, bf16[64,4096]{1,0:T(8,128)(2,1)S(1)}, u32[]{:S(2)}, u32[]{:S(2)}) collective-permute-start(bf16[64,4096]{1,0:T(8,128)(2,1)S(1)} %get-tuple-element.78), channel_id=1, source_target_pairs={{0,16},{1,17},{2,18},{3,19},{4,20},{5,21},{6,22},{7,23},{8,24},{9,... | collective-permute-start | bytes 1572872 | tf_op jit(solution)/shard_map/ppermute | solution.py:24
  61.7 7.0 %shard_map.71 = (bf16[160,4096]{1,0:T(8,128)(2,1)S(1)}, bf16[160,4096]{1,0:T(8,128)(2,1)S(1)}) custom-call(f32[1,128]{1,0:T(1,128)S(1)} %and_convert_fusion._.mine_ref, bf16[64,4224]{1,0:T(8,128)(2,1)S(1)} %get-tuple-element.65.refs_0_, bf16[96,4224]{1,0:T(8,128)(2,1)S(1)} %shard_map.70.refs_1_, bf16[64,4224]{1,0:T(8,128)(2,1)S(1)} %collective-permute-done.15.refs_2_, ...), custom_call_target="tpu_custom_call" | custom-call | flops 6039797760 | bytes 2621440 | tf_op jit(solution)/shard_map/pallas_call | solution.py:35
  68.7 4.3 %collective-permute-done.18.refs_2_ = bf16[64,4096]{1,0:T(8,128)(2,1)S(1)} collective-permute-done((bf16[64,4096]{1,0:T(8,128)(2,1)S(1)}, bf16[64,4096]{1,0:T(8,128)(2,1)S(1)}, u32[]{:S(2)}, u32[]{:S(2)}) %collective-permute-start.18) | collective-permute-done | bytes 524320 | tf_op jit(solution)/shard_map/ppermute | solution.py:24
  73.8 2.5 %collective-permute-done.21.refs_1_ = bf16[160,4096]{1,0:T(8,128)(2,1)S(1)} collective-permute-done((bf16[160,4096]{1,0:T(8,128)(2,1)S(1)}, bf16[160,4096]{1,0:T(8,128)(2,1)S(1)}, u32[]{:S(2)}, u32[]{:S(2)}) %collective-permute-start.21) | collective-permute-done | bytes 1310752 | tf_op jit(solution)/shard_map/ppermute | solution.py:24
  76.5 1.6 %collective-permute-start.22 = (bf16[32,4096]{1,0:T(8,128)(2,1)S(1)}, bf16[32,4096]{1,0:T(8,128)(2,1)S(1)}, u32[]{:S(2)}, u32[]{:S(2)}) collective-permute-start(bf16[32,4096]{1,0:T(8,128)(2,1)S(1)} %get-tuple-element.85), channel_id=1, source_target_pairs={{0,2},{1,3},{2,0},{3,1},{4,6},{5,7},{6,4},{7,5},{8,10},{9,11},{10,... | collective-permute-start | bytes 786440 | tf_op jit(solution)/shard_map/ppermute | solution.py:24
  79.4 5.5 %collective-permute-done.22.refs_2_ = bf16[32,4096]{1,0:T(8,128)(2,1)S(1)} collective-permute-done((bf16[32,4096]{1,0:T(8,128)(2,1)S(1)}, bf16[32,4096]{1,0:T(8,128)(2,1)S(1)}, u32[]{:S(2)}, u32[]{:S(2)}) %collective-permute-start.22) | collective-permute-done | bytes 262176 | tf_op jit(solution)/shard_map/ppermute | solution.py:24
  87.5 1.5 %collective-permute-start.26 = (bf16[32,4096]{1,0:T(8,128)(2,1)S(1)}, bf16[32,4096]{1,0:T(8,128)(2,1)S(1)}, u32[]{:S(2)}, u32[]{:S(2)}) collective-permute-start(bf16[32,4096]{1,0:T(8,128)(2,1)S(1)} %get-tuple-element.89), channel_id=1, source_target_pairs={{0,18},{1,19},{2,16},{3,17},{4,22},{5,23},{6,20},{7,21},{8,26},{9,... | collective-permute-start | bytes 786440 | tf_op jit(solution)/shard_map/ppermute | solution.py:24
  89.0 4.6 %collective-permute-done.25.refs_5_ = bf16[32,4096]{1,0:T(8,128)(2,1)S(1)} collective-permute-done((bf16[32,4096]{1,0:T(8,128)(2,1)S(1)}, bf16[32,4096]{1,0:T(8,128)(2,1)S(1)}, u32[]{:S(2)}, u32[]{:S(2)}) %collective-permute-start.25) | collective-permute-done | bytes 262176 | tf_op jit(solution)/shard_map/ppermute | solution.py:24
  93.6 1.5 %collective-permute-done.26.refs_6_ = bf16[32,4096]{1,0:T(8,128)(2,1)S(1)} collective-permute-done((bf16[32,4096]{1,0:T(8,128)(2,1)S(1)}, bf16[32,4096]{1,0:T(8,128)(2,1)S(1)}, u32[]{:S(2)}, u32[]{:S(2)}) %collective-permute-start.26) | collective-permute-done | bytes 262176 | tf_op jit(solution)/shard_map/ppermute | solution.py:24
  99.2 1.5 %collective-permute-start.31 = (bf16[32,4096]{1,0:T(8,128)(2,1)S(1)}, bf16[32,4096]{1,0:T(8,128)(2,1)S(1)}, u32[]{:S(2)}, u32[]{:S(2)}) collective-permute-start(bf16[32,4096]{1,0:T(8,128)(2,1)S(1)} %get-tuple-element.94), channel_id=1, source_target_pairs={{0,18},{1,19},{2,16},{3,17},{4,22},{5,23},{6,20},{7,21},{8,26},{9,... | collective-permute-start | bytes 786440 | tf_op jit(solution)/shard_map/ppermute | solution.py:24
  100.7 7.4 %collective-permute-done.27.refs_2_ = bf16[32,4096]{1,0:T(8,128)(2,1)S(1)} collective-permute-done((bf16[32,4096]{1,0:T(8,128)(2,1)S(1)}, bf16[32,4096]{1,0:T(8,128)(2,1)S(1)}, u32[]{:S(2)}, u32[]{:S(2)}) %collective-permute-start.27) | collective-permute-done | bytes 262176 | tf_op jit(solution)/shard_map/ppermute | solution.py:24
  (58 shorter events, 20.7 us)
Async XLA Ops:
  2.7 16.5 %collective-permute-start.3 = (bf16[32,4224]{1,0:T(8,128)(2,1)S(1)}, bf16[32,4224]{1,0:T(8,128)(2,1)S(1)}, u32[]{:S(2)}, u32[]{:S(2)}) collective-permute-start(bf16[32,4224]{1,0:T(8,128)(2,1)S(1)} %shard_map.64.after_ref.refs_0_), channel_id=1, source_target_pairs={{0,8},{1,9},{2,10},{3,11},{4,12},{5,13},{6,14},{7,15},{8,0},{9,1},... | collective-permute-start | bytes 811016 | tf_op jit(solution)/shard_map/ppermute | solution.py:24
  6.8 12.6 %collective-permute-start = (bf16[32,4224]{1,0:T(8,128)(2,1)S(1)}, bf16[32,4224]{1,0:T(8,128)(2,1)S(1)}, u32[]{:S(2)}, u32[]{:S(2)}) collective-permute-start(bf16[32,4224]{1,0:T(8,128)(2,1)S(1)} %shard_map.64.after_ref.refs_0_), channel_id=1, source_target_pairs={{0,4},{1,5},{2,6},{3,7},{4,0},{5,1},{6,2},{7,3},{8,12},{9,13},{10,... | collective-permute-start | bytes 811016 | tf_op jit(solution)/shard_map/ppermute | solution.py:24
  8.4 11.0 %collective-permute-start.1 = (bf16[32,4224]{1,0:T(8,128)(2,1)S(1)}, bf16[32,4224]{1,0:T(8,128)(2,1)S(1)}, u32[]{:S(2)}, u32[]{:S(2)}) collective-permute-start(bf16[32,4224]{1,0:T(8,128)(2,1)S(1)} %shard_map.64.after_ref.refs_0_), channel_id=1, source_target_pairs={{0,2},{1,3},{2,0},{3,1},{4,6},{5,7},{6,4},{7,5},{8,10},{9,11},{10,... | collective-permute-start | bytes 811016 | tf_op jit(solution)/shard_map/ppermute | solution.py:24
  9.9 13.2 %collective-permute-start.2 = (bf16[32,4224]{1,0:T(8,128)(2,1)S(1)}, bf16[32,4224]{1,0:T(8,128)(2,1)S(1)}, u32[]{:S(2)}, u32[]{:S(2)}) collective-permute-start(bf16[32,4224]{1,0:T(8,128)(2,1)S(1)} %shard_map.64.after_ref.refs_0_), channel_id=1, source_target_pairs={{0,16},{1,17},{2,18},{3,19},{4,20},{5,21},{6,22},{7,23},{8,24},{9,... | collective-permute-start | bytes 811016 | tf_op jit(solution)/shard_map/ppermute | solution.py:24
  11.4 11.7 %collective-permute-start.4 = (bf16[32,4224]{1,0:T(8,128)(2,1)S(1)}, bf16[32,4224]{1,0:T(8,128)(2,1)S(1)}, u32[]{:S(2)}, u32[]{:S(2)}) collective-permute-start(bf16[32,4224]{1,0:T(8,128)(2,1)S(1)} %shard_map.64.after_ref.refs_0_), channel_id=1, source_target_pairs={{0,18},{1,19},{2,16},{3,17},{4,22},{5,23},{6,20},{7,21},{8,26},{9,... | collective-permute-start | bytes 811016 | tf_op jit(solution)/shard_map/ppermute | solution.py:24
  23.3 21.4 %collective-permute-start.6 = (bf16[64,4224]{1,0:T(8,128)(2,1)S(1)}, bf16[64,4224]{1,0:T(8,128)(2,1)S(1)}, u32[]{:S(2)}, u32[]{:S(2)}) collective-permute-start(bf16[64,4224]{1,0:T(8,128)(2,1)S(1)} %get-tuple-element.57), channel_id=1, source_target_pairs={{0,2},{1,3},{2,0},{3,1},{4,6},{5,7},{6,4},{7,5},{8,10},{9,11},{10,... | collective-permute-start | bytes 1622024 | tf_op jit(solution)/shard_map/ppermute | solution.py:24
  24.6 20.1 %collective-permute-start.7 = (bf16[64,4224]{1,0:T(8,128)(2,1)S(1)}, bf16[64,4224]{1,0:T(8,128)(2,1)S(1)}, u32[]{:S(2)}, u32[]{:S(2)}) collective-permute-start(bf16[64,4224]{1,0:T(8,128)(2,1)S(1)} %get-tuple-element.57), channel_id=1, source_target_pairs={{0,16},{1,17},{2,18},{3,19},{4,20},{5,21},{6,22},{7,23},{8,24},{9,... | collective-permute-start | bytes 1622024 | tf_op jit(solution)/shard_map/ppermute | solution.py:24
  25.4 19.3 %collective-permute-start.8 = (bf16[64,4224]{1,0:T(8,128)(2,1)S(1)}, bf16[64,4224]{1,0:T(8,128)(2,1)S(1)}, u32[]{:S(2)}, u32[]{:S(2)}) collective-permute-start(bf16[64,4224]{1,0:T(8,128)(2,1)S(1)} %get-tuple-element.58), channel_id=1, source_target_pairs={{0,4},{1,5},{2,6},{3,7},{4,0},{5,1},{6,2},{7,3},{8,12},{9,13},{10,... | collective-permute-start | bytes 1622024 | tf_op jit(solution)/shard_map/ppermute | solution.py:24
  25.9 18.9 %collective-permute-start.9 = (bf16[32,4224]{1,0:T(8,128)(2,1)S(1)}, bf16[32,4224]{1,0:T(8,128)(2,1)S(1)}, u32[]{:S(2)}, u32[]{:S(2)}) collective-permute-start(bf16[32,4224]{1,0:T(8,128)(2,1)S(1)} %collective-permute-done.3.refs_4_), channel_id=1, source_target_pairs={{0,18},{1,19},{2,16},{3,17},{4,22},{5,23},{6,20},{7,21},{8,26},{9,... | collective-permute-start | bytes 811016 | tf_op jit(solution)/shard_map/ppermute | solution.py:24
  45.0 10.1 %collective-permute-start.12 = (bf16[32,4224]{1,0:T(8,128)(2,1)S(1)}, bf16[32,4224]{1,0:T(8,128)(2,1)S(1)}, u32[]{:S(2)}, u32[]{:S(2)}) collective-permute-start(bf16[32,4224]{1,0:T(8,128)(2,1)S(1)} %get-tuple-element.69), channel_id=1, source_target_pairs={{0,2},{1,3},{2,0},{3,1},{4,6},{5,7},{6,4},{7,5},{8,10},{9,11},{10,... | collective-permute-start | bytes 811016 | tf_op jit(solution)/shard_map/ppermute | solution.py:24
  45.9 9.3 %collective-permute-start.13 = (bf16[32,4224]{1,0:T(8,128)(2,1)S(1)}, bf16[32,4224]{1,0:T(8,128)(2,1)S(1)}, u32[]{:S(2)}, u32[]{:S(2)}) collective-permute-start(bf16[32,4224]{1,0:T(8,128)(2,1)S(1)} %get-tuple-element.69), channel_id=1, source_target_pairs={{0,16},{1,17},{2,18},{3,19},{4,20},{5,21},{6,22},{7,23},{8,24},{9,... | collective-permute-start | bytes 811016 | tf_op jit(solution)/shard_map/ppermute | solution.py:24
  47.4 8.3 %collective-permute-start.14 = (bf16[32,4224]{1,0:T(8,128)(2,1)S(1)}, bf16[32,4224]{1,0:T(8,128)(2,1)S(1)}, u32[]{:S(2)}, u32[]{:S(2)}) collective-permute-start(bf16[32,4224]{1,0:T(8,128)(2,1)S(1)} %collective-permute-done.9.refs_3_), channel_id=1, source_target_pairs={{0,4},{1,5},{2,6},{3,7},{4,0},{5,1},{6,2},{7,3},{8,12},{9,13},{10,... | collective-permute-start | bytes 811016 | tf_op jit(solution)/shard_map/ppermute | solution.py:24
  59.0 14.0 %collective-permute-start.18 = (bf16[64,4096]{1,0:T(8,128)(2,1)S(1)}, bf16[64,4096]{1,0:T(8,128)(2,1)S(1)}, u32[]{:S(2)}, u32[]{:S(2)}) collective-permute-start(bf16[64,4096]{1,0:T(8,128)(2,1)S(1)} %get-tuple-element.77), channel_id=1, source_target_pairs={{0,2},{1,3},{2,0},{3,1},{4,6},{5,7},{6,4},{7,5},{8,10},{9,11},{10,... | collective-permute-start | bytes 1572872 | tf_op jit(solution)/shard_map/ppermute | solution.py:24
  59.6 13.7 %collective-permute-start.19 = (bf16[64,4096]{1,0:T(8,128)(2,1)S(1)}, bf16[64,4096]{1,0:T(8,128)(2,1)S(1)}, u32[]{:S(2)}, u32[]{:S(2)}) collective-permute-start(bf16[64,4096]{1,0:T(8,128)(2,1)S(1)} %get-tuple-element.78), channel_id=1, source_target_pairs={{0,16},{1,17},{2,18},{3,19},{4,20},{5,21},{6,22},{7,23},{8,24},{9,... | collective-permute-start | bytes 1572872 | tf_op jit(solution)/shard_map/ppermute | solution.py:24
  60.9 7.8 %collective-permute-start.20 = (bf16[32,4096]{1,0:T(8,128)(2,1)S(1)}, bf16[32,4096]{1,0:T(8,128)(2,1)S(1)}, u32[]{:S(2)}, u32[]{:S(2)}) collective-permute-start(bf16[32,4096]{1,0:T(8,128)(2,1)S(1)} %get-tuple-element.79), channel_id=1, source_target_pairs={{0,4},{1,5},{2,6},{3,7},{4,0},{5,1},{6,2},{7,3},{8,12},{9,13},{10,... | collective-permute-start | bytes 786440 | tf_op jit(solution)/shard_map/ppermute | solution.py:24
  73.3 15.7 %collective-permute-start.10 = (bf16[192,4096]{1,0:T(8,128)(2,1)S(1)}, bf16[192,4096]{1,0:T(8,128)(2,1)S(1)}, u32[]{:S(2)}, u32[]{:S(2)}) collective-permute-start(bf16[192,4096]{1,0:T(8,128)(2,1)S(1)} %get-tuple-element.60), channel_id=1, source_target_pairs={{0,1},{1,0},{2,3},{3,2},{4,5},{5,4},{6,7},{7,6},{8,9},{9,8},{10,11... | collective-permute-start | bytes 4718600 | tf_op jit(solution)/shard_map/ppermute | solution.py:24
  76.5 8.4 %collective-permute-start.22 = (bf16[32,4096]{1,0:T(8,128)(2,1)S(1)}, bf16[32,4096]{1,0:T(8,128)(2,1)S(1)}, u32[]{:S(2)}, u32[]{:S(2)}) collective-permute-start(bf16[32,4096]{1,0:T(8,128)(2,1)S(1)} %get-tuple-element.85), channel_id=1, source_target_pairs={{0,2},{1,3},{2,0},{3,1},{4,6},{5,7},{6,4},{7,5},{8,10},{9,11},{10,... | collective-permute-start | bytes 786440 | tf_op jit(solution)/shard_map/ppermute | solution.py:24
  78.0 8.1 %collective-permute-start.23 = (bf16[32,4096]{1,0:T(8,128)(2,1)S(1)}, bf16[32,4096]{1,0:T(8,128)(2,1)S(1)}, u32[]{:S(2)}, u32[]{:S(2)}) collective-permute-start(bf16[32,4096]{1,0:T(8,128)(2,1)S(1)} %get-tuple-element.86), channel_id=1, source_target_pairs={{0,16},{1,17},{2,18},{3,19},{4,20},{5,21},{6,22},{7,23},{8,24},{9,... | collective-permute-start | bytes 786440 | tf_op jit(solution)/shard_map/ppermute | solution.py:24
  78.6 7.8 %collective-permute-start.24 = (bf16[32,4096]{1,0:T(8,128)(2,1)S(1)}, bf16[32,4096]{1,0:T(8,128)(2,1)S(1)}, u32[]{:S(2)}, u32[]{:S(2)}) collective-permute-start(bf16[32,4096]{1,0:T(8,128)(2,1)S(1)} %get-tuple-element.87), channel_id=1, source_target_pairs={{0,4},{1,5},{2,6},{3,7},{4,0},{5,1},{6,2},{7,3},{8,12},{9,13},{10,... | collective-permute-start | bytes 786440 | tf_op jit(solution)/shard_map/ppermute | solution.py:24
  95.6 12.5 %collective-permute-start.27 = (bf16[32,4096]{1,0:T(8,128)(2,1)S(1)}, bf16[32,4096]{1,0:T(8,128)(2,1)S(1)}, u32[]{:S(2)}, u32[]{:S(2)}) collective-permute-start(bf16[32,4096]{1,0:T(8,128)(2,1)S(1)} %get-tuple-element.90), channel_id=1, source_target_pairs={{0,8},{1,9},{2,10},{3,11},{4,12},{5,13},{6,14},{7,15},{8,0},{9,1},... | collective-permute-start | bytes 786440 | tf_op jit(solution)/shard_map/ppermute | solution.py:24
  96.0 12.0 %collective-permute-start.28 = (bf16[32,4096]{1,0:T(8,128)(2,1)S(1)}, bf16[32,4096]{1,0:T(8,128)(2,1)S(1)}, u32[]{:S(2)}, u32[]{:S(2)}) collective-permute-start(bf16[32,4096]{1,0:T(8,128)(2,1)S(1)} %get-tuple-element.91), channel_id=1, source_target_pairs={{0,2},{1,3},{2,0},{3,1},{4,6},{5,7},{6,4},{7,5},{8,10},{9,11},{10,... | collective-permute-start | bytes 786440 | tf_op jit(solution)/shard_map/ppermute | solution.py:24
  97.2 10.9 %collective-permute-start.29 = (bf16[32,4096]{1,0:T(8,128)(2,1)S(1)}, bf16[32,4096]{1,0:T(8,128)(2,1)S(1)}, u32[]{:S(2)}, u32[]{:S(2)}) collective-permute-start(bf16[32,4096]{1,0:T(8,128)(2,1)S(1)} %get-tuple-element.92), channel_id=1, source_target_pairs={{0,16},{1,17},{2,18},{3,19},{4,20},{5,21},{6,22},{7,23},{8,24},{9,... | collective-permute-start | bytes 786440 | tf_op jit(solution)/shard_map/ppermute | solution.py:24
  98.0 10.3 %collective-permute-start.30 = (bf16[32,4096]{1,0:T(8,128)(2,1)S(1)}, bf16[32,4096]{1,0:T(8,128)(2,1)S(1)}, u32[]{:S(2)}, u32[]{:S(2)}) collective-permute-start(bf16[32,4096]{1,0:T(8,128)(2,1)S(1)} %get-tuple-element.93), channel_id=1, source_target_pairs={{0,4},{1,5},{2,6},{3,7},{4,0},{5,1},{6,2},{7,3},{8,12},{9,13},{10,... | collective-permute-start | bytes 786440 | tf_op jit(solution)/shard_map/ppermute | solution.py:24
  99.2 9.2 %collective-permute-start.31 = (bf16[32,4096]{1,0:T(8,128)(2,1)S(1)}, bf16[32,4096]{1,0:T(8,128)(2,1)S(1)}, u32[]{:S(2)}, u32[]{:S(2)}) collective-permute-start(bf16[32,4096]{1,0:T(8,128)(2,1)S(1)} %get-tuple-element.94), channel_id=1, source_target_pairs={{0,18},{1,19},{2,16},{3,17},{4,22},{5,23},{6,20},{7,21},{8,26},{9,... | collective-permute-start | bytes 786440 | tf_op jit(solution)/shard_map/ppermute | solution.py:24
  (9 other events, 40.3 us)

commit v5 on v4

--- a/solution.py
+++ b/solution.py
@@ -43,32 +43,47 @@
     )(*operands, *after)
 
 
-def prepare_body(experts, hidden_ref, routes_ref, scores_ref, _, out_ref):
+def prepare_body(experts, *refs):
+    count = 3
+    sources, (_, out_ref), (held, sems) = refs[:count], refs[count : count + 2], (refs[count + 2 : -1], refs[-1])
+    copies = [pltpu.make_async_copy(sources[at], held[at], sems.at[at]) for at in range(count)]
+    for copy in copies:
+        copy.start()
+    for copy in copies:
+        copy.wait()
+    hidden_ref, routes_ref, scores_ref = held
     width = hidden_ref.shape[1]
     out_ref[:, :width] = normalise(hidden_ref[...])
     scores = scores_ref[...]
-    shares = scores / jnp.sum(scores, -1, keepdims=True)
-    lanes = lax.broadcasted_iota(jnp.int32, (hidden_ref.shape[0], 128), 1)
+    shares = scores / jnp.sum(scores, 0, keepdims=True)
+    lanes = lax.broadcasted_iota(jnp.int32, (128, hidden_ref.shape[0]), 0)
     table = jnp.zeros(lanes.shape, jnp.float32)
-    for k in range(routes_ref.shape[1]):
-        named = routes_ref[:, k : k + 1] == lanes % experts
-        table = table + jnp.where(named, shares[:, k : k + 1], 0.0)
+    for k in range(routes_ref.shape[0]):
+        named = routes_ref[k : k + 1, :] == lanes % experts
+        table = table + jnp.where(named, shares[k : k + 1, :], 0.0)
     packed = jnp.zeros(lanes.shape, jnp.float32)
     for at in range(TERMS):
         term = table.astype(jnp.bfloat16).astype(jnp.float32)
         packed = jnp.where(lanes // experts == at, term, packed)
         table = table - term
-    out_ref[:, width:] = packed.astype(jnp.bfloat16)
+    out_ref[:, width:] = packed.T.astype(jnp.bfloat16)
 
 
 def prepare(hidden_in, routes, scores, experts, after):
     rows, width = hidden_in.shape
-    return local(
+    arrays = hidden_in, routes.T, scores.T
+    anywhere = pl.BlockSpec(memory_space=pl.ANY)
+    return pl.pallas_call(
         functools.partial(prepare_body, experts),
-        [(rows, width + 128)],
-        (hidden_in, routes, scores),
-        after=after,
-    )[0]
+        out_shape=jax.ShapeDtypeStruct((rows, width + 128), jnp.bfloat16),
+        in_specs=[anywhere] * 4,
+        out_specs=VMEM,
+        scratch_shapes=[
+            *(pltpu.VMEM(a.shape, a.dtype) for a in arrays),
+            pltpu.SemaphoreType.DMA((len(arrays),)),
+        ],
+        compiler_params=pltpu.CompilerParams(vmem_limit_bytes=4 * 2**20),
+    )(*(pltpu.with_memory_space_constraint(a, pltpu.HBM) for a in arrays), after)
 
 
 def fetch_body(count, after_ref, *refs):
@@ -98,7 +113,7 @@
 
 def expert_body(count, mine_ref, *refs):
     blocks, (gate_ref, up_ref, down_ref) = refs[:count], refs[count : count + 3]
-    *outs, rows_ref, hidden_ref = refs[count + 3 :]
+    own_ref, *other_refs, rows_ref, hidden_ref = refs[count + 3 :]
     width, first = down_ref.shape[1], 0
     shares = []
     for block in blocks:
@@ -113,20 +128,22 @@
         hidden_ref[:, cols] = (gate_part / (1.0 + jnp.exp(-gate_part)) * up_part).astype(jnp.bfloat16)
     half = first // 2
 
-    @pl.loop(0, width // 1024)
-    def _(at):
-        cols = pl.ds(pl.multiple_of(at * 1024, 1024), 1024)
+    for start in range(0, width, 1024):
+        cols = slice(start, start + 1024)
         out = jnp.dot(hidden_ref[...], down_ref[:, cols], preferred_element_type=jnp.float32) * weight
-        outs[0][:, cols] = out[:half].astype(jnp.bfloat16)
-        outs[1][:, cols] = out[half:].astype(jnp.bfloat16)
-
-
-def expert_rows(blocks, mine, w_gate, w_up, w_down):
+        own_ref[:, cols] = out[:half].astype(jnp.bfloat16)
+        at = half
+        for other_ref in other_refs:
+            other_ref[:, cols] = out[at : at + other_ref.shape[0]].astype(jnp.bfloat16)
+            at += other_ref.shape[0]
+
+
+def expert_rows(blocks, mine, w_gate, w_up, w_down, cuts):
     rows = sum(block.shape[0] for block in blocks)
     width, units = w_down.shape[1], w_gate.shape[1]
     return local(
         functools.partial(expert_body, len(blocks)),
-        [(rows // 2, width)] * 2,
+        [(rows // 2, width), *((cut, width) for cut in cuts)],
         (mine, *blocks, w_gate, w_up, w_down),
         [pltpu.VMEM((rows, width), jnp.bfloat16), pltpu.VMEM((rows, units), jnp.bfloat16)],
         flops=6 * rows * width * units,
@@ -175,22 +192,29 @@
         names, array = piece
         return tuple(m ^ link for m in names), swap(array, link, devices)
 
-    def sums(pieces, *beside):
+    def shares(pieces, *cuts):
         names = sum((tuple(names) for names, _ in pieces), ())
         here = [array for _, array in pieces]
         there = [swap(array, CORE, devices) for array in here]
-        own, other = expert_rows(here + there, mine, *weights)
-        own, other, *arrays = lax.optimization_barrier(
-            (own, other, *(array for _, array in beside))
-        )
-        arrived = [(names, array) for (names, _), array in zip(beside, arrays)]
-        return [(names, own), (names, swap(other, CORE, devices))], *arrived
-
-    start = [0], prepare(hidden_in, routes, scores, experts, [mine])
-    zb, za, x, y, xy = [send(link, start) for link in (ZB, ZA, X, Y, X | Y)]
+        cuts = cuts or (len(names),)
+        own, *others = expert_rows(here + there, mine, *weights, [cut * rows for cut in cuts])
+        starts = [sum(cuts[:at]) for at in range(len(cuts))]
+        parts = [tuple(m ^ CORE for m in names[at : at + cut]) for at, cut in zip(starts, cuts)]
+        return [(names, own), *zip(parts, others)]
+
+    def tie(*pieces):
+        arrays = lax.optimization_barrier(tuple(array for _, array in pieces))
+        return [(names, array) for (names, _), array in zip(pieces, arrays)]
+
+    def sums(pieces, *beside):
+        own, other, *beside = tie(*shares(pieces), *beside)
+        return [own, send(CORE, other)], *beside
+
+    start = [0], prepare(hidden_in, routes, scores, experts, mine)
+    zb, x, y, xy, za = [send(link, start) for link in (ZB, X, Y, X | Y, ZA)]
     weights, token = fetch((w_gate[0], w_up[0], w_down[0]), start[1])
     near, zs, ps = combine(
-        [[0, ZA, X, Y, ZB, X | Y], [ZA, ZB], [X | Y, ZB]], [start, za, x, y, zb, xy], rows, [token]
+        [[0, ZA, X, Y, ZB, X | Y], [ZA, ZB], [X | Y, ZB]], [zb, x, y, xy, za, start], rows, [token]
     )
 
     near, xs, ys, pz, xyb = sums(
@@ -204,14 +228,20 @@
     side, *got = sums([side], send(X, zab), send(Y, zab), send(ZA, xyb))
     (far,) = combine([[X | ZA | ZB, Y | ZA | ZB, X | Y | ZA | ZB]], got, rows)
     x, y, xya = combine([[X | ZA, X | ZB], [Y | ZA, Y | ZB], [X | Y | ZA]], side, rows)
-    far, x, y, xya = sums([rest, far], send(X, x), send(Y, y), send(ZA, xya))
-
-    xa, ya, xyab = combine([[X | ZA | ZB], [Y | ZA | ZB], [X | Y | ZA | ZB]], far, rows)
+    own, *others = shares([far, rest], 1, 2, 2)
+    own, x, y, xya = tie(own, send(X, x), send(Y, y), send(ZA, xya))
+    far = [own, *(send(CORE, other) for other in others)]
+    (x,) = combine([[ZA, ZB]], [x, y], rows)
+
+    xa, ya, xyab = combine(
+        [[X | ZA | ZB], [Y | ZA | ZB], [X | Y | ZA | ZB]], far, rows, [x[1]]
+    )
     got = send(X, xa), send(Y, ya), send(ZA, xyab)
     zab, xyb = combine([[ZA | ZB], [X | Y | ZB]], [*far, *got], rows)
-    got = x, y, xya, send(ZA, zab), send(X | Y, xyb)
+    got = x, xya, send(ZA, zab), send(X | Y, xyb)
     ends = combine([[ZB], [X], [Y], [ZA], [X | Y]], [*near, *got], rows)
-    return combine([[0]], [*near, *(send(piece[0][0], piece) for piece in ends)], rows)[0][1]
+    ends = [send(piece[0][0], piece) for piece in ends]
+    return combine([[0]], [*ends, *near], rows)[0][1]
 
 
 def dispatch(hidden_in, routes, scores, w_gate, w_up, w_down):

time: 110 us -> 107 us (0.973)
  starting transfers between devices: 30.4 us -> 33.9 us
  waiting for transfers between devices: 44.6 us -> 41.5 us
  local copies, waits for them, and re-layouts: 2.47 us -> 0 us
    ppermute x32 -> x34, starting transfers between devices: 30.4 us -> 33.9 us  [swap(): return lax.ppermute(block, BOTH, [(i, i ^ mask) for i in range(devices)])]
    ppermute x32 -> x34, waiting for transfers between devices: 44.6 us -> 41.5 us  [swap(): return lax.ppermute(block, BOTH, [(i, i ^ mask) for i in range(devices)])]
    unnamed x4 -> x0, local copies, waits for them, and re-layouts: 2.47 us -> none
    pallas_call x12, Pallas kernels: 25.2 us -> 23.3 us  [local(): pl.pallas_call(body, out_shape=[jax.ShapeDtypeStruct(shape, jnp.bfloat16)...]
    pallas_call x0 -> x1, Pallas kernels: none -> 1.15 us  [prepare(): pl.pallas_call(functools.partial(prepare_body, experts), out_shape=jax.Sh...]
  transfers between devices with their start and end apart: 32 -> 34, of which waited for: 17 -> 18; matrix products, arithmetic and copies ran while one was open for 0% -> 0% of each run, Pallas kernels for 27% -> 26%
where the time goes in v5:
time: 107 us; the launch traced here: 106 us
  waiting for transfers between devices  41.5 us (39%)
  starting transfers between devices  33.9 us (32%)
  Pallas kernels  30.9 us (29%)
    ppermute x34, waiting for transfers between devices, swap(): return lax.ppermute(block, BOTH, [(i, i ^ mask) for i in range(devices)])  41.5 us
    ppermute x34, starting transfers between devices, swap(): return lax.ppermute(block, BOTH, [(i, i ^ mask) for i in range(devices)])  33.9 us
    pallas_call x12, Pallas kernels, local(): pl.pallas_call(body, out_shape=[jax.ShapeDtypeStruct(shape, jnp.bfloat16)...  23.3 us
    pallas_call x1, Pallas kernels, fetch(): pl.pallas_call(functools.partial(fetch_body, len(arrays)), out_shape=[plt...  6.42 us
  transfers between devices with their start and end apart: 34, of which 18 were waited for; matrix products, arithmetic and copies ran while one was open for 0% of the time, Pallas kernels for 26%

profile of v5, /device:TPU:0, one launch (start us, length us, event | category | flops | bytes accessed | tf_op | source)
XLA Modules:
  0.0 106.4 jit_solution(11946216882528487956)
XLA Ops:
  1.2 4.1 %collective-permute-start = (bf16[32,4224]{1,0:T(8,128)(2,1)S(1)}, bf16[32,4224]{1,0:T(8,128)(2,1)S(1)}, u32[]{:S(2)}, u32[]{:S(2)}) collective-permute-start(bf16[32,4224]{1,0:T(8,128)(2,1)S(1)} %shard_map.64.after_ref.refs_5_), channel_id=1, source_target_pairs={{0,8},{1,9},{2,10},{3,11},{4,12},{5,13},{6,14},{7,15},{8,0},{9,1},... | collective-permute-start | bytes 811016 | tf_op jit(solution)/shard_map/ppermute | solution.py:24
  5.3 1.5 %collective-permute-start.1 = (bf16[32,4224]{1,0:T(8,128)(2,1)S(1)}, bf16[32,4224]{1,0:T(8,128)(2,1)S(1)}, u32[]{:S(2)}, u32[]{:S(2)}) collective-permute-start(bf16[32,4224]{1,0:T(8,128)(2,1)S(1)} %shard_map.64.after_ref.refs_5_), channel_id=1, source_target_pairs={{0,2},{1,3},{2,0},{3,1},{4,6},{5,7},{6,4},{7,5},{8,10},{9,11},{10,... | collective-permute-start | bytes 811016 | tf_op jit(solution)/shard_map/ppermute | solution.py:24
  6.8 1.5 %collective-permute-start.2 = (bf16[32,4224]{1,0:T(8,128)(2,1)S(1)}, bf16[32,4224]{1,0:T(8,128)(2,1)S(1)}, u32[]{:S(2)}, u32[]{:S(2)}) collective-permute-start(bf16[32,4224]{1,0:T(8,128)(2,1)S(1)} %shard_map.64.after_ref.refs_5_), channel_id=1, source_target_pairs={{0,16},{1,17},{2,18},{3,19},{4,20},{5,21},{6,22},{7,23},{8,24},{9,... | collective-permute-start | bytes 811016 | tf_op jit(solution)/shard_map/ppermute | solution.py:24
  8.8 1.6 %collective-permute-start.4 = (bf16[32,4224]{1,0:T(8,128)(2,1)S(1)}, bf16[32,4224]{1,0:T(8,128)(2,1)S(1)}, u32[]{:S(2)}, u32[]{:S(2)}) collective-permute-start(bf16[32,4224]{1,0:T(8,128)(2,1)S(1)} %shard_map.64.after_ref.refs_5_), channel_id=1, source_target_pairs={{0,4},{1,5},{2,6},{3,7},{4,0},{5,1},{6,2},{7,3},{8,12},{9,13},{10,... | collective-permute-start | bytes 811016 | tf_op jit(solution)/shard_map/ppermute | solution.py:24
  10.3 6.4 %shard_map.65 = (bf16[4096,768]{1,0:T(8,128)(2,1)S(1)}, bf16[4096,768]{1,0:T(8,128)(2,1)S(1)}, bf16[768,4096]{1,0:T(8,128)(2,1)S(1)}, bf16[16,128]{1,0:T(8,128)(2,1)S(1)}) custom-call(bf16[32,4224]{1,0:T(8,128)(2,1)S(1)} %shard_map.64.after_ref.refs_5_, bf16[4096,768]{1,0:T(8,128)(2,1)} %bitcast.5, bf16[4096,768]{1,0:T(8,128)(2,1)} %bitcast.6, ...), custom_call_target="tpu_custom_call" | custom-call | tf_op jit(solution)/shard_map/pallas_call | solution.py:102
  17.7 2.6 %collective-permute-done.2.refs_2_ = bf16[32,4224]{1,0:T(8,128)(2,1)S(1)} collective-permute-done((bf16[32,4224]{1,0:T(8,128)(2,1)S(1)}, bf16[32,4224]{1,0:T(8,128)(2,1)S(1)}, u32[]{:S(2)}, u32[]{:S(2)}) %collective-permute-start.2) | collective-permute-done | bytes 270368 | tf_op jit(solution)/shard_map/ppermute | solution.py:24
  20.8 1.6 %collective-permute-start.6 = (bf16[64,4224]{1,0:T(8,128)(2,1)S(1)}, bf16[64,4224]{1,0:T(8,128)(2,1)S(1)}, u32[]{:S(2)}, u32[]{:S(2)}) collective-permute-start(bf16[64,4224]{1,0:T(8,128)(2,1)S(1)} %get-tuple-element.58), channel_id=1, source_target_pairs={{0,2},{1,3},{2,0},{3,1},{4,6},{5,7},{6,4},{7,5},{8,10},{9,11},{10,... | collective-permute-start | bytes 1622024 | tf_op jit(solution)/shard_map/ppermute | solution.py:24
  22.4 1.5 %collective-permute-start.7 = (bf16[64,4224]{1,0:T(8,128)(2,1)S(1)}, bf16[64,4224]{1,0:T(8,128)(2,1)S(1)}, u32[]{:S(2)}, u32[]{:S(2)}) collective-permute-start(bf16[64,4224]{1,0:T(8,128)(2,1)S(1)} %get-tuple-element.58), channel_id=1, source_target_pairs={{0,16},{1,17},{2,18},{3,19},{4,20},{5,21},{6,22},{7,23},{8,24},{9,... | collective-permute-start | bytes 1622024 | tf_op jit(solution)/shard_map/ppermute | solution.py:24
  25.6 7.6 %shard_map.67 = (bf16[192,4096]{1,0:T(8,128)(2,1)S(1)}, bf16[192,4096]{1,0:T(8,128)(2,1)S(1)}) custom-call(f32[1,128]{1,0:T(1,128)S(1)} %and_convert_fusion.refs_3_.mine_ref, bf16[192,4224]{1,0:T(8,128)(2,1)S(1)} %get-tuple-element.52.refs_0_, bf16[192,4224]{1,0:T(8,128)(2,1)S(1)} %collective-permute-done.5.refs_1_, ...), custom_call_target="tpu_custom_call" | custom-call | flops 7247757312 | bytes 3145728 | tf_op jit(solution)/shard_map/pallas_call | solution.py:35
  33.3 9.1 %collective-permute-done.9.refs_3_ = bf16[32,4224]{1,0:T(8,128)(2,1)S(1)} collective-permute-done((bf16[32,4224]{1,0:T(8,128)(2,1)S(1)}, bf16[32,4224]{1,0:T(8,128)(2,1)S(1)}, u32[]{:S(2)}, u32[]{:S(2)}) %collective-permute-start.9) | collective-permute-done | bytes 270368 | tf_op jit(solution)/shard_map/ppermute | solution.py:24
  46.1 6.4 %shard_map.69 = (bf16[160,4096]{1,0:T(8,128)(2,1)S(1)}, bf16[160,4096]{1,0:T(8,128)(2,1)S(1)}) custom-call(f32[1,128]{1,0:T(1,128)S(1)} %and_convert_fusion.refs_3_.mine_ref, bf16[160,4224]{1,0:T(8,128)(2,1)S(1)} %get-tuple-element.66.refs_0_, bf16[160,4224]{1,0:T(8,128)(2,1)S(1)} %collective-permute-done.11.refs_1_, ...), custom_call_target="tpu_custom_call" | custom-call | flops 6039797760 | bytes 2621440 | tf_op jit(solution)/shard_map/pallas_call | solution.py:35
  54.3 1.9 %collective-permute-done.17.refs_1_ = bf16[160,4096]{1,0:T(8,128)(2,1)S(1)} collective-permute-done((bf16[160,4096]{1,0:T(8,128)(2,1)S(1)}, bf16[160,4096]{1,0:T(8,128)(2,1)S(1)}, u32[]{:S(2)}, u32[]{:S(2)}) %collective-permute-start.17) | collective-permute-done | bytes 1310752 | tf_op jit(solution)/shard_map/ppermute | solution.py:24
  56.5 1.6 %collective-permute-start.18 = (bf16[64,4096]{1,0:T(8,128)(2,1)S(1)}, bf16[64,4096]{1,0:T(8,128)(2,1)S(1)}, u32[]{:S(2)}, u32[]{:S(2)}) collective-permute-start(bf16[64,4096]{1,0:T(8,128)(2,1)S(1)} %get-tuple-element.77), channel_id=1, source_target_pairs={{0,2},{1,3},{2,0},{3,1},{4,6},{5,7},{6,4},{7,5},{8,10},{9,11},{10,... | collective-permute-start | bytes 1572872 | tf_op jit(solution)/shard_map/ppermute | solution.py:24
  59.6 6.6 %shard_map.71 = (bf16[160,4096]{1,0:T(8,128)(2,1)S(1)}, bf16[32,4096]{1,0:T(8,128)(2,1)S(1)}, bf16[64,4096]{1,0:T(8,128)(2,1)S(1)}, bf16[64,4096]{1,0:T(8,128)(2,1)S(1)}) custom-call(f32[1,128]{1,0:T(1,128)S(1)} %and_convert_fusion.refs_3_.mine_ref, bf16[96,4224]{1,0:T(8,128)(2,1)S(1)} %shard_map.70.refs_0_, bf16[64,4224]{1,0:T(8,128)(2,1)S(1)} %get-tuple-element.73.refs_1_, ...), custom_call_target="tpu_custom_call" | custom-call | flops 6039797760 | bytes 2621440 | tf_op jit(solution)/shard_map/pallas_call | solution.py:35
  66.7 3.7 %collective-permute-done.18.refs_0_ = bf16[64,4096]{1,0:T(8,128)(2,1)S(1)} collective-permute-done((bf16[64,4096]{1,0:T(8,128)(2,1)S(1)}, bf16[64,4096]{1,0:T(8,128)(2,1)S(1)}, u32[]{:S(2)}, u32[]{:S(2)}) %collective-permute-start.18) | collective-permute-done | bytes 524320 | tf_op jit(solution)/shard_map/ppermute | solution.py:24
  72.2 1.6 %collective-permute-start.24 = (bf16[32,4096]{1,0:T(8,128)(2,1)S(1)}, bf16[32,4096]{1,0:T(8,128)(2,1)S(1)}, u32[]{:S(2)}, u32[]{:S(2)}) collective-permute-start(bf16[32,4096]{1,0:T(8,128)(2,1)S(1)} %get-tuple-element.87), channel_id=1, source_target_pairs={{0,2},{1,3},{2,0},{3,1},{4,6},{5,7},{6,4},{7,5},{8,10},{9,11},{10,... | collective-permute-start | bytes 786440 | tf_op jit(solution)/shard_map/ppermute | solution.py:24
  75.3 5.3 %collective-permute-done.24.refs_4_ = bf16[32,4096]{1,0:T(8,128)(2,1)S(1)} collective-permute-done((bf16[32,4096]{1,0:T(8,128)(2,1)S(1)}, bf16[32,4096]{1,0:T(8,128)(2,1)S(1)}, u32[]{:S(2)}, u32[]{:S(2)}) %collective-permute-start.24) | collective-permute-done | bytes 262176 | tf_op jit(solution)/shard_map/ppermute | solution.py:24
  83.4 1.7 %collective-permute-start.28 = (bf16[32,4096]{1,0:T(8,128)(2,1)S(1)}, bf16[32,4096]{1,0:T(8,128)(2,1)S(1)}, u32[]{:S(2)}, u32[]{:S(2)}) collective-permute-start(bf16[32,4096]{1,0:T(8,128)(2,1)S(1)} %get-tuple-element.91), channel_id=1, source_target_pairs={{0,18},{1,19},{2,16},{3,17},{4,22},{5,23},{6,20},{7,21},{8,26},{9,... | collective-permute-start | bytes 786440 | tf_op jit(solution)/shard_map/ppermute | solution.py:24
  85.1 4.2 %collective-permute-done.27.refs_4_ = bf16[32,4096]{1,0:T(8,128)(2,1)S(1)} collective-permute-done((bf16[32,4096]{1,0:T(8,128)(2,1)S(1)}, bf16[32,4096]{1,0:T(8,128)(2,1)S(1)}, u32[]{:S(2)}, u32[]{:S(2)}) %collective-permute-start.27) | collective-permute-done | bytes 262176 | tf_op jit(solution)/shard_map/ppermute | solution.py:24
  89.3 1.5 %collective-permute-done.28.refs_5_ = bf16[32,4096]{1,0:T(8,128)(2,1)S(1)} collective-permute-done((bf16[32,4096]{1,0:T(8,128)(2,1)S(1)}, bf16[32,4096]{1,0:T(8,128)(2,1)S(1)}, u32[]{:S(2)}, u32[]{:S(2)}) %collective-permute-start.28) | collective-permute-done | bytes 262176 | tf_op jit(solution)/shard_map/ppermute | solution.py:24
  91.3 2.1 %collective-permute-start.29 = (bf16[32,4096]{1,0:T(8,128)(2,1)S(1)}, bf16[32,4096]{1,0:T(8,128)(2,1)S(1)}, u32[]{:S(2)}, u32[]{:S(2)}) collective-permute-start(bf16[32,4096]{1,0:T(8,128)(2,1)S(1)} %get-tuple-element.92), channel_id=1, source_target_pairs={{0,8},{1,9},{2,10},{3,11},{4,12},{5,13},{6,14},{7,15},{8,0},{9,1},... | collective-permute-start | bytes 786440 | tf_op jit(solution)/shard_map/ppermute | solution.py:24
  95.8 1.5 %collective-permute-start.33 = (bf16[32,4096]{1,0:T(8,128)(2,1)S(1)}, bf16[32,4096]{1,0:T(8,128)(2,1)S(1)}, u32[]{:S(2)}, u32[]{:S(2)}) collective-permute-start(bf16[32,4096]{1,0:T(8,128)(2,1)S(1)} %get-tuple-element.96), channel_id=1, source_target_pairs={{0,18},{1,19},{2,16},{3,17},{4,22},{5,23},{6,20},{7,21},{8,26},{9,... | collective-permute-start | bytes 786440 | tf_op jit(solution)/shard_map/ppermute | solution.py:24
  97.3 6.4 %collective-permute-done.29.refs_0_ = bf16[32,4096]{1,0:T(8,128)(2,1)S(1)} collective-permute-done((bf16[32,4096]{1,0:T(8,128)(2,1)S(1)}, bf16[32,4096]{1,0:T(8,128)(2,1)S(1)}, u32[]{:S(2)}, u32[]{:S(2)}) %collective-permute-start.29) | collective-permute-done | bytes 262176 | tf_op jit(solution)/shard_map/ppermute | solution.py:24
  103.7 1.7 %collective-permute-done.31.refs_2_ = bf16[32,4096]{1,0:T(8,128)(2,1)S(1)} collective-permute-done((bf16[32,4096]{1,0:T(8,128)(2,1)S(1)}, bf16[32,4096]{1,0:T(8,128)(2,1)S(1)}, u32[]{:S(2)}, u32[]{:S(2)}) %collective-permute-start.31) | collective-permute-done | bytes 262176 | tf_op jit(solution)/shard_map/ppermute | solution.py:24
  (59 shorter events, 22.4 us)
Async XLA Ops:
  1.2 16.5 %collective-permute-start = (bf16[32,4224]{1,0:T(8,128)(2,1)S(1)}, bf16[32,4224]{1,0:T(8,128)(2,1)S(1)}, u32[]{:S(2)}, u32[]{:S(2)}) collective-permute-start(bf16[32,4224]{1,0:T(8,128)(2,1)S(1)} %shard_map.64.after_ref.refs_5_), channel_id=1, source_target_pairs={{0,8},{1,9},{2,10},{3,11},{4,12},{5,13},{6,14},{7,15},{8,0},{9,1},... | collective-permute-start | bytes 811016 | tf_op jit(solution)/shard_map/ppermute | solution.py:24
  5.3 12.4 %collective-permute-start.1 = (bf16[32,4224]{1,0:T(8,128)(2,1)S(1)}, bf16[32,4224]{1,0:T(8,128)(2,1)S(1)}, u32[]{:S(2)}, u32[]{:S(2)}) collective-permute-start(bf16[32,4224]{1,0:T(8,128)(2,1)S(1)} %shard_map.64.after_ref.refs_5_), channel_id=1, source_target_pairs={{0,2},{1,3},{2,0},{3,1},{4,6},{5,7},{6,4},{7,5},{8,10},{9,11},{10,... | collective-permute-start | bytes 811016 | tf_op jit(solution)/shard_map/ppermute | solution.py:24
  6.8 13.5 %collective-permute-start.2 = (bf16[32,4224]{1,0:T(8,128)(2,1)S(1)}, bf16[32,4224]{1,0:T(8,128)(2,1)S(1)}, u32[]{:S(2)}, u32[]{:S(2)}) collective-permute-start(bf16[32,4224]{1,0:T(8,128)(2,1)S(1)} %shard_map.64.after_ref.refs_5_), channel_id=1, source_target_pairs={{0,16},{1,17},{2,18},{3,19},{4,20},{5,21},{6,22},{7,23},{8,24},{9,... | collective-permute-start | bytes 811016 | tf_op jit(solution)/shard_map/ppermute | solution.py:24
  8.3 11.9 %collective-permute-start.3 = (bf16[32,4224]{1,0:T(8,128)(2,1)S(1)}, bf16[32,4224]{1,0:T(8,128)(2,1)S(1)}, u32[]{:S(2)}, u32[]{:S(2)}) collective-permute-start(bf16[32,4224]{1,0:T(8,128)(2,1)S(1)} %shard_map.64.after_ref.refs_5_), channel_id=1, source_target_pairs={{0,18},{1,19},{2,16},{3,17},{4,22},{5,23},{6,20},{7,21},{8,26},{9,... | collective-permute-start | bytes 811016 | tf_op jit(solution)/shard_map/ppermute | solution.py:24
  8.8 11.7 %collective-permute-start.4 = (bf16[32,4224]{1,0:T(8,128)(2,1)S(1)}, bf16[32,4224]{1,0:T(8,128)(2,1)S(1)}, u32[]{:S(2)}, u32[]{:S(2)}) collective-permute-start(bf16[32,4224]{1,0:T(8,128)(2,1)S(1)} %shard_map.64.after_ref.refs_5_), channel_id=1, source_target_pairs={{0,4},{1,5},{2,6},{3,7},{4,0},{5,1},{6,2},{7,3},{8,12},{9,13},{10,... | collective-permute-start | bytes 811016 | tf_op jit(solution)/shard_map/ppermute | solution.py:24
  20.8 21.6 %collective-permute-start.6 = (bf16[64,4224]{1,0:T(8,128)(2,1)S(1)}, bf16[64,4224]{1,0:T(8,128)(2,1)S(1)}, u32[]{:S(2)}, u32[]{:S(2)}) collective-permute-start(bf16[64,4224]{1,0:T(8,128)(2,1)S(1)} %get-tuple-element.58), channel_id=1, source_target_pairs={{0,2},{1,3},{2,0},{3,1},{4,6},{5,7},{6,4},{7,5},{8,10},{9,11},{10,... | collective-permute-start | bytes 1622024 | tf_op jit(solution)/shard_map/ppermute | solution.py:24
  22.4 20.1 %collective-permute-start.7 = (bf16[64,4224]{1,0:T(8,128)(2,1)S(1)}, bf16[64,4224]{1,0:T(8,128)(2,1)S(1)}, u32[]{:S(2)}, u32[]{:S(2)}) collective-permute-start(bf16[64,4224]{1,0:T(8,128)(2,1)S(1)} %get-tuple-element.58), channel_id=1, source_target_pairs={{0,16},{1,17},{2,18},{3,19},{4,20},{5,21},{6,22},{7,23},{8,24},{9,... | collective-permute-start | bytes 1622024 | tf_op jit(solution)/shard_map/ppermute | solution.py:24
  23.9 18.6 %collective-permute-start.8 = (bf16[64,4224]{1,0:T(8,128)(2,1)S(1)}, bf16[64,4224]{1,0:T(8,128)(2,1)S(1)}, u32[]{:S(2)}, u32[]{:S(2)}) collective-permute-start(bf16[64,4224]{1,0:T(8,128)(2,1)S(1)} %get-tuple-element.59), channel_id=1, source_target_pairs={{0,4},{1,5},{2,6},{3,7},{4,0},{5,1},{6,2},{7,3},{8,12},{9,13},{10,... | collective-permute-start | bytes 1622024 | tf_op jit(solution)/shard_map/ppermute | solution.py:24
  24.2 18.2 %collective-permute-start.9 = (bf16[32,4224]{1,0:T(8,128)(2,1)S(1)}, bf16[32,4224]{1,0:T(8,128)(2,1)S(1)}, u32[]{:S(2)}, u32[]{:S(2)}) collective-permute-start(bf16[32,4224]{1,0:T(8,128)(2,1)S(1)} %collective-permute-done.refs_0_), channel_id=1, source_target_pairs={{0,18},{1,19},{2,16},{3,17},{4,22},{5,23},{6,20},{7,21},{8,26},{9,... | collective-permute-start | bytes 811016 | tf_op jit(solution)/shard_map/ppermute | solution.py:24
  42.7 9.8 %collective-permute-start.12 = (bf16[32,4224]{1,0:T(8,128)(2,1)S(1)}, bf16[32,4224]{1,0:T(8,128)(2,1)S(1)}, u32[]{:S(2)}, u32[]{:S(2)}) collective-permute-start(bf16[32,4224]{1,0:T(8,128)(2,1)S(1)} %get-tuple-element.69), channel_id=1, source_target_pairs={{0,2},{1,3},{2,0},{3,1},{4,6},{5,7},{6,4},{7,5},{8,10},{9,11},{10,... | collective-permute-start | bytes 811016 | tf_op jit(solution)/shard_map/ppermute | solution.py:24
  44.0 8.6 %collective-permute-start.13 = (bf16[32,4224]{1,0:T(8,128)(2,1)S(1)}, bf16[32,4224]{1,0:T(8,128)(2,1)S(1)}, u32[]{:S(2)}, u32[]{:S(2)}) collective-permute-start(bf16[32,4224]{1,0:T(8,128)(2,1)S(1)} %get-tuple-element.69), channel_id=1, source_target_pairs={{0,16},{1,17},{2,18},{3,19},{4,20},{5,21},{6,22},{7,23},{8,24},{9,... | collective-permute-start | bytes 811016 | tf_op jit(solution)/shard_map/ppermute | solution.py:24
  44.9 8.3 %collective-permute-start.14 = (bf16[32,4224]{1,0:T(8,128)(2,1)S(1)}, bf16[32,4224]{1,0:T(8,128)(2,1)S(1)}, u32[]{:S(2)}, u32[]{:S(2)}) collective-permute-start(bf16[32,4224]{1,0:T(8,128)(2,1)S(1)} %collective-permute-done.9.refs_3_), channel_id=1, source_target_pairs={{0,4},{1,5},{2,6},{3,7},{4,0},{5,1},{6,2},{7,3},{8,12},{9,13},{10,... | collective-permute-start | bytes 811016 | tf_op jit(solution)/shard_map/ppermute | solution.py:24
  53.8 31.3 %collective-permute-start.10 = (bf16[192,4096]{1,0:T(8,128)(2,1)S(1)}, bf16[192,4096]{1,0:T(8,128)(2,1)S(1)}, u32[]{:S(2)}, u32[]{:S(2)}) collective-permute-start(bf16[192,4096]{1,0:T(8,128)(2,1)S(1)} %get-tuple-element.61), channel_id=1, source_target_pairs={{0,1},{1,0},{2,3},{3,2},{4,5},{5,4},{6,7},{7,6},{8,9},{9,8},{10,11... | collective-permute-start | bytes 4718600 | tf_op jit(solution)/shard_map/ppermute | solution.py:24
  56.5 14.0 %collective-permute-start.18 = (bf16[64,4096]{1,0:T(8,128)(2,1)S(1)}, bf16[64,4096]{1,0:T(8,128)(2,1)S(1)}, u32[]{:S(2)}, u32[]{:S(2)}) collective-permute-start(bf16[64,4096]{1,0:T(8,128)(2,1)S(1)} %get-tuple-element.77), channel_id=1, source_target_pairs={{0,2},{1,3},{2,0},{3,1},{4,6},{5,7},{6,4},{7,5},{8,10},{9,11},{10,... | collective-permute-start | bytes 1572872 | tf_op jit(solution)/shard_map/ppermute | solution.py:24
  58.0 13.7 %collective-permute-start.19 = (bf16[64,4096]{1,0:T(8,128)(2,1)S(1)}, bf16[64,4096]{1,0:T(8,128)(2,1)S(1)}, u32[]{:S(2)}, u32[]{:S(2)}) collective-permute-start(bf16[64,4096]{1,0:T(8,128)(2,1)S(1)} %get-tuple-element.78), channel_id=1, source_target_pairs={{0,16},{1,17},{2,18},{3,19},{4,20},{5,21},{6,22},{7,23},{8,24},{9,... | collective-permute-start | bytes 1572872 | tf_op jit(solution)/shard_map/ppermute | solution.py:24
  58.5 7.9 %collective-permute-start.20 = (bf16[32,4096]{1,0:T(8,128)(2,1)S(1)}, bf16[32,4096]{1,0:T(8,128)(2,1)S(1)}, u32[]{:S(2)}, u32[]{:S(2)}) collective-permute-start(bf16[32,4096]{1,0:T(8,128)(2,1)S(1)} %get-tuple-element.79), channel_id=1, source_target_pairs={{0,4},{1,5},{2,6},{3,7},{4,0},{5,1},{6,2},{7,3},{8,12},{9,13},{10,... | collective-permute-start | bytes 786440 | tf_op jit(solution)/shard_map/ppermute | solution.py:24
  72.2 8.4 %collective-permute-start.24 = (bf16[32,4096]{1,0:T(8,128)(2,1)S(1)}, bf16[32,4096]{1,0:T(8,128)(2,1)S(1)}, u32[]{:S(2)}, u32[]{:S(2)}) collective-permute-start(bf16[32,4096]{1,0:T(8,128)(2,1)S(1)} %get-tuple-element.87), channel_id=1, source_target_pairs={{0,2},{1,3},{2,0},{3,1},{4,6},{5,7},{6,4},{7,5},{8,10},{9,11},{10,... | collective-permute-start | bytes 786440 | tf_op jit(solution)/shard_map/ppermute | solution.py:24
  73.8 8.1 %collective-permute-start.25 = (bf16[32,4096]{1,0:T(8,128)(2,1)S(1)}, bf16[32,4096]{1,0:T(8,128)(2,1)S(1)}, u32[]{:S(2)}, u32[]{:S(2)}) collective-permute-start(bf16[32,4096]{1,0:T(8,128)(2,1)S(1)} %get-tuple-element.88), channel_id=1, source_target_pairs={{0,16},{1,17},{2,18},{3,19},{4,20},{5,21},{6,22},{7,23},{8,24},{9,... | collective-permute-start | bytes 786440 | tf_op jit(solution)/shard_map/ppermute | solution.py:24
  74.3 7.8 %collective-permute-start.26 = (bf16[32,4096]{1,0:T(8,128)(2,1)S(1)}, bf16[32,4096]{1,0:T(8,128)(2,1)S(1)}, u32[]{:S(2)}, u32[]{:S(2)}) collective-permute-start(bf16[32,4096]{1,0:T(8,128)(2,1)S(1)} %get-tuple-element.89), channel_id=1, source_target_pairs={{0,4},{1,5},{2,6},{3,7},{4,0},{5,1},{6,2},{7,3},{8,12},{9,13},{10,... | collective-permute-start | bytes 786440 | tf_op jit(solution)/shard_map/ppermute | solution.py:24
  91.3 12.4 %collective-permute-start.29 = (bf16[32,4096]{1,0:T(8,128)(2,1)S(1)}, bf16[32,4096]{1,0:T(8,128)(2,1)S(1)}, u32[]{:S(2)}, u32[]{:S(2)}) collective-permute-start(bf16[32,4096]{1,0:T(8,128)(2,1)S(1)} %get-tuple-element.92), channel_id=1, source_target_pairs={{0,8},{1,9},{2,10},{3,11},{4,12},{5,13},{6,14},{7,15},{8,0},{9,1},... | collective-permute-start | bytes 786440 | tf_op jit(solution)/shard_map/ppermute | solution.py:24
  93.4 10.3 %collective-permute-start.30 = (bf16[32,4096]{1,0:T(8,128)(2,1)S(1)}, bf16[32,4096]{1,0:T(8,128)(2,1)S(1)}, u32[]{:S(2)}, u32[]{:S(2)}) collective-permute-start(bf16[32,4096]{1,0:T(8,128)(2,1)S(1)} %get-tuple-element.93), channel_id=1, source_target_pairs={{0,2},{1,3},{2,0},{3,1},{4,6},{5,7},{6,4},{7,5},{8,10},{9,11},{10,... | collective-permute-start | bytes 786440 | tf_op jit(solution)/shard_map/ppermute | solution.py:24
  94.6 10.8 %collective-permute-start.31 = (bf16[32,4096]{1,0:T(8,128)(2,1)S(1)}, bf16[32,4096]{1,0:T(8,128)(2,1)S(1)}, u32[]{:S(2)}, u32[]{:S(2)}) collective-permute-start(bf16[32,4096]{1,0:T(8,128)(2,1)S(1)} %get-tuple-element.94), channel_id=1, source_target_pairs={{0,16},{1,17},{2,18},{3,19},{4,20},{5,21},{6,22},{7,23},{8,24},{9,... | collective-permute-start | bytes 786440 | tf_op jit(solution)/shard_map/ppermute | solution.py:24
  95.4 10.0 %collective-permute-start.32 = (bf16[32,4096]{1,0:T(8,128)(2,1)S(1)}, bf16[32,4096]{1,0:T(8,128)(2,1)S(1)}, u32[]{:S(2)}, u32[]{:S(2)}) collective-permute-start(bf16[32,4096]{1,0:T(8,128)(2,1)S(1)} %get-tuple-element.95), channel_id=1, source_target_pairs={{0,4},{1,5},{2,6},{3,7},{4,0},{5,1},{6,2},{7,3},{8,12},{9,13},{10,... | collective-permute-start | bytes 786440 | tf_op jit(solution)/shard_map/ppermute | solution.py:24
  95.8 9.7 %collective-permute-start.33 = (bf16[32,4096]{1,0:T(8,128)(2,1)S(1)}, bf16[32,4096]{1,0:T(8,128)(2,1)S(1)}, u32[]{:S(2)}, u32[]{:S(2)}) collective-permute-start(bf16[32,4096]{1,0:T(8,128)(2,1)S(1)} %get-tuple-element.96), channel_id=1, source_target_pairs={{0,18},{1,19},{2,16},{3,17},{4,22},{5,23},{6,20},{7,21},{8,26},{9,... | collective-permute-start | bytes 786440 | tf_op jit(solution)/shard_map/ppermute | solution.py:24
  (10 other events, 50.1 us)

commit v6 on v5

--- a/solution.py
+++ b/solution.py
@@ -214,7 +214,7 @@
     zb, x, y, xy, za = [send(link, start) for link in (ZB, X, Y, X | Y, ZA)]
     weights, token = fetch((w_gate[0], w_up[0], w_down[0]), start[1])
     near, zs, ps = combine(
-        [[0, ZA, X, Y, ZB, X | Y], [ZA, ZB], [X | Y, ZB]], [zb, x, y, xy, za, start], rows, [token]
+        [[0, ZA, X, Y, ZB, X | Y], [ZA, ZB], [X | Y, ZB]], [start, za, x, y, zb, xy], rows, [token]
     )
 
     near, xs, ys, pz, xyb = sums(
@@ -233,12 +233,14 @@
     far = [own, *(send(CORE, other) for other in others)]
     (x,) = combine([[ZA, ZB]], [x, y], rows)
 
-    xa, ya, xyab = combine(
-        [[X | ZA | ZB], [Y | ZA | ZB], [X | Y | ZA | ZB]], far, rows, [x[1]]
-    )
-    got = send(X, xa), send(Y, ya), send(ZA, xyab)
-    zab, xyb = combine([[ZA | ZB], [X | Y | ZB]], [*far, *got], rows)
-    got = x, xya, send(ZA, zab), send(X | Y, xyb)
+    xyab, xa, ya = combine(
+        [[X | Y | ZA | ZB], [X | ZA | ZB], [Y | ZA | ZB]], far, rows, [x[1]]
+    )
+    xyab, xa, ya = send(ZA, xyab), send(X, xa), send(Y, ya)
+    (xyb,) = combine([[X | Y | ZB]], [*far, xyab], rows)
+    xyb = send(X | Y, xyb)
+    (zab,) = combine([[ZA | ZB]], [*far, xa, ya], rows)
+    got = x, xya, xyb, send(ZA, zab)
     ends = combine([[ZB], [X], [Y], [ZA], [X | Y]], [*near, *got], rows)
     ends = [send(piece[0][0], piece) for piece in ends]
     return combine([[0]], [*ends, *near], rows)[0][1]

time: 107 us -> 105 us (0.981)
  starting transfers between devices: 33.9 us -> 29.4 us
  waiting for transfers between devices: 41.5 us -> 44.7 us
    ppermute x34, starting transfers between devices: 33.9 us -> 29.4 us  [swap(): return lax.ppermute(block, BOTH, [(i, i ^ mask) for i in range(devices)])]
    ppermute x34, waiting for transfers between devices: 41.5 us -> 44.7 us  [swap(): return lax.ppermute(block, BOTH, [(i, i ^ mask) for i in range(devices)])]
    pallas_call x12 -> x13, Pallas kernels: 23.3 us -> 23.3 us  [local(): pl.pallas_call(body, out_shape=[jax.ShapeDtypeStruct(shape, jnp.bfloat16)...]
  transfers between devices with their start and end apart: 34 -> 34, of which waited for: 18 -> 19; matrix products, arithmetic and copies ran while one was open for 0% -> 0% of each run, Pallas kernels for 26% -> 27%
where the time goes in v6:
time: 105 us
  waiting for transfers between devices  44.7 us (43%)
  Pallas kernels  30.9 us (29%)
  starting transfers between devices  29.4 us (28%)
    ppermute x34, waiting for transfers between devices, swap(): return lax.ppermute(block, BOTH, [(i, i ^ mask) for i in range(devices)])  44.7 us
    ppermute x34, starting transfers between devices, swap(): return lax.ppermute(block, BOTH, [(i, i ^ mask) for i in range(devices)])  29.4 us
    pallas_call x13, Pallas kernels, local(): pl.pallas_call(body, out_shape=[jax.ShapeDtypeStruct(shape, jnp.bfloat16)...  23.3 us
    pallas_call x1, Pallas kernels, fetch(): pl.pallas_call(functools.partial(fetch_body, len(arrays)), out_shape=[plt...  6.42 us
  transfers between devices with their start and end apart: 34, of which 19 were waited for; matrix products, arithmetic and copies ran while one was open for 0% of the time, Pallas kernels for 27%

profile of v6, /device:TPU:0, one launch (start us, length us, event | category | flops | bytes accessed | tf_op | source)
XLA Modules:
  0.0 105.2 jit_solution(2212767583004298183)
XLA Ops:
  1.2 4.1 %collective-permute-start.3 = (bf16[32,4224]{1,0:T(8,128)(2,1)S(1)}, bf16[32,4224]{1,0:T(8,128)(2,1)S(1)}, u32[]{:S(2)}, u32[]{:S(2)}) collective-permute-start(bf16[32,4224]{1,0:T(8,128)(2,1)S(1)} %shard_map.64.after_ref.refs_0_), channel_id=1, source_target_pairs={{0,8},{1,9},{2,10},{3,11},{4,12},{5,13},{6,14},{7,15},{8,0},{9,1},... | collective-permute-start | bytes 811016 | tf_op jit(solution)/shard_map/ppermute | solution.py:24
  5.3 1.6 %collective-permute-start = (bf16[32,4224]{1,0:T(8,128)(2,1)S(1)}, bf16[32,4224]{1,0:T(8,128)(2,1)S(1)}, u32[]{:S(2)}, u32[]{:S(2)}) collective-permute-start(bf16[32,4224]{1,0:T(8,128)(2,1)S(1)} %shard_map.64.after_ref.refs_0_), channel_id=1, source_target_pairs={{0,4},{1,5},{2,6},{3,7},{4,0},{5,1},{6,2},{7,3},{8,12},{9,13},{10,... | collective-permute-start | bytes 811016 | tf_op jit(solution)/shard_map/ppermute | solution.py:24
  6.8 1.5 %collective-permute-start.1 = (bf16[32,4224]{1,0:T(8,128)(2,1)S(1)}, bf16[32,4224]{1,0:T(8,128)(2,1)S(1)}, u32[]{:S(2)}, u32[]{:S(2)}) collective-permute-start(bf16[32,4224]{1,0:T(8,128)(2,1)S(1)} %shard_map.64.after_ref.refs_0_), channel_id=1, source_target_pairs={{0,2},{1,3},{2,0},{3,1},{4,6},{5,7},{6,4},{7,5},{8,10},{9,11},{10,... | collective-permute-start | bytes 811016 | tf_op jit(solution)/shard_map/ppermute | solution.py:24
  8.3 1.5 %collective-permute-start.2 = (bf16[32,4224]{1,0:T(8,128)(2,1)S(1)}, bf16[32,4224]{1,0:T(8,128)(2,1)S(1)}, u32[]{:S(2)}, u32[]{:S(2)}) collective-permute-start(bf16[32,4224]{1,0:T(8,128)(2,1)S(1)} %shard_map.64.after_ref.refs_0_), channel_id=1, source_target_pairs={{0,16},{1,17},{2,18},{3,19},{4,20},{5,21},{6,22},{7,23},{8,24},{9,... | collective-permute-start | bytes 811016 | tf_op jit(solution)/shard_map/ppermute | solution.py:24
  10.3 6.4 %shard_map.65 = (bf16[4096,768]{1,0:T(8,128)(2,1)S(1)}, bf16[4096,768]{1,0:T(8,128)(2,1)S(1)}, bf16[768,4096]{1,0:T(8,128)(2,1)S(1)}, bf16[16,128]{1,0:T(8,128)(2,1)S(1)}) custom-call(bf16[32,4224]{1,0:T(8,128)(2,1)S(1)} %shard_map.64.after_ref.refs_0_, bf16[4096,768]{1,0:T(8,128)(2,1)} %bitcast.5, bf16[4096,768]{1,0:T(8,128)(2,1)} %bitcast.6, ...), custom_call_target="tpu_custom_call" | custom-call | tf_op jit(solution)/shard_map/pallas_call | solution.py:102
  17.8 3.7 %collective-permute-done.2.refs_3_ = bf16[32,4224]{1,0:T(8,128)(2,1)S(1)} collective-permute-done((bf16[32,4224]{1,0:T(8,128)(2,1)S(1)}, bf16[32,4224]{1,0:T(8,128)(2,1)S(1)}, u32[]{:S(2)}, u32[]{:S(2)}) %collective-permute-start.2) | collective-permute-done | bytes 270368 | tf_op jit(solution)/shard_map/ppermute | solution.py:24
  21.8 1.3 %collective-permute-start.6 = (bf16[64,4224]{1,0:T(8,128)(2,1)S(1)}, bf16[64,4224]{1,0:T(8,128)(2,1)S(1)}, u32[]{:S(2)}, u32[]{:S(2)}) collective-permute-start(bf16[64,4224]{1,0:T(8,128)(2,1)S(1)} %get-tuple-element.56), channel_id=1, source_target_pairs={{0,2},{1,3},{2,0},{3,1},{4,6},{5,7},{6,4},{7,5},{8,10},{9,11},{10,... | collective-permute-start | bytes 1622024 | tf_op jit(solution)/shard_map/ppermute | solution.py:24
  24.4 1.4 %collective-permute-start.9 = (bf16[32,4224]{1,0:T(8,128)(2,1)S(1)}, bf16[32,4224]{1,0:T(8,128)(2,1)S(1)}, u32[]{:S(2)}, u32[]{:S(2)}) collective-permute-start(bf16[32,4224]{1,0:T(8,128)(2,1)S(1)} %collective-permute-done.3.refs_4_), channel_id=1, source_target_pairs={{0,18},{1,19},{2,16},{3,17},{4,22},{5,23},{6,20},{7,21},{8,26},{9,... | collective-permute-start | bytes 811016 | tf_op jit(solution)/shard_map/ppermute | solution.py:24
  25.8 7.6 %shard_map.67 = (bf16[192,4096]{1,0:T(8,128)(2,1)S(1)}, bf16[192,4096]{1,0:T(8,128)(2,1)S(1)}) custom-call(f32[1,128]{1,0:T(1,128)S(1)} %and_convert_fusion.refs_3_.mine_ref, bf16[192,4224]{1,0:T(8,128)(2,1)S(1)} %get-tuple-element.50.refs_0_, bf16[192,4224]{1,0:T(8,128)(2,1)S(1)} %collective-permute-done.5.refs_1_, ...), custom_call_target="tpu_custom_call" | custom-call | flops 7247757312 | bytes 3145728 | tf_op jit(solution)/shard_map/pallas_call | solution.py:35
  33.4 9.8 %collective-permute-done.9.refs_3_ = bf16[32,4224]{1,0:T(8,128)(2,1)S(1)} collective-permute-done((bf16[32,4224]{1,0:T(8,128)(2,1)S(1)}, bf16[32,4224]{1,0:T(8,128)(2,1)S(1)}, u32[]{:S(2)}, u32[]{:S(2)}) %collective-permute-start.9) | collective-permute-done | bytes 270368 | tf_op jit(solution)/shard_map/ppermute | solution.py:24
  44.3 1.5 %collective-permute-start.13 = (bf16[32,4224]{1,0:T(8,128)(2,1)S(1)}, bf16[32,4224]{1,0:T(8,128)(2,1)S(1)}, u32[]{:S(2)}, u32[]{:S(2)}) collective-permute-start(bf16[32,4224]{1,0:T(8,128)(2,1)S(1)} %get-tuple-element.67), channel_id=1, source_target_pairs={{0,16},{1,17},{2,18},{3,19},{4,20},{5,21},{6,22},{7,23},{8,24},{9,... | collective-permute-start | bytes 811016 | tf_op jit(solution)/shard_map/ppermute | solution.py:24
  46.5 6.4 %shard_map.69 = (bf16[160,4096]{1,0:T(8,128)(2,1)S(1)}, bf16[160,4096]{1,0:T(8,128)(2,1)S(1)}) custom-call(f32[1,128]{1,0:T(1,128)S(1)} %and_convert_fusion.refs_3_.mine_ref, bf16[160,4224]{1,0:T(8,128)(2,1)S(1)} %get-tuple-element.64.refs_0_, bf16[160,4224]{1,0:T(8,128)(2,1)S(1)} %collective-permute-done.11.refs_1_, ...), custom_call_target="tpu_custom_call" | custom-call | flops 6039797760 | bytes 2621440 | tf_op jit(solution)/shard_map/pallas_call | solution.py:35
  55.2 1.9 %collective-permute-done.17.refs_1_ = bf16[160,4096]{1,0:T(8,128)(2,1)S(1)} collective-permute-done((bf16[160,4096]{1,0:T(8,128)(2,1)S(1)}, bf16[160,4096]{1,0:T(8,128)(2,1)S(1)}, u32[]{:S(2)}, u32[]{:S(2)}) %collective-permute-start.17) | collective-permute-done | bytes 1310752 | tf_op jit(solution)/shard_map/ppermute | solution.py:24
  58.0 1.2 %collective-permute-start.19 = (bf16[64,4096]{1,0:T(8,128)(2,1)S(1)}, bf16[64,4096]{1,0:T(8,128)(2,1)S(1)}, u32[]{:S(2)}, u32[]{:S(2)}) collective-permute-start(bf16[64,4096]{1,0:T(8,128)(2,1)S(1)} %get-tuple-element.76), channel_id=1, source_target_pairs={{0,16},{1,17},{2,18},{3,19},{4,20},{5,21},{6,22},{7,23},{8,24},{9,... | collective-permute-start | bytes 1572872 | tf_op jit(solution)/shard_map/ppermute | solution.py:24
  59.7 6.6 %shard_map.71 = (bf16[160,4096]{1,0:T(8,128)(2,1)S(1)}, bf16[32,4096]{1,0:T(8,128)(2,1)S(1)}, bf16[64,4096]{1,0:T(8,128)(2,1)S(1)}, bf16[64,4096]{1,0:T(8,128)(2,1)S(1)}) custom-call(f32[1,128]{1,0:T(1,128)S(1)} %and_convert_fusion.refs_3_.mine_ref, bf16[96,4224]{1,0:T(8,128)(2,1)S(1)} %shard_map.70.refs_0_, bf16[64,4224]{1,0:T(8,128)(2,1)S(1)} %get-tuple-element.71.refs_1_, ...), custom_call_target="tpu_custom_call" | custom-call | flops 6039797760 | bytes 2621440 | tf_op jit(solution)/shard_map/pallas_call | solution.py:35
  67.4 4.0 %collective-permute-done.18.refs_0_ = bf16[64,4096]{1,0:T(8,128)(2,1)S(1)} collective-permute-done((bf16[64,4096]{1,0:T(8,128)(2,1)S(1)}, bf16[64,4096]{1,0:T(8,128)(2,1)S(1)}, u32[]{:S(2)}, u32[]{:S(2)}) %collective-permute-start.18) | collective-permute-done | bytes 524320 | tf_op jit(solution)/shard_map/ppermute | solution.py:24
  73.8 1.2 %collective-permute-start.27 = (bf16[32,4096]{1,0:T(8,128)(2,1)S(1)}, bf16[32,4096]{1,0:T(8,128)(2,1)S(1)}, u32[]{:S(2)}, u32[]{:S(2)}) collective-permute-start(bf16[32,4096]{1,0:T(8,128)(2,1)S(1)} %get-tuple-element.87), channel_id=1, source_target_pairs={{0,16},{1,17},{2,18},{3,19},{4,20},{5,21},{6,22},{7,23},{8,24},{9,... | collective-permute-start | bytes 786440 | tf_op jit(solution)/shard_map/ppermute | solution.py:24
  75.5 6.1 %collective-permute-done.26.refs_4_ = bf16[32,4096]{1,0:T(8,128)(2,1)S(1)} collective-permute-done((bf16[32,4096]{1,0:T(8,128)(2,1)S(1)}, bf16[32,4096]{1,0:T(8,128)(2,1)S(1)}, u32[]{:S(2)}, u32[]{:S(2)}) %collective-permute-start.26) | collective-permute-done | bytes 262176 | tf_op jit(solution)/shard_map/ppermute | solution.py:24
  82.9 1.8 %collective-permute-start.25 = (bf16[32,4096]{1,0:T(8,128)(2,1)S(1)}, bf16[32,4096]{1,0:T(8,128)(2,1)S(1)}, u32[]{:S(2)}, u32[]{:S(2)}) collective-permute-start(bf16[32,4096]{1,0:T(8,128)(2,1)S(1)} %shard_map.75), channel_id=1, source_target_pairs={{0,18},{1,19},{2,16},{3,17},{4,22},{5,23},{6,20},{7,21},{8,26},{9,... | collective-permute-start | bytes 786440 | tf_op jit(solution)/shard_map/ppermute | solution.py:24
  84.7 4.6 %collective-permute-done.28.refs_5_ = bf16[32,4096]{1,0:T(8,128)(2,1)S(1)} collective-permute-done((bf16[32,4096]{1,0:T(8,128)(2,1)S(1)}, bf16[32,4096]{1,0:T(8,128)(2,1)S(1)}, u32[]{:S(2)}, u32[]{:S(2)}) %collective-permute-start.28) | collective-permute-done | bytes 262176 | tf_op jit(solution)/shard_map/ppermute | solution.py:24
  89.3 1.4 %collective-permute-done.25.refs_4_ = bf16[32,4096]{1,0:T(8,128)(2,1)S(1)} collective-permute-done((bf16[32,4096]{1,0:T(8,128)(2,1)S(1)}, bf16[32,4096]{1,0:T(8,128)(2,1)S(1)}, u32[]{:S(2)}, u32[]{:S(2)}) %collective-permute-start.25) | collective-permute-done | bytes 262176 | tf_op jit(solution)/shard_map/ppermute | solution.py:24
  91.7 1.2 %collective-permute-start.30 = (bf16[32,4096]{1,0:T(8,128)(2,1)S(1)}, bf16[32,4096]{1,0:T(8,128)(2,1)S(1)}, u32[]{:S(2)}, u32[]{:S(2)}) collective-permute-start(bf16[32,4096]{1,0:T(8,128)(2,1)S(1)} %get-tuple-element.89), channel_id=1, source_target_pairs={{0,2},{1,3},{2,0},{3,1},{4,6},{5,7},{6,4},{7,5},{8,10},{9,11},{10,... | collective-permute-start | bytes 786440 | tf_op jit(solution)/shard_map/ppermute | solution.py:24
  95.0 1.6 %collective-permute-start.33 = (bf16[32,4096]{1,0:T(8,128)(2,1)S(1)}, bf16[32,4096]{1,0:T(8,128)(2,1)S(1)}, u32[]{:S(2)}, u32[]{:S(2)}) collective-permute-start(bf16[32,4096]{1,0:T(8,128)(2,1)S(1)} %get-tuple-element.92), channel_id=1, source_target_pairs={{0,18},{1,19},{2,16},{3,17},{4,22},{5,23},{6,20},{7,21},{8,26},{9,... | collective-permute-start | bytes 786440 | tf_op jit(solution)/shard_map/ppermute | solution.py:24
  96.5 7.3 %collective-permute-done.29.refs_0_ = bf16[32,4096]{1,0:T(8,128)(2,1)S(1)} collective-permute-done((bf16[32,4096]{1,0:T(8,128)(2,1)S(1)}, bf16[32,4096]{1,0:T(8,128)(2,1)S(1)}, u32[]{:S(2)}, u32[]{:S(2)}) %collective-permute-start.29) | collective-permute-done | bytes 262176 | tf_op jit(solution)/shard_map/ppermute | solution.py:24
  (60 shorter events, 19.1 us)
Async XLA Ops:
  1.2 16.5 %collective-permute-start.3 = (bf16[32,4224]{1,0:T(8,128)(2,1)S(1)}, bf16[32,4224]{1,0:T(8,128)(2,1)S(1)}, u32[]{:S(2)}, u32[]{:S(2)}) collective-permute-start(bf16[32,4224]{1,0:T(8,128)(2,1)S(1)} %shard_map.64.after_ref.refs_0_), channel_id=1, source_target_pairs={{0,8},{1,9},{2,10},{3,11},{4,12},{5,13},{6,14},{7,15},{8,0},{9,1},... | collective-permute-start | bytes 811016 | tf_op jit(solution)/shard_map/ppermute | solution.py:24
  5.3 12.6 %collective-permute-start = (bf16[32,4224]{1,0:T(8,128)(2,1)S(1)}, bf16[32,4224]{1,0:T(8,128)(2,1)S(1)}, u32[]{:S(2)}, u32[]{:S(2)}) collective-permute-start(bf16[32,4224]{1,0:T(8,128)(2,1)S(1)} %shard_map.64.after_ref.refs_0_), channel_id=1, source_target_pairs={{0,4},{1,5},{2,6},{3,7},{4,0},{5,1},{6,2},{7,3},{8,12},{9,13},{10,... | collective-permute-start | bytes 811016 | tf_op jit(solution)/shard_map/ppermute | solution.py:24
  6.8 11.0 %collective-permute-start.1 = (bf16[32,4224]{1,0:T(8,128)(2,1)S(1)}, bf16[32,4224]{1,0:T(8,128)(2,1)S(1)}, u32[]{:S(2)}, u32[]{:S(2)}) collective-permute-start(bf16[32,4224]{1,0:T(8,128)(2,1)S(1)} %shard_map.64.after_ref.refs_0_), channel_id=1, source_target_pairs={{0,2},{1,3},{2,0},{3,1},{4,6},{5,7},{6,4},{7,5},{8,10},{9,11},{10,... | collective-permute-start | bytes 811016 | tf_op jit(solution)/shard_map/ppermute | solution.py:24
  8.3 13.2 %collective-permute-start.2 = (bf16[32,4224]{1,0:T(8,128)(2,1)S(1)}, bf16[32,4224]{1,0:T(8,128)(2,1)S(1)}, u32[]{:S(2)}, u32[]{:S(2)}) collective-permute-start(bf16[32,4224]{1,0:T(8,128)(2,1)S(1)} %shard_map.64.after_ref.refs_0_), channel_id=1, source_target_pairs={{0,16},{1,17},{2,18},{3,19},{4,20},{5,21},{6,22},{7,23},{8,24},{9,... | collective-permute-start | bytes 811016 | tf_op jit(solution)/shard_map/ppermute | solution.py:24
  9.9 11.7 %collective-permute-start.4 = (bf16[32,4224]{1,0:T(8,128)(2,1)S(1)}, bf16[32,4224]{1,0:T(8,128)(2,1)S(1)}, u32[]{:S(2)}, u32[]{:S(2)}) collective-permute-start(bf16[32,4224]{1,0:T(8,128)(2,1)S(1)} %shard_map.64.after_ref.refs_0_), channel_id=1, source_target_pairs={{0,18},{1,19},{2,16},{3,17},{4,22},{5,23},{6,20},{7,21},{8,26},{9,... | collective-permute-start | bytes 811016 | tf_op jit(solution)/shard_map/ppermute | solution.py:24
  21.8 21.4 %collective-permute-start.6 = (bf16[64,4224]{1,0:T(8,128)(2,1)S(1)}, bf16[64,4224]{1,0:T(8,128)(2,1)S(1)}, u32[]{:S(2)}, u32[]{:S(2)}) collective-permute-start(bf16[64,4224]{1,0:T(8,128)(2,1)S(1)} %get-tuple-element.56), channel_id=1, source_target_pairs={{0,2},{1,3},{2,0},{3,1},{4,6},{5,7},{6,4},{7,5},{8,10},{9,11},{10,... | collective-permute-start | bytes 1622024 | tf_op jit(solution)/shard_map/ppermute | solution.py:24
  23.1 20.1 %collective-permute-start.7 = (bf16[64,4224]{1,0:T(8,128)(2,1)S(1)}, bf16[64,4224]{1,0:T(8,128)(2,1)S(1)}, u32[]{:S(2)}, u32[]{:S(2)}) collective-permute-start(bf16[64,4224]{1,0:T(8,128)(2,1)S(1)} %get-tuple-element.56), channel_id=1, source_target_pairs={{0,16},{1,17},{2,18},{3,19},{4,20},{5,21},{6,22},{7,23},{8,24},{9,... | collective-permute-start | bytes 1622024 | tf_op jit(solution)/shard_map/ppermute | solution.py:24
  23.9 19.3 %collective-permute-start.8 = (bf16[64,4224]{1,0:T(8,128)(2,1)S(1)}, bf16[64,4224]{1,0:T(8,128)(2,1)S(1)}, u32[]{:S(2)}, u32[]{:S(2)}) collective-permute-start(bf16[64,4224]{1,0:T(8,128)(2,1)S(1)} %get-tuple-element.57), channel_id=1, source_target_pairs={{0,4},{1,5},{2,6},{3,7},{4,0},{5,1},{6,2},{7,3},{8,12},{9,13},{10,... | collective-permute-start | bytes 1622024 | tf_op jit(solution)/shard_map/ppermute | solution.py:24
  24.4 18.9 %collective-permute-start.9 = (bf16[32,4224]{1,0:T(8,128)(2,1)S(1)}, bf16[32,4224]{1,0:T(8,128)(2,1)S(1)}, u32[]{:S(2)}, u32[]{:S(2)}) collective-permute-start(bf16[32,4224]{1,0:T(8,128)(2,1)S(1)} %collective-permute-done.3.refs_4_), channel_id=1, source_target_pairs={{0,18},{1,19},{2,16},{3,17},{4,22},{5,23},{6,20},{7,21},{8,26},{9,... | collective-permute-start | bytes 811016 | tf_op jit(solution)/shard_map/ppermute | solution.py:24
  43.5 9.5 %collective-permute-start.12 = (bf16[32,4224]{1,0:T(8,128)(2,1)S(1)}, bf16[32,4224]{1,0:T(8,128)(2,1)S(1)}, u32[]{:S(2)}, u32[]{:S(2)}) collective-permute-start(bf16[32,4224]{1,0:T(8,128)(2,1)S(1)} %get-tuple-element.67), channel_id=1, source_target_pairs={{0,2},{1,3},{2,0},{3,1},{4,6},{5,7},{6,4},{7,5},{8,10},{9,11},{10,... | collective-permute-start | bytes 811016 | tf_op jit(solution)/shard_map/ppermute | solution.py:24
  44.3 8.7 %collective-permute-start.13 = (bf16[32,4224]{1,0:T(8,128)(2,1)S(1)}, bf16[32,4224]{1,0:T(8,128)(2,1)S(1)}, u32[]{:S(2)}, u32[]{:S(2)}) collective-permute-start(bf16[32,4224]{1,0:T(8,128)(2,1)S(1)} %get-tuple-element.67), channel_id=1, source_target_pairs={{0,16},{1,17},{2,18},{3,19},{4,20},{5,21},{6,22},{7,23},{8,24},{9,... | collective-permute-start | bytes 811016 | tf_op jit(solution)/shard_map/ppermute | solution.py:24
  45.8 8.3 %collective-permute-start.14 = (bf16[32,4224]{1,0:T(8,128)(2,1)S(1)}, bf16[32,4224]{1,0:T(8,128)(2,1)S(1)}, u32[]{:S(2)}, u32[]{:S(2)}) collective-permute-start(bf16[32,4224]{1,0:T(8,128)(2,1)S(1)} %collective-permute-done.9.refs_3_), channel_id=1, source_target_pairs={{0,4},{1,5},{2,6},{3,7},{4,0},{5,1},{6,2},{7,3},{8,12},{9,13},{10,... | collective-permute-start | bytes 811016 | tf_op jit(solution)/shard_map/ppermute | solution.py:24
  54.8 29.9 %collective-permute-start.10 = (bf16[192,4096]{1,0:T(8,128)(2,1)S(1)}, bf16[192,4096]{1,0:T(8,128)(2,1)S(1)}, u32[]{:S(2)}, u32[]{:S(2)}) collective-permute-start(bf16[192,4096]{1,0:T(8,128)(2,1)S(1)} %get-tuple-element.59), channel_id=1, source_target_pairs={{0,1},{1,0},{2,3},{3,2},{4,5},{5,4},{6,7},{7,6},{8,9},{9,8},{10,11... | collective-permute-start | bytes 4718600 | tf_op jit(solution)/shard_map/ppermute | solution.py:24
  57.4 14.0 %collective-permute-start.18 = (bf16[64,4096]{1,0:T(8,128)(2,1)S(1)}, bf16[64,4096]{1,0:T(8,128)(2,1)S(1)}, u32[]{:S(2)}, u32[]{:S(2)}) collective-permute-start(bf16[64,4096]{1,0:T(8,128)(2,1)S(1)} %get-tuple-element.75), channel_id=1, source_target_pairs={{0,2},{1,3},{2,0},{3,1},{4,6},{5,7},{6,4},{7,5},{8,10},{9,11},{10,... | collective-permute-start | bytes 1572872 | tf_op jit(solution)/shard_map/ppermute | solution.py:24
  58.0 13.7 %collective-permute-start.19 = (bf16[64,4096]{1,0:T(8,128)(2,1)S(1)}, bf16[64,4096]{1,0:T(8,128)(2,1)S(1)}, u32[]{:S(2)}, u32[]{:S(2)}) collective-permute-start(bf16[64,4096]{1,0:T(8,128)(2,1)S(1)} %get-tuple-element.76), channel_id=1, source_target_pairs={{0,16},{1,17},{2,18},{3,19},{4,20},{5,21},{6,22},{7,23},{8,24},{9,... | collective-permute-start | bytes 1572872 | tf_op jit(solution)/shard_map/ppermute | solution.py:24
  59.3 8.2 %collective-permute-start.20 = (bf16[32,4096]{1,0:T(8,128)(2,1)S(1)}, bf16[32,4096]{1,0:T(8,128)(2,1)S(1)}, u32[]{:S(2)}, u32[]{:S(2)}) collective-permute-start(bf16[32,4096]{1,0:T(8,128)(2,1)S(1)} %get-tuple-element.77), channel_id=1, source_target_pairs={{0,4},{1,5},{2,6},{3,7},{4,0},{5,1},{6,2},{7,3},{8,12},{9,13},{10,... | collective-permute-start | bytes 786440 | tf_op jit(solution)/shard_map/ppermute | solution.py:24
  73.2 8.4 %collective-permute-start.26 = (bf16[32,4096]{1,0:T(8,128)(2,1)S(1)}, bf16[32,4096]{1,0:T(8,128)(2,1)S(1)}, u32[]{:S(2)}, u32[]{:S(2)}) collective-permute-start(bf16[32,4096]{1,0:T(8,128)(2,1)S(1)} %get-tuple-element.86), channel_id=1, source_target_pairs={{0,2},{1,3},{2,0},{3,1},{4,6},{5,7},{6,4},{7,5},{8,10},{9,11},{10,... | collective-permute-start | bytes 786440 | tf_op jit(solution)/shard_map/ppermute | solution.py:24
  73.8 8.1 %collective-permute-start.27 = (bf16[32,4096]{1,0:T(8,128)(2,1)S(1)}, bf16[32,4096]{1,0:T(8,128)(2,1)S(1)}, u32[]{:S(2)}, u32[]{:S(2)}) collective-permute-start(bf16[32,4096]{1,0:T(8,128)(2,1)S(1)} %get-tuple-element.87), channel_id=1, source_target_pairs={{0,16},{1,17},{2,18},{3,19},{4,20},{5,21},{6,22},{7,23},{8,24},{9,... | collective-permute-start | bytes 786440 | tf_op jit(solution)/shard_map/ppermute | solution.py:24
  82.9 7.8 %collective-permute-start.25 = (bf16[32,4096]{1,0:T(8,128)(2,1)S(1)}, bf16[32,4096]{1,0:T(8,128)(2,1)S(1)}, u32[]{:S(2)}, u32[]{:S(2)}) collective-permute-start(bf16[32,4096]{1,0:T(8,128)(2,1)S(1)} %shard_map.75), channel_id=1, source_target_pairs={{0,18},{1,19},{2,16},{3,17},{4,22},{5,23},{6,20},{7,21},{8,26},{9,... | collective-permute-start | bytes 786440 | tf_op jit(solution)/shard_map/ppermute | solution.py:24
  91.2 12.6 %collective-permute-start.29 = (bf16[32,4096]{1,0:T(8,128)(2,1)S(1)}, bf16[32,4096]{1,0:T(8,128)(2,1)S(1)}, u32[]{:S(2)}, u32[]{:S(2)}) collective-permute-start(bf16[32,4096]{1,0:T(8,128)(2,1)S(1)} %get-tuple-element.88), channel_id=1, source_target_pairs={{0,8},{1,9},{2,10},{3,11},{4,12},{5,13},{6,14},{7,15},{8,0},{9,1},... | collective-permute-start | bytes 786440 | tf_op jit(solution)/shard_map/ppermute | solution.py:24
  91.7 12.2 %collective-permute-start.30 = (bf16[32,4096]{1,0:T(8,128)(2,1)S(1)}, bf16[32,4096]{1,0:T(8,128)(2,1)S(1)}, u32[]{:S(2)}, u32[]{:S(2)}) collective-permute-start(bf16[32,4096]{1,0:T(8,128)(2,1)S(1)} %get-tuple-element.89), channel_id=1, source_target_pairs={{0,2},{1,3},{2,0},{3,1},{4,6},{5,7},{6,4},{7,5},{8,10},{9,11},{10,... | collective-permute-start | bytes 786440 | tf_op jit(solution)/shard_map/ppermute | solution.py:24
  92.9 11.1 %collective-permute-start.31 = (bf16[32,4096]{1,0:T(8,128)(2,1)S(1)}, bf16[32,4096]{1,0:T(8,128)(2,1)S(1)}, u32[]{:S(2)}, u32[]{:S(2)}) collective-permute-start(bf16[32,4096]{1,0:T(8,128)(2,1)S(1)} %get-tuple-element.90), channel_id=1, source_target_pairs={{0,16},{1,17},{2,18},{3,19},{4,20},{5,21},{6,22},{7,23},{8,24},{9,... | collective-permute-start | bytes 786440 | tf_op jit(solution)/shard_map/ppermute | solution.py:24
  93.9 10.2 %collective-permute-start.32 = (bf16[32,4096]{1,0:T(8,128)(2,1)S(1)}, bf16[32,4096]{1,0:T(8,128)(2,1)S(1)}, u32[]{:S(2)}, u32[]{:S(2)}) collective-permute-start(bf16[32,4096]{1,0:T(8,128)(2,1)S(1)} %get-tuple-element.91), channel_id=1, source_target_pairs={{0,4},{1,5},{2,6},{3,7},{4,0},{5,1},{6,2},{7,3},{8,12},{9,13},{10,... | collective-permute-start | bytes 786440 | tf_op jit(solution)/shard_map/ppermute | solution.py:24
  95.0 9.2 %collective-permute-start.33 = (bf16[32,4096]{1,0:T(8,128)(2,1)S(1)}, bf16[32,4096]{1,0:T(8,128)(2,1)S(1)}, u32[]{:S(2)}, u32[]{:S(2)}) collective-permute-start(bf16[32,4096]{1,0:T(8,128)(2,1)S(1)} %get-tuple-element.92), channel_id=1, source_target_pairs={{0,18},{1,19},{2,16},{3,17},{4,22},{5,23},{6,20},{7,21},{8,26},{9,... | collective-permute-start | bytes 786440 | tf_op jit(solution)/shard_map/ppermute | solution.py:24
  (10 other events, 49.3 us)

commit v7 on v6

--- a/solution.py
+++ b/solution.py
@@ -241,7 +241,8 @@
     xyb = send(X | Y, xyb)
     (zab,) = combine([[ZA | ZB]], [*far, xa, ya], rows)
     got = x, xya, xyb, send(ZA, zab)
-    ends = combine([[ZB], [X], [Y], [ZA], [X | Y]], [*near, *got], rows)
+    ends = combine([[ZB]], [*near, *got], rows)
+    ends += combine([[X], [Y], [ZA], [X | Y]], [*near, *got], rows)
     ends = [send(piece[0][0], piece) for piece in ends]
     return combine([[0]], [*ends, *near], rows)[0][1]
 

time: 105 us -> 109 us (1.038)
  waiting for transfers between devices: 44.7 us -> 48.2 us
    ppermute x34, waiting for transfers between devices: 44.7 us -> 48.2 us  [swap(): return lax.ppermute(block, BOTH, [(i, i ^ mask) for i in range(devices)])]
    pallas_call x13 -> x14, Pallas kernels: 23.3 us -> 23.2 us  [local(): pl.pallas_call(body, out_shape=[jax.ShapeDtypeStruct(shape, jnp.bfloat16)...]
  transfers between devices with their start and end apart: 34 -> 34, of which waited for: 19 -> 19; matrix products, arithmetic and copies ran while one was open for 0% -> 0% of each run, Pallas kernels for 27% -> 26%
where the time goes in v7:
time: 109 us
  waiting for transfers between devices  48.2 us (44%)
  Pallas kernels  30.8 us (28%)
  starting transfers between devices  29.5 us (27%)
    ppermute x34, waiting for transfers between devices, swap(): return lax.ppermute(block, BOTH, [(i, i ^ mask) for i in range(devices)])  48.2 us
    ppermute x34, starting transfers between devices, swap(): return lax.ppermute(block, BOTH, [(i, i ^ mask) for i in range(devices)])  29.5 us
    pallas_call x14, Pallas kernels, local(): pl.pallas_call(body, out_shape=[jax.ShapeDtypeStruct(shape, jnp.bfloat16)...  23.2 us
    pallas_call x1, Pallas kernels, fetch(): pl.pallas_call(functools.partial(fetch_body, len(arrays)), out_shape=[plt...  6.42 us
  transfers between devices with their start and end apart: 34, of which 19 were waited for; matrix products, arithmetic and copies ran while one was open for 0% of the time, Pallas kernels for 26%

profile of v7, /device:TPU:0, one launch (start us, length us, event | category | flops | bytes accessed | tf_op | source)
XLA Modules:
  0.0 108.6 jit_solution(8552506367849353250)
XLA Ops:
  1.2 4.1 %collective-permute-start.3 = (bf16[32,4224]{1,0:T(8,128)(2,1)S(1)}, bf16[32,4224]{1,0:T(8,128)(2,1)S(1)}, u32[]{:S(2)}, u32[]{:S(2)}) collective-permute-start(bf16[32,4224]{1,0:T(8,128)(2,1)S(1)} %shard_map.64.after_ref.refs_0_), channel_id=1, source_target_pairs={{0,8},{1,9},{2,10},{3,11},{4,12},{5,13},{6,14},{7,15},{8,0},{9,1},... | collective-permute-start | bytes 811016 | tf_op jit(solution)/shard_map/ppermute | solution.py:24
  5.3 1.6 %collective-permute-start = (bf16[32,4224]{1,0:T(8,128)(2,1)S(1)}, bf16[32,4224]{1,0:T(8,128)(2,1)S(1)}, u32[]{:S(2)}, u32[]{:S(2)}) collective-permute-start(bf16[32,4224]{1,0:T(8,128)(2,1)S(1)} %shard_map.64.after_ref.refs_0_), channel_id=1, source_target_pairs={{0,4},{1,5},{2,6},{3,7},{4,0},{5,1},{6,2},{7,3},{8,12},{9,13},{10,... | collective-permute-start | bytes 811016 | tf_op jit(solution)/shard_map/ppermute | solution.py:24
  6.8 1.5 %collective-permute-start.1 = (bf16[32,4224]{1,0:T(8,128)(2,1)S(1)}, bf16[32,4224]{1,0:T(8,128)(2,1)S(1)}, u32[]{:S(2)}, u32[]{:S(2)}) collective-permute-start(bf16[32,4224]{1,0:T(8,128)(2,1)S(1)} %shard_map.64.after_ref.refs_0_), channel_id=1, source_target_pairs={{0,2},{1,3},{2,0},{3,1},{4,6},{5,7},{6,4},{7,5},{8,10},{9,11},{10,... | collective-permute-start | bytes 811016 | tf_op jit(solution)/shard_map/ppermute | solution.py:24
  8.3 1.5 %collective-permute-start.2 = (bf16[32,4224]{1,0:T(8,128)(2,1)S(1)}, bf16[32,4224]{1,0:T(8,128)(2,1)S(1)}, u32[]{:S(2)}, u32[]{:S(2)}) collective-permute-start(bf16[32,4224]{1,0:T(8,128)(2,1)S(1)} %shard_map.64.after_ref.refs_0_), channel_id=1, source_target_pairs={{0,16},{1,17},{2,18},{3,19},{4,20},{5,21},{6,22},{7,23},{8,24},{9,... | collective-permute-start | bytes 811016 | tf_op jit(solution)/shard_map/ppermute | solution.py:24
  10.3 6.4 %shard_map.65 = (bf16[4096,768]{1,0:T(8,128)(2,1)S(1)}, bf16[4096,768]{1,0:T(8,128)(2,1)S(1)}, bf16[768,4096]{1,0:T(8,128)(2,1)S(1)}, bf16[16,128]{1,0:T(8,128)(2,1)S(1)}) custom-call(bf16[32,4224]{1,0:T(8,128)(2,1)S(1)} %shard_map.64.after_ref.refs_0_, bf16[4096,768]{1,0:T(8,128)(2,1)} %bitcast.5, bf16[4096,768]{1,0:T(8,128)(2,1)} %bitcast.6, ...), custom_call_target="tpu_custom_call" | custom-call | tf_op jit(solution)/shard_map/pallas_call | solution.py:102
  17.8 3.7 %collective-permute-done.2.refs_3_ = bf16[32,4224]{1,0:T(8,128)(2,1)S(1)} collective-permute-done((bf16[32,4224]{1,0:T(8,128)(2,1)S(1)}, bf16[32,4224]{1,0:T(8,128)(2,1)S(1)}, u32[]{:S(2)}, u32[]{:S(2)}) %collective-permute-start.2) | collective-permute-done | bytes 270368 | tf_op jit(solution)/shard_map/ppermute | solution.py:24
  21.8 1.3 %collective-permute-start.6 = (bf16[64,4224]{1,0:T(8,128)(2,1)S(1)}, bf16[64,4224]{1,0:T(8,128)(2,1)S(1)}, u32[]{:S(2)}, u32[]{:S(2)}) collective-permute-start(bf16[64,4224]{1,0:T(8,128)(2,1)S(1)} %get-tuple-element.55), channel_id=1, source_target_pairs={{0,2},{1,3},{2,0},{3,1},{4,6},{5,7},{6,4},{7,5},{8,10},{9,11},{10,... | collective-permute-start | bytes 1622024 | tf_op jit(solution)/shard_map/ppermute | solution.py:24
  24.4 1.4 %collective-permute-start.9 = (bf16[32,4224]{1,0:T(8,128)(2,1)S(1)}, bf16[32,4224]{1,0:T(8,128)(2,1)S(1)}, u32[]{:S(2)}, u32[]{:S(2)}) collective-permute-start(bf16[32,4224]{1,0:T(8,128)(2,1)S(1)} %collective-permute-done.3.refs_4_), channel_id=1, source_target_pairs={{0,18},{1,19},{2,16},{3,17},{4,22},{5,23},{6,20},{7,21},{8,26},{9,... | collective-permute-start | bytes 811016 | tf_op jit(solution)/shard_map/ppermute | solution.py:24
  25.8 7.5 %shard_map.67 = (bf16[192,4096]{1,0:T(8,128)(2,1)S(1)}, bf16[192,4096]{1,0:T(8,128)(2,1)S(1)}) custom-call(f32[1,128]{1,0:T(1,128)S(1)} %and_convert_fusion.refs_3_.mine_ref, bf16[192,4224]{1,0:T(8,128)(2,1)S(1)} %get-tuple-element.49.refs_0_, bf16[192,4224]{1,0:T(8,128)(2,1)S(1)} %collective-permute-done.5.refs_1_, ...), custom_call_target="tpu_custom_call" | custom-call | flops 7247757312 | bytes 3145728 | tf_op jit(solution)/shard_map/pallas_call | solution.py:35
  33.3 9.9 %collective-permute-done.9.refs_3_ = bf16[32,4224]{1,0:T(8,128)(2,1)S(1)} collective-permute-done((bf16[32,4224]{1,0:T(8,128)(2,1)S(1)}, bf16[32,4224]{1,0:T(8,128)(2,1)S(1)}, u32[]{:S(2)}, u32[]{:S(2)}) %collective-permute-start.9) | collective-permute-done | bytes 270368 | tf_op jit(solution)/shard_map/ppermute | solution.py:24
  44.3 1.5 %collective-permute-start.13 = (bf16[32,4224]{1,0:T(8,128)(2,1)S(1)}, bf16[32,4224]{1,0:T(8,128)(2,1)S(1)}, u32[]{:S(2)}, u32[]{:S(2)}) collective-permute-start(bf16[32,4224]{1,0:T(8,128)(2,1)S(1)} %get-tuple-element.66), channel_id=1, source_target_pairs={{0,16},{1,17},{2,18},{3,19},{4,20},{5,21},{6,22},{7,23},{8,24},{9,... | collective-permute-start | bytes 811016 | tf_op jit(solution)/shard_map/ppermute | solution.py:24
  46.5 6.4 %shard_map.69 = (bf16[160,4096]{1,0:T(8,128)(2,1)S(1)}, bf16[160,4096]{1,0:T(8,128)(2,1)S(1)}) custom-call(f32[1,128]{1,0:T(1,128)S(1)} %and_convert_fusion.refs_3_.mine_ref, bf16[160,4224]{1,0:T(8,128)(2,1)S(1)} %get-tuple-element.63.refs_0_, bf16[160,4224]{1,0:T(8,128)(2,1)S(1)} %collective-permute-done.11.refs_1_, ...), custom_call_target="tpu_custom_call" | custom-call | flops 6039797760 | bytes 2621440 | tf_op jit(solution)/shard_map/pallas_call | solution.py:35
  55.2 1.9 %collective-permute-done.17.refs_1_ = bf16[160,4096]{1,0:T(8,128)(2,1)S(1)} collective-permute-done((bf16[160,4096]{1,0:T(8,128)(2,1)S(1)}, bf16[160,4096]{1,0:T(8,128)(2,1)S(1)}, u32[]{:S(2)}, u32[]{:S(2)}) %collective-permute-start.17) | collective-permute-done | bytes 1310752 | tf_op jit(solution)/shard_map/ppermute | solution.py:24
  59.7 6.6 %shard_map.71 = (bf16[160,4096]{1,0:T(8,128)(2,1)S(1)}, bf16[32,4096]{1,0:T(8,128)(2,1)S(1)}, bf16[64,4096]{1,0:T(8,128)(2,1)S(1)}, bf16[64,4096]{1,0:T(8,128)(2,1)S(1)}) custom-call(f32[1,128]{1,0:T(1,128)S(1)} %and_convert_fusion.refs_3_.mine_ref, bf16[96,4224]{1,0:T(8,128)(2,1)S(1)} %shard_map.70.refs_0_, bf16[64,4224]{1,0:T(8,128)(2,1)S(1)} %get-tuple-element.70.refs_1_, ...), custom_call_target="tpu_custom_call" | custom-call | flops 6039797760 | bytes 2621440 | tf_op jit(solution)/shard_map/pallas_call | solution.py:35
  67.4 4.0 %collective-permute-done.18.refs_0_ = bf16[64,4096]{1,0:T(8,128)(2,1)S(1)} collective-permute-done((bf16[64,4096]{1,0:T(8,128)(2,1)S(1)}, bf16[64,4096]{1,0:T(8,128)(2,1)S(1)}, u32[]{:S(2)}, u32[]{:S(2)}) %collective-permute-start.18) | collective-permute-done | bytes 524320 | tf_op jit(solution)/shard_map/ppermute | solution.py:24
  75.5 6.1 %collective-permute-done.26.refs_4_ = bf16[32,4096]{1,0:T(8,128)(2,1)S(1)} collective-permute-done((bf16[32,4096]{1,0:T(8,128)(2,1)S(1)}, bf16[32,4096]{1,0:T(8,128)(2,1)S(1)}, u32[]{:S(2)}, u32[]{:S(2)}) %collective-permute-start.26) | collective-permute-done | bytes 262176 | tf_op jit(solution)/shard_map/ppermute | solution.py:24
  82.9 1.8 %collective-permute-start.25 = (bf16[32,4096]{1,0:T(8,128)(2,1)S(1)}, bf16[32,4096]{1,0:T(8,128)(2,1)S(1)}, u32[]{:S(2)}, u32[]{:S(2)}) collective-permute-start(bf16[32,4096]{1,0:T(8,128)(2,1)S(1)} %shard_map.75), channel_id=1, source_target_pairs={{0,18},{1,19},{2,16},{3,17},{4,22},{5,23},{6,20},{7,21},{8,26},{9,... | collective-permute-start | bytes 786440 | tf_op jit(solution)/shard_map/ppermute | solution.py:24
  84.7 4.6 %collective-permute-done.28.refs_5_ = bf16[32,4096]{1,0:T(8,128)(2,1)S(1)} collective-permute-done((bf16[32,4096]{1,0:T(8,128)(2,1)S(1)}, bf16[32,4096]{1,0:T(8,128)(2,1)S(1)}, u32[]{:S(2)}, u32[]{:S(2)}) %collective-permute-start.28) | collective-permute-done | bytes 262176 | tf_op jit(solution)/shard_map/ppermute | solution.py:24
  89.3 1.4 %collective-permute-done.25.refs_4_ = bf16[32,4096]{1,0:T(8,128)(2,1)S(1)} collective-permute-done((bf16[32,4096]{1,0:T(8,128)(2,1)S(1)}, bf16[32,4096]{1,0:T(8,128)(2,1)S(1)}, u32[]{:S(2)}, u32[]{:S(2)}) %collective-permute-start.25) | collective-permute-done | bytes 262176 | tf_op jit(solution)/shard_map/ppermute | solution.py:24
  91.1 1.3 %collective-permute-start.30 = (bf16[32,4096]{1,0:T(8,128)(2,1)S(1)}, bf16[32,4096]{1,0:T(8,128)(2,1)S(1)}, u32[]{:S(2)}, u32[]{:S(2)}) collective-permute-start(bf16[32,4096]{1,0:T(8,128)(2,1)S(1)} %get-tuple-element.87), channel_id=1, source_target_pairs={{0,2},{1,3},{2,0},{3,1},{4,6},{5,7},{6,4},{7,5},{8,10},{9,11},{10,... | collective-permute-start | bytes 786440 | tf_op jit(solution)/shard_map/ppermute | solution.py:24
  94.5 1.6 %collective-permute-start.33 = (bf16[32,4096]{1,0:T(8,128)(2,1)S(1)}, bf16[32,4096]{1,0:T(8,128)(2,1)S(1)}, u32[]{:S(2)}, u32[]{:S(2)}) collective-permute-start(bf16[32,4096]{1,0:T(8,128)(2,1)S(1)} %get-tuple-element.90), channel_id=1, source_target_pairs={{0,18},{1,19},{2,16},{3,17},{4,22},{5,23},{6,20},{7,21},{8,26},{9,... | collective-permute-start | bytes 786440 | tf_op jit(solution)/shard_map/ppermute | solution.py:24
  96.6 3.4 %collective-permute-done.30.refs_1_ = bf16[32,4096]{1,0:T(8,128)(2,1)S(1)} collective-permute-done((bf16[32,4096]{1,0:T(8,128)(2,1)S(1)}, bf16[32,4096]{1,0:T(8,128)(2,1)S(1)}, u32[]{:S(2)}, u32[]{:S(2)}) %collective-permute-start.30) | collective-permute-done | bytes 262176 | tf_op jit(solution)/shard_map/ppermute | solution.py:24
  100.0 3.7 %collective-permute-done.31.refs_2_ = bf16[32,4096]{1,0:T(8,128)(2,1)S(1)} collective-permute-done((bf16[32,4096]{1,0:T(8,128)(2,1)S(1)}, bf16[32,4096]{1,0:T(8,128)(2,1)S(1)}, u32[]{:S(2)}, u32[]{:S(2)}) %collective-permute-start.31) | collective-permute-done | bytes 262176 | tf_op jit(solution)/shard_map/ppermute | solution.py:24
  103.7 3.9 %collective-permute-done.29.refs_0_ = bf16[32,4096]{1,0:T(8,128)(2,1)S(1)} collective-permute-done((bf16[32,4096]{1,0:T(8,128)(2,1)S(1)}, bf16[32,4096]{1,0:T(8,128)(2,1)S(1)}, u32[]{:S(2)}, u32[]{:S(2)}) %collective-permute-start.29) | collective-permute-done | bytes 262176 | tf_op jit(solution)/shard_map/ppermute | solution.py:24
  (61 shorter events, 21.2 us)
Async XLA Ops:
  1.2 16.5 %collective-permute-start.3 = (bf16[32,4224]{1,0:T(8,128)(2,1)S(1)}, bf16[32,4224]{1,0:T(8,128)(2,1)S(1)}, u32[]{:S(2)}, u32[]{:S(2)}) collective-permute-start(bf16[32,4224]{1,0:T(8,128)(2,1)S(1)} %shard_map.64.after_ref.refs_0_), channel_id=1, source_target_pairs={{0,8},{1,9},{2,10},{3,11},{4,12},{5,13},{6,14},{7,15},{8,0},{9,1},... | collective-permute-start | bytes 811016 | tf_op jit(solution)/shard_map/ppermute | solution.py:24
  5.3 12.6 %collective-permute-start = (bf16[32,4224]{1,0:T(8,128)(2,1)S(1)}, bf16[32,4224]{1,0:T(8,128)(2,1)S(1)}, u32[]{:S(2)}, u32[]{:S(2)}) collective-permute-start(bf16[32,4224]{1,0:T(8,128)(2,1)S(1)} %shard_map.64.after_ref.refs_0_), channel_id=1, source_target_pairs={{0,4},{1,5},{2,6},{3,7},{4,0},{5,1},{6,2},{7,3},{8,12},{9,13},{10,... | collective-permute-start | bytes 811016 | tf_op jit(solution)/shard_map/ppermute | solution.py:24
  6.8 11.0 %collective-permute-start.1 = (bf16[32,4224]{1,0:T(8,128)(2,1)S(1)}, bf16[32,4224]{1,0:T(8,128)(2,1)S(1)}, u32[]{:S(2)}, u32[]{:S(2)}) collective-permute-start(bf16[32,4224]{1,0:T(8,128)(2,1)S(1)} %shard_map.64.after_ref.refs_0_), channel_id=1, source_target_pairs={{0,2},{1,3},{2,0},{3,1},{4,6},{5,7},{6,4},{7,5},{8,10},{9,11},{10,... | collective-permute-start | bytes 811016 | tf_op jit(solution)/shard_map/ppermute | solution.py:24
  8.3 13.2 %collective-permute-start.2 = (bf16[32,4224]{1,0:T(8,128)(2,1)S(1)}, bf16[32,4224]{1,0:T(8,128)(2,1)S(1)}, u32[]{:S(2)}, u32[]{:S(2)}) collective-permute-start(bf16[32,4224]{1,0:T(8,128)(2,1)S(1)} %shard_map.64.after_ref.refs_0_), channel_id=1, source_target_pairs={{0,16},{1,17},{2,18},{3,19},{4,20},{5,21},{6,22},{7,23},{8,24},{9,... | collective-permute-start | bytes 811016 | tf_op jit(solution)/shard_map/ppermute | solution.py:24
  9.9 11.7 %collective-permute-start.4 = (bf16[32,4224]{1,0:T(8,128)(2,1)S(1)}, bf16[32,4224]{1,0:T(8,128)(2,1)S(1)}, u32[]{:S(2)}, u32[]{:S(2)}) collective-permute-start(bf16[32,4224]{1,0:T(8,128)(2,1)S(1)} %shard_map.64.after_ref.refs_0_), channel_id=1, source_target_pairs={{0,18},{1,19},{2,16},{3,17},{4,22},{5,23},{6,20},{7,21},{8,26},{9,... | collective-permute-start | bytes 811016 | tf_op jit(solution)/shard_map/ppermute | solution.py:24
  21.8 21.4 %collective-permute-start.6 = (bf16[64,4224]{1,0:T(8,128)(2,1)S(1)}, bf16[64,4224]{1,0:T(8,128)(2,1)S(1)}, u32[]{:S(2)}, u32[]{:S(2)}) collective-permute-start(bf16[64,4224]{1,0:T(8,128)(2,1)S(1)} %get-tuple-element.55), channel_id=1, source_target_pairs={{0,2},{1,3},{2,0},{3,1},{4,6},{5,7},{6,4},{7,5},{8,10},{9,11},{10,... | collective-permute-start | bytes 1622024 | tf_op jit(solution)/shard_map/ppermute | solution.py:24
  23.1 20.1 %collective-permute-start.7 = (bf16[64,4224]{1,0:T(8,128)(2,1)S(1)}, bf16[64,4224]{1,0:T(8,128)(2,1)S(1)}, u32[]{:S(2)}, u32[]{:S(2)}) collective-permute-start(bf16[64,4224]{1,0:T(8,128)(2,1)S(1)} %get-tuple-element.55), channel_id=1, source_target_pairs={{0,16},{1,17},{2,18},{3,19},{4,20},{5,21},{6,22},{7,23},{8,24},{9,... | collective-permute-start | bytes 1622024 | tf_op jit(solution)/shard_map/ppermute | solution.py:24
  23.9 19.3 %collective-permute-start.8 = (bf16[64,4224]{1,0:T(8,128)(2,1)S(1)}, bf16[64,4224]{1,0:T(8,128)(2,1)S(1)}, u32[]{:S(2)}, u32[]{:S(2)}) collective-permute-start(bf16[64,4224]{1,0:T(8,128)(2,1)S(1)} %get-tuple-element.56), channel_id=1, source_target_pairs={{0,4},{1,5},{2,6},{3,7},{4,0},{5,1},{6,2},{7,3},{8,12},{9,13},{10,... | collective-permute-start | bytes 1622024 | tf_op jit(solution)/shard_map/ppermute | solution.py:24
  24.4 18.9 %collective-permute-start.9 = (bf16[32,4224]{1,0:T(8,128)(2,1)S(1)}, bf16[32,4224]{1,0:T(8,128)(2,1)S(1)}, u32[]{:S(2)}, u32[]{:S(2)}) collective-permute-start(bf16[32,4224]{1,0:T(8,128)(2,1)S(1)} %collective-permute-done.3.refs_4_), channel_id=1, source_target_pairs={{0,18},{1,19},{2,16},{3,17},{4,22},{5,23},{6,20},{7,21},{8,26},{9,... | collective-permute-start | bytes 811016 | tf_op jit(solution)/shard_map/ppermute | solution.py:24
  43.5 9.5 %collective-permute-start.12 = (bf16[32,4224]{1,0:T(8,128)(2,1)S(1)}, bf16[32,4224]{1,0:T(8,128)(2,1)S(1)}, u32[]{:S(2)}, u32[]{:S(2)}) collective-permute-start(bf16[32,4224]{1,0:T(8,128)(2,1)S(1)} %get-tuple-element.66), channel_id=1, source_target_pairs={{0,2},{1,3},{2,0},{3,1},{4,6},{5,7},{6,4},{7,5},{8,10},{9,11},{10,... | collective-permute-start | bytes 811016 | tf_op jit(solution)/shard_map/ppermute | solution.py:24
  44.3 8.6 %collective-permute-start.13 = (bf16[32,4224]{1,0:T(8,128)(2,1)S(1)}, bf16[32,4224]{1,0:T(8,128)(2,1)S(1)}, u32[]{:S(2)}, u32[]{:S(2)}) collective-permute-start(bf16[32,4224]{1,0:T(8,128)(2,1)S(1)} %get-tuple-element.66), channel_id=1, source_target_pairs={{0,16},{1,17},{2,18},{3,19},{4,20},{5,21},{6,22},{7,23},{8,24},{9,... | collective-permute-start | bytes 811016 | tf_op jit(solution)/shard_map/ppermute | solution.py:24
  45.8 8.3 %collective-permute-start.14 = (bf16[32,4224]{1,0:T(8,128)(2,1)S(1)}, bf16[32,4224]{1,0:T(8,128)(2,1)S(1)}, u32[]{:S(2)}, u32[]{:S(2)}) collective-permute-start(bf16[32,4224]{1,0:T(8,128)(2,1)S(1)} %collective-permute-done.9.refs_3_), channel_id=1, source_target_pairs={{0,4},{1,5},{2,6},{3,7},{4,0},{5,1},{6,2},{7,3},{8,12},{9,13},{10,... | collective-permute-start | bytes 811016 | tf_op jit(solution)/shard_map/ppermute | solution.py:24
  54.8 29.9 %collective-permute-start.10 = (bf16[192,4096]{1,0:T(8,128)(2,1)S(1)}, bf16[192,4096]{1,0:T(8,128)(2,1)S(1)}, u32[]{:S(2)}, u32[]{:S(2)}) collective-permute-start(bf16[192,4096]{1,0:T(8,128)(2,1)S(1)} %get-tuple-element.58), channel_id=1, source_target_pairs={{0,1},{1,0},{2,3},{3,2},{4,5},{5,4},{6,7},{7,6},{8,9},{9,8},{10,11... | collective-permute-start | bytes 4718600 | tf_op jit(solution)/shard_map/ppermute | solution.py:24
  57.4 14.0 %collective-permute-start.18 = (bf16[64,4096]{1,0:T(8,128)(2,1)S(1)}, bf16[64,4096]{1,0:T(8,128)(2,1)S(1)}, u32[]{:S(2)}, u32[]{:S(2)}) collective-permute-start(bf16[64,4096]{1,0:T(8,128)(2,1)S(1)} %get-tuple-element.74), channel_id=1, source_target_pairs={{0,2},{1,3},{2,0},{3,1},{4,6},{5,7},{6,4},{7,5},{8,10},{9,11},{10,... | collective-permute-start | bytes 1572872 | tf_op jit(solution)/shard_map/ppermute | solution.py:24
  58.0 13.7 %collective-permute-start.19 = (bf16[64,4096]{1,0:T(8,128)(2,1)S(1)}, bf16[64,4096]{1,0:T(8,128)(2,1)S(1)}, u32[]{:S(2)}, u32[]{:S(2)}) collective-permute-start(bf16[64,4096]{1,0:T(8,128)(2,1)S(1)} %get-tuple-element.75), channel_id=1, source_target_pairs={{0,16},{1,17},{2,18},{3,19},{4,20},{5,21},{6,22},{7,23},{8,24},{9,... | collective-permute-start | bytes 1572872 | tf_op jit(solution)/shard_map/ppermute | solution.py:24
  59.3 8.2 %collective-permute-start.20 = (bf16[32,4096]{1,0:T(8,128)(2,1)S(1)}, bf16[32,4096]{1,0:T(8,128)(2,1)S(1)}, u32[]{:S(2)}, u32[]{:S(2)}) collective-permute-start(bf16[32,4096]{1,0:T(8,128)(2,1)S(1)} %get-tuple-element.76), channel_id=1, source_target_pairs={{0,4},{1,5},{2,6},{3,7},{4,0},{5,1},{6,2},{7,3},{8,12},{9,13},{10,... | collective-permute-start | bytes 786440 | tf_op jit(solution)/shard_map/ppermute | solution.py:24
  73.2 8.4 %collective-permute-start.26 = (bf16[32,4096]{1,0:T(8,128)(2,1)S(1)}, bf16[32,4096]{1,0:T(8,128)(2,1)S(1)}, u32[]{:S(2)}, u32[]{:S(2)}) collective-permute-start(bf16[32,4096]{1,0:T(8,128)(2,1)S(1)} %get-tuple-element.85), channel_id=1, source_target_pairs={{0,2},{1,3},{2,0},{3,1},{4,6},{5,7},{6,4},{7,5},{8,10},{9,11},{10,... | collective-permute-start | bytes 786440 | tf_op jit(solution)/shard_map/ppermute | solution.py:24
  73.8 8.1 %collective-permute-start.27 = (bf16[32,4096]{1,0:T(8,128)(2,1)S(1)}, bf16[32,4096]{1,0:T(8,128)(2,1)S(1)}, u32[]{:S(2)}, u32[]{:S(2)}) collective-permute-start(bf16[32,4096]{1,0:T(8,128)(2,1)S(1)} %get-tuple-element.86), channel_id=1, source_target_pairs={{0,16},{1,17},{2,18},{3,19},{4,20},{5,21},{6,22},{7,23},{8,24},{9,... | collective-permute-start | bytes 786440 | tf_op jit(solution)/shard_map/ppermute | solution.py:24
  82.9 7.8 %collective-permute-start.25 = (bf16[32,4096]{1,0:T(8,128)(2,1)S(1)}, bf16[32,4096]{1,0:T(8,128)(2,1)S(1)}, u32[]{:S(2)}, u32[]{:S(2)}) collective-permute-start(bf16[32,4096]{1,0:T(8,128)(2,1)S(1)} %shard_map.75), channel_id=1, source_target_pairs={{0,18},{1,19},{2,16},{3,17},{4,22},{5,23},{6,20},{7,21},{8,26},{9,... | collective-permute-start | bytes 786440 | tf_op jit(solution)/shard_map/ppermute | solution.py:24
  91.1 9.0 %collective-permute-start.30 = (bf16[32,4096]{1,0:T(8,128)(2,1)S(1)}, bf16[32,4096]{1,0:T(8,128)(2,1)S(1)}, u32[]{:S(2)}, u32[]{:S(2)}) collective-permute-start(bf16[32,4096]{1,0:T(8,128)(2,1)S(1)} %get-tuple-element.87), channel_id=1, source_target_pairs={{0,2},{1,3},{2,0},{3,1},{4,6},{5,7},{6,4},{7,5},{8,10},{9,11},{10,... | collective-permute-start | bytes 786440 | tf_op jit(solution)/shard_map/ppermute | solution.py:24
  92.4 11.4 %collective-permute-start.31 = (bf16[32,4096]{1,0:T(8,128)(2,1)S(1)}, bf16[32,4096]{1,0:T(8,128)(2,1)S(1)}, u32[]{:S(2)}, u32[]{:S(2)}) collective-permute-start(bf16[32,4096]{1,0:T(8,128)(2,1)S(1)} %get-tuple-element.88), channel_id=1, source_target_pairs={{0,16},{1,17},{2,18},{3,19},{4,20},{5,21},{6,22},{7,23},{8,24},{9,... | collective-permute-start | bytes 786440 | tf_op jit(solution)/shard_map/ppermute | solution.py:24
  93.4 10.3 %collective-permute-start.32 = (bf16[32,4096]{1,0:T(8,128)(2,1)S(1)}, bf16[32,4096]{1,0:T(8,128)(2,1)S(1)}, u32[]{:S(2)}, u32[]{:S(2)}) collective-permute-start(bf16[32,4096]{1,0:T(8,128)(2,1)S(1)} %get-tuple-element.89), channel_id=1, source_target_pairs={{0,4},{1,5},{2,6},{3,7},{4,0},{5,1},{6,2},{7,3},{8,12},{9,13},{10,... | collective-permute-start | bytes 786440 | tf_op jit(solution)/shard_map/ppermute | solution.py:24
  94.5 9.3 %collective-permute-start.33 = (bf16[32,4096]{1,0:T(8,128)(2,1)S(1)}, bf16[32,4096]{1,0:T(8,128)(2,1)S(1)}, u32[]{:S(2)}, u32[]{:S(2)}) collective-permute-start(bf16[32,4096]{1,0:T(8,128)(2,1)S(1)} %get-tuple-element.90), channel_id=1, source_target_pairs={{0,18},{1,19},{2,16},{3,17},{4,22},{5,23},{6,20},{7,21},{8,26},{9,... | collective-permute-start | bytes 786440 | tf_op jit(solution)/shard_map/ppermute | solution.py:24
  96.2 11.5 %collective-permute-start.29 = (bf16[32,4096]{1,0:T(8,128)(2,1)S(1)}, bf16[32,4096]{1,0:T(8,128)(2,1)S(1)}, u32[]{:S(2)}, u32[]{:S(2)}) collective-permute-start(bf16[32,4096]{1,0:T(8,128)(2,1)S(1)} %shard_map.77), channel_id=1, source_target_pairs={{0,8},{1,9},{2,10},{3,11},{4,12},{5,13},{6,14},{7,15},{8,0},{9,1},... | collective-permute-start | bytes 786440 | tf_op jit(solution)/shard_map/ppermute | solution.py:24
  (10 other events, 49.3 us)
